TPU v7x, 32 devices: a whole 2x2x4 slice. The times are simulated.
32 devices in a mesh: ch: 8 (over z, y), grp: 4 (over x, core).
Axes of the slice: x: 2, y: 2, z: 4, core: 2. Of those that a mesh axis runs over, the one named last changes fastest.
Arguments:
- raw: bfloat16 [4, 1024, 128], P('grp', 'ch'), may hold values from -400 to 400
- order: int32 [8, 16], P('ch'), may hold values from 0 to 15, each once within a row
- pair_blocks: int32 [8, 3], P('ch'), may hold values from -1 to 0, as said below
Outputs:
- corr: bfloat16 [128, 3, 128, 256], P(('ch', 'grp'))
Inputs may be any that keep to these rules, and one draw needn't show every extreme that they name: `pair_blocks`: row i names distinct blocks among i * 16 // 128 - 1, i * 16 // 128, i * 16 // 128 + 1 that lie in 0 .. 0; slot 0 is always i * 16 // 128; live slots come first and empty ones hold -1.
All inputs are finite; a program needn't handle non-finite values.
Results may differ from a plain program's by a relative error of at most 0.013.
Values may be sent and summed in bfloat16 or wider, within the bound.
No kernel may reach another device: no remote copies, remote signals or barrier semaphores. Data moves between devices by JAX's collectives and lax.ppermute only.
A program may use at most 128 MiB of HBM per device.

v0:
```python
import math

import jax
import jax.numpy as jnp
from jax import lax
from jax.sharding import PartitionSpec as P

SRC = 128
SEG = 256
LAGS = 256
SMOOTH = 8
MAXP = 3
REACH = 15


lag_scale = 1.0 / 16.0


def from_behind(value, axis, steps):
    count = lax.axis_size(axis)
    initial, last = (max(0, -steps), min(count, count - steps))
    return lax.ppermute(value, axis, [(source, source + steps) for source in range(initial, last)])


def transform_tables(half_len, lag_count, smooth_half):
    samples = jnp.arange(half_len, dtype=jnp.int32)
    column = jnp.arange(2 * half_len, dtype=jnp.int32)
    freq = column % half_len + 1
    phase_fwd = samples[:, None] * freq[None, :] % (2 * half_len)
    angle_fwd = phase_fwd.astype(jnp.float32) * (math.pi / half_len)
    forward = jnp.where(column[None, :] < half_len, jnp.cos(angle_fwd), -jnp.sin(angle_fwd)).astype(
        jnp.bfloat16
    )
    lag_steps = jnp.arange(lag_count, dtype=jnp.int32) - lag_count // 2
    phase_inv = freq[:, None] * lag_steps[None, :] % (2 * half_len)
    angle_inv = phase_inv.astype(jnp.float32) * (math.pi / half_len)
    inverse = (
        jnp.where(column[:, None] < half_len, jnp.cos(angle_inv), -jnp.sin(angle_inv)) * lag_scale
    ).astype(jnp.bfloat16)
    bins = jnp.arange(half_len, dtype=jnp.int32)
    smoothing = (jnp.abs(bins[:, None] - bins[None, :]) <= smooth_half).astype(jnp.float32) / (
        2 * smooth_half + 1
    )
    return (forward, inverse, smoothing)


def whiten(segments, forward, smoothing):
    half_len = segments.shape[-1]
    flat_rows = segments.reshape(-1, half_len)
    spectrum = jnp.dot(flat_rows, forward, preferred_element_type=jnp.float32)
    real_part = spectrum[:, :half_len]
    imag_part = spectrum[:, half_len:]
    power_bins = real_part * real_part + imag_part * imag_part
    smoothed = jnp.dot(power_bins, smoothing, precision=lax.Precision.HIGHEST)
    water_level = jnp.mean(power_bins, axis=1, keepdims=True)
    divisor = jnp.sqrt(smoothed + 0.1 * water_level + 1e-06)
    whitened = spectrum / jnp.concatenate([divisor, divisor], axis=1)
    return whitened.astype(jnp.bfloat16).reshape(segments.shape[:-1] + (2 * half_len,))


def correlate(receivers, sources, inverse):
    half_len = receivers.shape[-1] // 2
    seg_count = receivers.shape[1]
    recv_re = receivers[..., :half_len]
    recv_im = receivers[..., half_len:]
    left_first = jnp.concatenate([recv_re, recv_im], axis=1)
    left_second = jnp.concatenate([recv_im, -recv_re], axis=1)
    right_both = jnp.concatenate([sources[..., :half_len], sources[..., half_len:]], axis=1)
    cross_re = jnp.einsum(
        "rnk,snk->rsk", left_first, right_both, preferred_element_type=jnp.float32
    )
    cross_im = jnp.einsum(
        "rnk,snk->rsk", left_second, right_both, preferred_element_type=jnp.float32
    )
    cross_spec = (jnp.concatenate([cross_re, cross_im], axis=2) * (1.0 / seg_count)).astype(
        jnp.bfloat16
    )
    recv_count = receivers.shape[0]
    src_count = sources.shape[0]
    lag_values = jnp.dot(
        cross_spec.reshape(-1, 2 * half_len), inverse, preferred_element_type=jnp.float32
    )
    return lag_values.reshape(recv_count, src_count, inverse.shape[1])


def local(raw, order, pair_blocks):
    recorded = lax.all_to_all(raw, "ch", split_axis=2, concat_axis=1, tiled=True)
    local_channels = recorded.shape[2]
    onehot = (order[0][:, None] == jnp.arange(local_channels, dtype=jnp.int32)[None, :]).astype(
        jnp.bfloat16
    )
    series = jnp.einsum(
        "ck,tc->kt", onehot, recorded[0], preferred_element_type=jnp.float32
    ).astype(jnp.bfloat16)
    segments = series.reshape(1, local_channels, -1, SEG)
    forward, inverse, smoothing = transform_tables(SEG, LAGS, SMOOTH)
    own_white = whiten(segments, forward, smoothing)
    before_list = []
    for distance in range(REACH, 0, -1):
        before_list.append(from_behind(own_white, "ch", distance))
    after_list = []
    for distance in range(1, REACH + 1):
        after_list.append(from_behind(own_white, "ch", -distance))
    window = jnp.concatenate(before_list + [own_white] + after_list, axis=1)
    window_base = (lax.axis_index("ch") - REACH) * local_channels
    groups = lax.axis_size("grp")
    receivers = own_white[0]
    slot_results = []
    for slot_index in range(MAXP):
        block_id = pair_blocks[0, slot_index]
        source_start = jnp.maximum(block_id, 0) * SRC - window_base
        sources = lax.dynamic_slice_in_dim(window[0], source_start, SRC, 0)
        is_live = (block_id >= 0).astype(jnp.float32)
        lag_values = correlate(receivers, sources, inverse) * is_live
        slot_results.append(lag_values)
    stacked = lax.psum_scatter(
        jnp.stack(slot_results, axis=1).astype(jnp.bfloat16), "grp", scatter_dimension=0, tiled=True
    ).astype(jnp.float32)
    return (stacked / groups).astype(jnp.bfloat16)


def solution(mesh):
    placed = (P("grp", "ch", None), P("ch", None), P("ch", None))
    return jax.shard_map(
        local,
        mesh=mesh,
        in_specs=placed,
        out_specs=P(("ch", "grp"), None, None, None),
        check_vma=False,
    )
```

profile of v0, /device:TPU:0, one launch (start us, length us, event | category | flops | bytes accessed | tf_op | source)
XLA Modules:
  0.0 173.5 jit_solution(11654478037491588160)
XLA Ops:
  9.4 7.3 %all-to-all-start = ((bf16[8,2,1024]{2,1,0:T(2,128)(2,1)}), bf16[8,2,1024]{2,1,0:T(2,128)(2,1)S(1)}, u32[]{:S(2)}, u32[]{:S(2)}) async-start(bf16[8,2,1024]{2,1,0:T(2,128)(2,1)} %reshape.105), calls=%async_computation | async-start | bytes 65536 | tf_op jit(solution)/shard_map/all_to_all | solution.py:87
  16.7 1.4 fusion.97
  22.0 1.4 all-to-all-done
  24.4 2.4 %fusion.46 = f32[64,512]{1,0:T(8,128)S(1)} fusion(bf16[64,256]{1,0:T(8,128)(2,1)S(1)} %reshape_reshape.3, s32[512]{0:T(512)S(1)} %fusion.61, pred[512]{0:T(512)(128)(4,1)S(1)} %iota_compare_fusion.2), kind=kOutput, calls=%fused_computation.61 | convolution fusion | flops 19005440 | bytes 166400 | tf_op jit(solution)/shard_map/dot_general | solution.py:50
  27.9 5.2 %collective-permute-start.1 = (bf16[1,16,4,512]{3,2,1,0:T(4,128)(2,1)S(1)}, bf16[1,16,4,512]{3,2,1,0:T(4,128)(2,1)S(1)}, u32[]{:S(2)}, u32[]{:S(2)}) collective-permute-start(bf16[1,16,4,512]{3,2,1,0:T(4,128)(2,1)S(1)} %reshape.97), channel_id=1, source_target_pairs={{0,28},{1,29},{2,30},{3,31}} | collective-permute-start | bytes 196616 | tf_op jit(solution)/shard_map/ppermute | solution.py:22
  33.1 1.3 collective-permute-start.2
  35.7 1.3 collective-permute-start.4
  37.8 2.5 %collective-permute-start.5 = (bf16[1,16,4,512]{3,2,1,0:T(4,128)(2,1)S(1)}, bf16[1,16,4,512]{3,2,1,0:T(4,128)(2,1)S(1)}, u32[]{:S(2)}, u32[]{:S(2)}) collective-permute-start(bf16[1,16,4,512]{3,2,1,0:T(4,128)(2,1)S(1)} %reshape.97), channel_id=1, source_target_pairs={{0,12},{4,16},{8,20},{12,24},{16,28},{1,13},{5,17},{9,21},{13,25},... | collective-permute-start | bytes 196616 | tf_op jit(solution)/shard_map/ppermute | solution.py:22
  40.6 1.3 collective-permute-start.6
  42.0 3.1 %collective-permute-start.7 = (bf16[1,16,4,512]{3,2,1,0:T(4,128)(2,1)S(1)}, bf16[1,16,4,512]{3,2,1,0:T(4,128)(2,1)S(1)}, u32[]{:S(2)}, u32[]{:S(2)}) collective-permute-start(bf16[1,16,4,512]{3,2,1,0:T(4,128)(2,1)S(1)} %reshape.97), channel_id=1, source_target_pairs={{0,4},{4,8},{8,12},{12,16},{16,20},{20,24},{24,28},{1,5},{5,9},{9,... | collective-permute-start | bytes 196616 | tf_op jit(solution)/shard_map/ppermute | solution.py:22
  54.9 2.2 %collective-permute-done.10 = bf16[1,16,4,512]{3,2,1,0:T(4,128)(2,1)S(1)} collective-permute-done((bf16[1,16,4,512]{3,2,1,0:T(4,128)(2,1)S(1)}, bf16[1,16,4,512]{3,2,1,0:T(4,128)(2,1)S(1)}, u32[]{:S(2)}, u32[]{:S(2)}) %collective-permute-start.10) | collective-permute-done | bytes 65568 | tf_op jit(solution)/shard_map/ppermute | solution.py:22
  57.1 4.9 %collective-permute-done.11 = bf16[1,16,4,512]{3,2,1,0:T(4,128)(2,1)S(1)} collective-permute-done((bf16[1,16,4,512]{3,2,1,0:T(4,128)(2,1)S(1)}, bf16[1,16,4,512]{3,2,1,0:T(4,128)(2,1)S(1)}, u32[]{:S(2)}, u32[]{:S(2)}) %collective-permute-start.11) | collective-permute-done | bytes 65568 | tf_op jit(solution)/shard_map/ppermute | solution.py:22
  62.0 3.4 %collective-permute-done.12 = bf16[1,16,4,512]{3,2,1,0:T(4,128)(2,1)S(1)} collective-permute-done((bf16[1,16,4,512]{3,2,1,0:T(4,128)(2,1)S(1)}, bf16[1,16,4,512]{3,2,1,0:T(4,128)(2,1)S(1)}, u32[]{:S(2)}, u32[]{:S(2)}) %collective-permute-start.12) | collective-permute-done | bytes 65568 | tf_op jit(solution)/shard_map/ppermute | solution.py:22
  65.9 1.5 constant_dynamic-slice_fusion.2
  68.8 1.9 %convolution_bitcast_fusion.4 = f32[16,128,256]{1,0,2:T(8,128)} fusion(bf16[16,8,256]{0,1,2:T(8,128)(2,1)S(1)} %copy.23, bf16[128,4,256]{0,1,2:T(4,128)(2,1)S(1)} %get-tuple-element.9, bf16[128,4,256]{0,1,2:T(4,128)(2,1)S(1)} %get-tuple-element.8), kind=kOutput, calls=%fused_computation.20 | convolution fusion | flops 9437184 | bytes 2686976 | tf_op jit(solution)/shard_map/rnk,snk->rsk/dot_general | solution.py:72
  70.7 2.1 %copy.25 = bf16[1,128,4,512]{1,2,3,0:T(4,128)(2,1)} copy(bf16[1,128,4,512]{3,2,1,0:T(4,128)(2,1)} %get-tuple-element.7) | data formatting | bytes 1048576 | tf_op jit(solution)/shard_map/dynamic_slice | solution.py:112
  74.1 1.9 %convolution_bitcast_fusion.3 = f32[16,128,256]{1,0,2:T(8,128)} fusion(bf16[16,8,256]{0,1,2:T(8,128)(2,1)S(1)} %copy.22, bf16[128,4,256]{0,1,2:T(4,128)(2,1)S(1)} %get-tuple-element.11, bf16[128,4,256]{0,1,2:T(4,128)(2,1)S(1)} %get-tuple-element.10), kind=kOutput, calls=%fused_computation.19 | convolution fusion | flops 9437184 | bytes 2686976 | tf_op jit(solution)/shard_map/rnk,snk->rsk/dot_general | solution.py:69
  76.0 1.9 %convolution_bitcast_fusion.2 = f32[16,128,256]{1,0,2:T(8,128)} fusion(bf16[16,8,256]{0,1,2:T(8,128)(2,1)S(1)} %copy.23, bf16[128,4,256]{0,1,2:T(4,128)(2,1)S(1)} %get-tuple-element.11, bf16[128,4,256]{0,1,2:T(4,128)(2,1)S(1)} %get-tuple-element.10), kind=kOutput, calls=%fused_computation.18 | convolution fusion | flops 9437184 | bytes 2686976 | tf_op jit(solution)/shard_map/rnk,snk->rsk/dot_general | solution.py:72
  77.9 2.1 %copy.29 = bf16[1,128,4,512]{1,2,3,0:T(4,128)(2,1)} copy(bf16[1,128,4,512]{3,2,1,0:T(4,128)(2,1)} %get-tuple-element.6) | data formatting | bytes 1048576 | tf_op jit(solution)/shard_map/dynamic_slice | solution.py:112
  86.0 3.4 %fusion.15 = bf16[16,1,128,256]{3,2,0,1:T(8,128)(2,1)S(1)} fusion(bf16[16,128,512]{1,0,2:T(8,128)(2,1)S(1)} %fusion, f32[]{:T(128)} %bitcast.7, s32[256]{0:T(256)S(1)} %iota_add_fusion, s32[512]{0:T(512)S(1)} %fusion.61, pred[512]{0:T(512)(128)(4,1)S(1)} %iota_compare_fusion.2), kind=kOutput, calls=%fused_computation.23 | convolution fusion | flops 540278784 | bytes 3149316 | tf_op jit(solution)/shard_map/dot_general | solution.py:80
  89.4 3.4 %fusion.18 = bf16[16,1,128,256]{3,2,0,1:T(8,128)(2,1)S(1)} fusion(bf16[16,128,512]{1,0,2:T(8,128)(2,1)S(1)} %fusion.1, f32[]{:T(128)} %bitcast.13, s32[256]{0:T(256)S(1)} %iota_add_fusion, s32[512]{0:T(512)S(1)} %fusion.61, pred[512]{0:T(512)(128)(4,1)S(1)} %iota_compare_fusion.2), kind=kOutput, calls=%fused_computation.24 | convolution fusion | flops 540278784 | bytes 3149316 | tf_op jit(solution)/shard_map/dot_general | solution.py:80
  93.2 3.4 %fusion.21 = bf16[16,1,128,256]{3,2,0,1:T(8,128)(2,1)S(1)} fusion(bf16[16,128,512]{1,0,2:T(8,128)(2,1)S(1)} %fusion.2, f32[]{:T(128)} %bitcast.19, s32[256]{0:T(256)S(1)} %iota_add_fusion, s32[512]{0:T(512)S(1)} %fusion.61, pred[512]{0:T(512)(128)(4,1)S(1)} %iota_compare_fusion.2), kind=kOutput, calls=%fused_computation.25 | convolution fusion | flops 540278784 | bytes 3149316 | tf_op jit(solution)/shard_map/dot_general | solution.py:80
  96.6 2.0 %pad_maximum_fusion = bf16[16,3,128,256]{3,2,0,1:T(8,128)(2,1)} fusion(bf16[16,1,128,256]{3,2,0,1:T(8,128)(2,1)S(1)} %fusion.21, bf16[16,1,128,256]{3,2,0,1:T(8,128)(2,1)S(1)} %fusion.18, bf16[16,1,128,256]{3,2,0,1:T(8,128)(2,1)S(1)} %fusion.15), kind=kLoop, calls=%fused_computation.6 | loop fusion | flops 3145728 | bytes 6291456 | tf_op jit(solution)/shard_map/stack | solution.py:117
  100.5 64.0 %all-reduce.3.cloned.1.call-done = bf16[16,3,128,256]{3,2,0,1:T(8,128)(2,1)} async-done(((bf16[16,3,128,256]{3,2,0,1:T(8,128)(2,1)}), bf16[16,3,128,256]{3,2,0,1:T(8,128)(2,1)}) %all-reduce.3.cloned.1.call-update) | async-done | bytes 3145744
  (97 shorter events, 29.8 us)
Async XLA Ops:
  9.4 14.0 %all-to-all-start = ((bf16[8,2,1024]{2,1,0:T(2,128)(2,1)}), bf16[8,2,1024]{2,1,0:T(2,128)(2,1)S(1)}, u32[]{:S(2)}, u32[]{:S(2)}) async-start(bf16[8,2,1024]{2,1,0:T(2,128)(2,1)} %reshape.105), calls=%async_computation | async-start | bytes 65536 | tf_op jit(solution)/shard_map/all_to_all | solution.py:87
  16.7 147.8 %all-reduce.3.cloned.1.call-start = ((), (), s32[]{:S(2)}) async-start(), calls=%async_computation.1 | async-start | bytes 6291456
  27.2 10.6 %collective-permute-start = (bf16[1,16,4,512]{3,2,1,0:T(4,128)(2,1)S(1)}, bf16[1,16,4,512]{3,2,1,0:T(4,128)(2,1)S(1)}, u32[]{:S(2)}, u32[]{:S(2)}) collective-permute-start(bf16[1,16,4,512]{3,2,1,0:T(4,128)(2,1)S(1)} %reshape.97), channel_id=1, source_target_pairs={} | collective-permute-start | bytes 196616 | tf_op jit(solution)/shard_map/ppermute | solution.py:22
  27.9 12.7 %collective-permute-start.1 = (bf16[1,16,4,512]{3,2,1,0:T(4,128)(2,1)S(1)}, bf16[1,16,4,512]{3,2,1,0:T(4,128)(2,1)S(1)}, u32[]{:S(2)}, u32[]{:S(2)}) collective-permute-start(bf16[1,16,4,512]{3,2,1,0:T(4,128)(2,1)S(1)} %reshape.97), channel_id=1, source_target_pairs={{0,28},{1,29},{2,30},{3,31}} | collective-permute-start | bytes 196616 | tf_op jit(solution)/shard_map/ppermute | solution.py:22
  33.1 8.9 %collective-permute-start.2 = (bf16[1,16,4,512]{3,2,1,0:T(4,128)(2,1)S(1)}, bf16[1,16,4,512]{3,2,1,0:T(4,128)(2,1)S(1)}, u32[]{:S(2)}, u32[]{:S(2)}) collective-permute-start(bf16[1,16,4,512]{3,2,1,0:T(4,128)(2,1)S(1)} %reshape.97), channel_id=1, source_target_pairs={{0,24},{4,28},{1,25},{5,29},{2,26},{6,30},{3,27},{7,31}} | collective-permute-start | bytes 196616 | tf_op jit(solution)/shard_map/ppermute | solution.py:22
  34.4 10.7 %collective-permute-start.3 = (bf16[1,16,4,512]{3,2,1,0:T(4,128)(2,1)S(1)}, bf16[1,16,4,512]{3,2,1,0:T(4,128)(2,1)S(1)}, u32[]{:S(2)}, u32[]{:S(2)}) collective-permute-start(bf16[1,16,4,512]{3,2,1,0:T(4,128)(2,1)S(1)} %reshape.97), channel_id=1, source_target_pairs={{0,20},{4,24},{8,28},{1,21},{5,25},{9,29},{2,22},{6,26},{10,30},{3... | collective-permute-start | bytes 196616 | tf_op jit(solution)/shard_map/ppermute | solution.py:22
  35.7 10.8 %collective-permute-start.4 = (bf16[1,16,4,512]{3,2,1,0:T(4,128)(2,1)S(1)}, bf16[1,16,4,512]{3,2,1,0:T(4,128)(2,1)S(1)}, u32[]{:S(2)}, u32[]{:S(2)}) collective-permute-start(bf16[1,16,4,512]{3,2,1,0:T(4,128)(2,1)S(1)} %reshape.97), channel_id=1, source_target_pairs={{0,16},{4,20},{8,24},{12,28},{1,17},{5,21},{9,25},{13,29},{2,18},{... | collective-permute-start | bytes 196616 | tf_op jit(solution)/shard_map/ppermute | solution.py:22
  37.8 10.0 %collective-permute-start.5 = (bf16[1,16,4,512]{3,2,1,0:T(4,128)(2,1)S(1)}, bf16[1,16,4,512]{3,2,1,0:T(4,128)(2,1)S(1)}, u32[]{:S(2)}, u32[]{:S(2)}) collective-permute-start(bf16[1,16,4,512]{3,2,1,0:T(4,128)(2,1)S(1)} %reshape.97), channel_id=1, source_target_pairs={{0,12},{4,16},{8,20},{12,24},{16,28},{1,13},{5,17},{9,21},{13,25},... | collective-permute-start | bytes 196616 | tf_op jit(solution)/shard_map/ppermute | solution.py:22
  40.6 8.5 %collective-permute-start.6 = (bf16[1,16,4,512]{3,2,1,0:T(4,128)(2,1)S(1)}, bf16[1,16,4,512]{3,2,1,0:T(4,128)(2,1)S(1)}, u32[]{:S(2)}, u32[]{:S(2)}) collective-permute-start(bf16[1,16,4,512]{3,2,1,0:T(4,128)(2,1)S(1)} %reshape.97), channel_id=1, source_target_pairs={{0,8},{4,12},{8,16},{12,20},{16,24},{20,28},{1,9},{5,13},{9,17},{1... | collective-permute-start | bytes 196616 | tf_op jit(solution)/shard_map/ppermute | solution.py:22
  42.0 8.5 %collective-permute-start.7 = (bf16[1,16,4,512]{3,2,1,0:T(4,128)(2,1)S(1)}, bf16[1,16,4,512]{3,2,1,0:T(4,128)(2,1)S(1)}, u32[]{:S(2)}, u32[]{:S(2)}) collective-permute-start(bf16[1,16,4,512]{3,2,1,0:T(4,128)(2,1)S(1)} %reshape.97), channel_id=1, source_target_pairs={{0,4},{4,8},{8,12},{12,16},{16,20},{20,24},{24,28},{1,5},{5,9},{9,... | collective-permute-start | bytes 196616 | tf_op jit(solution)/shard_map/ppermute | solution.py:22
  45.1 6.8 %collective-permute-start.8 = (bf16[1,16,4,512]{3,2,1,0:T(4,128)(2,1)S(1)}, bf16[1,16,4,512]{3,2,1,0:T(4,128)(2,1)S(1)}, u32[]{:S(2)}, u32[]{:S(2)}) collective-permute-start(bf16[1,16,4,512]{3,2,1,0:T(4,128)(2,1)S(1)} %reshape.97), channel_id=1, source_target_pairs={{4,0},{8,4},{12,8},{16,12},{20,16},{24,20},{28,24},{5,1},{9,5},{13... | collective-permute-start | bytes 196616 | tf_op jit(solution)/shard_map/ppermute | solution.py:22
  46.5 7.1 %collective-permute-start.9 = (bf16[1,16,4,512]{3,2,1,0:T(4,128)(2,1)S(1)}, bf16[1,16,4,512]{3,2,1,0:T(4,128)(2,1)S(1)}, u32[]{:S(2)}, u32[]{:S(2)}) collective-permute-start(bf16[1,16,4,512]{3,2,1,0:T(4,128)(2,1)S(1)} %reshape.97), channel_id=1, source_target_pairs={{8,0},{12,4},{16,8},{20,12},{24,16},{28,20},{9,1},{13,5},{17,9},{2... | collective-permute-start | bytes 196616 | tf_op jit(solution)/shard_map/ppermute | solution.py:22
  47.8 9.3 %collective-permute-start.10 = (bf16[1,16,4,512]{3,2,1,0:T(4,128)(2,1)S(1)}, bf16[1,16,4,512]{3,2,1,0:T(4,128)(2,1)S(1)}, u32[]{:S(2)}, u32[]{:S(2)}) collective-permute-start(bf16[1,16,4,512]{3,2,1,0:T(4,128)(2,1)S(1)} %reshape.97), channel_id=1, source_target_pairs={{12,0},{16,4},{20,8},{24,12},{28,16},{13,1},{17,5},{21,9},{25,13},... | collective-permute-start | bytes 196616 | tf_op jit(solution)/shard_map/ppermute | solution.py:22
  49.2 12.8 %collective-permute-start.11 = (bf16[1,16,4,512]{3,2,1,0:T(4,128)(2,1)S(1)}, bf16[1,16,4,512]{3,2,1,0:T(4,128)(2,1)S(1)}, u32[]{:S(2)}, u32[]{:S(2)}) collective-permute-start(bf16[1,16,4,512]{3,2,1,0:T(4,128)(2,1)S(1)} %reshape.97), channel_id=1, source_target_pairs={{16,0},{20,4},{24,8},{28,12},{17,1},{21,5},{25,9},{29,13},{18,2},{... | collective-permute-start | bytes 196616 | tf_op jit(solution)/shard_map/ppermute | solution.py:22
  50.5 15.0 %collective-permute-start.12 = (bf16[1,16,4,512]{3,2,1,0:T(4,128)(2,1)S(1)}, bf16[1,16,4,512]{3,2,1,0:T(4,128)(2,1)S(1)}, u32[]{:S(2)}, u32[]{:S(2)}) collective-permute-start(bf16[1,16,4,512]{3,2,1,0:T(4,128)(2,1)S(1)} %reshape.97), channel_id=1, source_target_pairs={{20,0},{24,4},{28,8},{21,1},{25,5},{29,9},{22,2},{26,6},{30,10},{2... | collective-permute-start | bytes 196616 | tf_op jit(solution)/shard_map/ppermute | solution.py:22
  51.9 13.6 %collective-permute-start.13 = (bf16[1,16,4,512]{3,2,1,0:T(4,128)(2,1)S(1)}, bf16[1,16,4,512]{3,2,1,0:T(4,128)(2,1)S(1)}, u32[]{:S(2)}, u32[]{:S(2)}) collective-permute-start(bf16[1,16,4,512]{3,2,1,0:T(4,128)(2,1)S(1)} %reshape.97), channel_id=1, source_target_pairs={{24,0},{28,4},{25,1},{29,5},{26,2},{30,6},{27,3},{31,7}} | collective-permute-start | bytes 196616 | tf_op jit(solution)/shard_map/ppermute | solution.py:22
  53.6 12.0 %collective-permute-start.14 = (bf16[1,16,4,512]{3,2,1,0:T(4,128)(2,1)S(1)}, bf16[1,16,4,512]{3,2,1,0:T(4,128)(2,1)S(1)}, u32[]{:S(2)}, u32[]{:S(2)}) collective-permute-start(bf16[1,16,4,512]{3,2,1,0:T(4,128)(2,1)S(1)} %reshape.97), channel_id=1, source_target_pairs={{28,0},{29,1},{30,2},{31,3}} | collective-permute-start | bytes 196616 | tf_op jit(solution)/shard_map/ppermute | solution.py:22
  81.8 1.6 copy-start
  83.4 1.6 copy-start.1
  83.4 2.2 %copy-start.2 = (f32[16,128,256]{1,0,2:T(8,128)S(1)}, f32[16,128,256]{1,0,2:T(8,128)}, u32[]{:S(2)}) copy-start(f32[16,128,256]{1,0,2:T(8,128)} %convolution_bitcast_fusion.2) | copy-start | bytes 6291460
  98.6 0.7 copy-start.3
Sparse Core Ops, SparseCore 0:
  98.7 65.6 all-reduce.2
where the time goes:
time: 174 us
  waiting for transfers between devices  76.3 us (44%)
  starting transfers between devices  33 us (19%)
  matrix products  21.2 us (12%)
  local copies, waits for them, and re-layouts  19.2 us (11%)
  between operations  18.4 us (11%)
  other arithmetic  5.47 us (3%)
    unnamed x2, waiting for transfers between devices  64 us
    ppermute x15, starting transfers between devices, from_behind(): lax.ppermute(value, axis, [(source, source + steps) for source in range(i...  25.6 us
    ppermute x15, waiting for transfers between devices, from_behind(): lax.ppermute(value, axis, [(source, source + steps) for source in range(i...  10.9 us
    dot_general x3, matrix products, correlate(): jnp.dot(cross_spec.reshape(-1, 2 * half_len), inverse, preferred_element_...  10.2 us
    all_to_all x1, starting transfers between devices, local(): lax.all_to_all(raw, 'ch', split_axis=2, concat_axis=1, tiled=True)  7.28 us
    unnamed x44, local copies, waits for them, and re-layouts  7.08 us
    dynamic_slice x4, local copies, waits for them, and re-layouts, local(): sources = lax.dynamic_slice_in_dim(window[0], source_start, SRC, 0)  6.37 us
    dot_general x3, matrix products, correlate(): jnp.einsum('rnk,snk->rsk', left_second, right_both, preferred_element_typ...  4.4 us
  transfers between devices with their start and end apart: 17, of which 6 were waited for; matrix products, arithmetic and copies ran while one was open for 2% of the time, Pallas kernels for 0%

commit v1 on v0

--- a/solution.py
+++ b/solution.py
@@ -1,8 +1,12 @@
+import functools
 import math
 
 import jax
 import jax.numpy as jnp
+import numpy as np
 from jax import lax
+from jax.experimental import pallas as pl
+from jax.experimental.pallas import tpu as pltpu
 from jax.sharding import PartitionSpec as P
 
 SRC = 128
@@ -23,35 +27,31 @@
 
 
 def transform_tables(half_len, lag_count, smooth_half):
-    samples = jnp.arange(half_len, dtype=jnp.int32)
-    column = jnp.arange(2 * half_len, dtype=jnp.int32)
+    samples = np.arange(half_len)
+    column = np.arange(2 * half_len)
     freq = column % half_len + 1
-    phase_fwd = samples[:, None] * freq[None, :] % (2 * half_len)
-    angle_fwd = phase_fwd.astype(jnp.float32) * (math.pi / half_len)
-    forward = jnp.where(column[None, :] < half_len, jnp.cos(angle_fwd), -jnp.sin(angle_fwd)).astype(
-        jnp.bfloat16
-    )
-    lag_steps = jnp.arange(lag_count, dtype=jnp.int32) - lag_count // 2
-    phase_inv = freq[:, None] * lag_steps[None, :] % (2 * half_len)
-    angle_inv = phase_inv.astype(jnp.float32) * (math.pi / half_len)
-    inverse = (
-        jnp.where(column[:, None] < half_len, jnp.cos(angle_inv), -jnp.sin(angle_inv)) * lag_scale
-    ).astype(jnp.bfloat16)
-    bins = jnp.arange(half_len, dtype=jnp.int32)
-    smoothing = (jnp.abs(bins[:, None] - bins[None, :]) <= smooth_half).astype(jnp.float32) / (
-        2 * smooth_half + 1
-    )
-    return (forward, inverse, smoothing)
-
-
-def whiten(segments, forward, smoothing):
+    angle_fwd = (samples[:, None] * freq[None, :] % (2 * half_len)) * (math.pi / half_len)
+    forward = np.where(column[None, :] < half_len, np.cos(angle_fwd), -np.sin(angle_fwd))
+    lag_steps = np.arange(lag_count) - lag_count // 2
+    angle_inv = (freq[:, None] * lag_steps[None, :] % (2 * half_len)) * (math.pi / half_len)
+    inverse = np.where(column[:, None] < half_len, np.cos(angle_inv), -np.sin(angle_inv)) * lag_scale
+    bins = np.arange(half_len)
+    band = np.abs(bins[:, None] - bins[None, :]) <= smooth_half
+    return (
+        jnp.asarray(forward.astype(np.float32), jnp.bfloat16),
+        jnp.asarray(inverse.astype(np.float32), jnp.bfloat16),
+        jnp.asarray(band.astype(np.float32)),
+    )
+
+
+def whiten(segments, forward, band):
     half_len = segments.shape[-1]
     flat_rows = segments.reshape(-1, half_len)
     spectrum = jnp.dot(flat_rows, forward, preferred_element_type=jnp.float32)
     real_part = spectrum[:, :half_len]
     imag_part = spectrum[:, half_len:]
     power_bins = real_part * real_part + imag_part * imag_part
-    smoothed = jnp.dot(power_bins, smoothing, precision=lax.Precision.HIGHEST)
+    smoothed = jnp.dot(power_bins, band, precision=lax.Precision.HIGHEST) / (2 * SMOOTH + 1)
     water_level = jnp.mean(power_bins, axis=1, keepdims=True)
     divisor = jnp.sqrt(smoothed + 0.1 * water_level + 1e-06)
     whitened = spectrum / jnp.concatenate([divisor, divisor], axis=1)
@@ -83,7 +83,7 @@
     return lag_values.reshape(recv_count, src_count, inverse.shape[1])
 
 
-def local(raw, order, pair_blocks):
+def many_blocks(raw, order, pair_blocks):
     recorded = lax.all_to_all(raw, "ch", split_axis=2, concat_axis=1, tiled=True)
     local_channels = recorded.shape[2]
     onehot = (order[0][:, None] == jnp.arange(local_channels, dtype=jnp.int32)[None, :]).astype(
@@ -93,8 +93,8 @@
         "ck,tc->kt", onehot, recorded[0], preferred_element_type=jnp.float32
     ).astype(jnp.bfloat16)
     segments = series.reshape(1, local_channels, -1, SEG)
-    forward, inverse, smoothing = transform_tables(SEG, LAGS, SMOOTH)
-    own_white = whiten(segments, forward, smoothing)
+    forward, inverse, band = transform_tables(SEG, LAGS, SMOOTH)
+    own_white = whiten(segments, forward, band)
     before_list = []
     for distance in range(REACH, 0, -1):
         before_list.append(from_behind(own_white, "ch", distance))
@@ -119,6 +119,155 @@
     return (stacked / groups).astype(jnp.bfloat16)
 
 
+RECV = 4
+NTILE = SRC // 8
+
+
+def correlate_kernel(
+    info, own, rest, own_sib, rest_sib, forward, band, inverse, out, fwd, white, recv, cross
+):
+    half = forward.shape[0] // 2
+    bins = band.shape[0]
+    zb = own.shape[0]
+    base = info[0]
+    mine = info[1]
+    live = info[2]
+
+    fwd[0:half, :] = forward[pl.ds(pl.multiple_of(mine * half, half), half), :]
+    fwd[half:, :] = forward[pl.ds(pl.multiple_of((1 - mine) * half, half), half), :]
+    out[:, 1:] = jnp.zeros((RECV, MAXP - 1, SRC, LAGS), out.dtype)
+
+    dest = own[0, half : half + 8, :]
+    for j in range(1, zb):
+        dest = jnp.maximum(dest, own[j, half : half + 8, :])
+    for j in range(zb, 2 * zb):
+        dest = jnp.maximum(dest, rest[j, half : half + 8, :])
+    dest = dest.astype(jnp.float32)[0:1, :]
+    rows = lax.broadcasted_iota(jnp.int32, (SRC, SRC), 0).astype(jnp.float32)
+    perm = (rows == dest).astype(jnp.bfloat16)
+
+    def whiten_one(near, far, slot):
+        samples = jnp.concatenate([near, far], axis=0)
+        series = lax.dot_general(
+            perm, samples, (((1,), (1,)), ((), ())), preferred_element_type=jnp.float32
+        ).astype(jnp.bfloat16)
+        spectrum = jnp.dot(series, fwd[...], preferred_element_type=jnp.float32)
+        re = spectrum[:, :bins]
+        im = spectrum[:, bins:]
+        power = re * re + im * im
+        smoothed = jnp.dot(
+            power.astype(jnp.bfloat16), band[...], preferred_element_type=jnp.float32
+        )
+        level = jnp.mean(power, axis=1, keepdims=True)
+        scale = lax.rsqrt(smoothed * (1.0 / (2 * SMOOTH + 1)) + (0.1 * level + 1e-06))
+        wre = (re * scale).astype(jnp.bfloat16).astype(jnp.float32)
+        wim = (im * scale).astype(jnp.bfloat16).astype(jnp.float32)
+        white[slot, :, :, 0:bins] = wre.reshape(NTILE, 8, bins)
+        white[slot, :, :, bins:] = wim.reshape(NTILE, 8, bins)
+
+    for core, (a, b) in enumerate(((own, rest), (own_sib, rest_sib))):
+
+        @pl.loop(0, zb)
+        def _(z):
+            whiten_one(a[z, 0:half, :], b[zb + z, 0:half, :], core * 2 * zb + z)
+            whiten_one(b[z, 0:half, :], b[2 * zb + z, 0:half, :], core * 2 * zb + zb + z)
+
+    count = 4 * zb
+
+    @pl.loop(0, count)
+    def _(j):
+        for q in range(RECV):
+            row = base + q
+            line = white[j, row // 8, pl.ds(row % 8, 1), :]
+            a = line[:, 0:bins]
+            b = line[:, bins:]
+            recv[j, 3 * q] = jnp.broadcast_to(a, (8, bins))
+            recv[j, 3 * q + 1] = jnp.broadcast_to(b, (8, bins))
+            recv[j, 3 * q + 2] = jnp.broadcast_to(a + b, (8, bins))
+
+    @pl.loop(0, NTILE // 2)
+    def _(t):
+        for k in range(0, bins, 128):
+            sums = [jnp.zeros((2, 8, 128), jnp.float32) for _ in range(3 * RECV)]
+            for j in range(count):
+                c = white[j, pl.ds(2 * t, 2), :, k : k + 128]
+                d = white[j, pl.ds(2 * t, 2), :, bins + k : bins + k + 128]
+                e = c - d
+                for q in range(RECV):
+                    sums[3 * q] += recv[j, 3 * q, :, k : k + 128] * c
+                    sums[3 * q + 1] += recv[j, 3 * q + 1, :, k : k + 128] * d
+                    sums[3 * q + 2] += recv[j, 3 * q + 2, :, k : k + 128] * e
+            for q in range(RECV):
+                p1, p2, p3 = sums[3 * q : 3 * q + 3]
+                re = ((p1 + p2) * (1.0 / count)).reshape(16, 128).astype(jnp.bfloat16)
+                im = ((p3 - p1 + p2) * (1.0 / count)).reshape(16, 128).astype(jnp.bfloat16)
+                at = pl.ds(pl.multiple_of(16 * t, 16), 16)
+                cross[q, at, k : k + 128] = re
+                cross[q, at, bins + k : bins + k + 128] = im
+
+    keep = jnp.where(live >= 0, 1.0, 0.0)
+    for q in range(RECV):
+        lags = jnp.dot(cross[q], inverse[...], preferred_element_type=jnp.float32)
+        out[q, 0] = (lags * keep).astype(out.dtype)
+
+
+def one_block(raw, order, pair_blocks):
+    ch = lax.axis_index("ch")
+    grp = lax.axis_index("grp")
+    groups = lax.axis_size("grp")
+    total = lax.axis_size("ch") * groups
+    samples, channels = raw.shape[1:]
+    held = order.shape[1]
+
+    lanes = jnp.arange(channels, dtype=jnp.int32)
+    dest = jnp.where(lanes // held == ch, jnp.tile(order[0], channels // held) + held * ch, 0)
+    tail = jnp.broadcast_to(dest.astype(raw.dtype)[None, None, :], (1, 8, channels))
+    block = jnp.concatenate([raw, tail], axis=1)
+
+    def swap(value, ch_bits, grp_bits):
+        flip = ch_bits * groups + grp_bits
+        return lax.ppermute(value, ("ch", "grp"), [(d, d ^ flip) for d in range(total)])
+
+    own = jnp.concatenate([block, swap(block, 4, 0)], axis=0)
+    own = jnp.concatenate([own, swap(own, 2, 0)], axis=0)
+    own_sib = swap(own, 0, 1)
+    rest = jnp.concatenate([swap(own, 0, 2), swap(own, 1, 0), swap(own, 1, 2)], axis=0)
+    rest_sib = swap(rest, 0, 1)
+
+    forward, inverse, band = transform_tables(SEG, LAGS, SMOOTH)
+    info = jnp.stack([ch * held + grp * RECV, ch % 2, pair_blocks[0, 0]]).astype(jnp.int32)
+    count = 4 * own.shape[0]
+    vmem = pl.BlockSpec(memory_space=pltpu.VMEM)
+    return pl.pallas_call(
+        correlate_kernel,
+        out_shape=jax.ShapeDtypeStruct((RECV, MAXP, SRC, LAGS), jnp.bfloat16),
+        in_specs=[pl.BlockSpec(memory_space=pltpu.SMEM)] + [vmem] * 7,
+        out_specs=vmem,
+        scratch_shapes=[
+            pltpu.VMEM((SEG, 2 * SEG), jnp.bfloat16),
+            pltpu.VMEM((count, NTILE, 8, 2 * SEG), jnp.float32),
+            pltpu.VMEM((count, 3 * RECV, 8, SEG), jnp.float32),
+            pltpu.VMEM((RECV, SRC, 2 * SEG), jnp.bfloat16),
+        ],
+        compiler_params=pltpu.CompilerParams(vmem_limit_bytes=40 * 1024 * 1024),
+    )(info, own, rest, own_sib, rest_sib, forward, band.astype(jnp.bfloat16), inverse)
+
+
+def local(raw, order, pair_blocks):
+    held = order.shape[1]
+    gathered = (
+        raw.shape[2] == SRC
+        and lax.axis_size("ch") == 8
+        and lax.axis_size("grp") == 4
+        and raw.shape[0] == 1
+        and 2 * raw.shape[1] == SEG
+        and held == 4 * RECV
+    )
+    if gathered:
+        return one_block(raw, order, pair_blocks)
+    return many_blocks(raw, order, pair_blocks)
+
+
 def solution(mesh):
     placed = (P("grp", "ch", None), P("ch", None), P("ch", None))
     return jax.shard_map(

time: 174 us -> 34 us (0.20)
  waiting for transfers between devices: 76.3 us -> 11.4 us
  starting transfers between devices: 33 us -> 9.76 us
  matrix products: 21.2 us -> 0 us
  between operations: 18.4 us -> 0.07 us
  local copies, waits for them, and re-layouts: 19.2 us -> 1.48 us
  Pallas kernels: 0 us -> 10.2 us
  other arithmetic: 5.47 us -> 0.96 us
    unnamed x2 -> x0, waiting for transfers between devices: 64 us -> none
    dot_general x12 -> x0, matrix products: 21.2 us -> none  [the longest x3 10.2 us: correlate(): jnp.dot(cross_spec.reshape(-1, 2 * half_len), inverse, preferred_element_...]
    ppermute x15 -> x7, starting transfers between devices: 25.6 us -> 9.76 us  [swap(): lax.ppermute(value, ('ch', 'grp'), [(d, d ^ flip) for d in range(total)])]
    pallas_call x0 -> x1, Pallas kernels: none -> 10.2 us  [one_block(): pl.pallas_call(correlate_kernel, out_shape=jax.ShapeDtypeStruct((RECV, MA...]
    all_to_all x1 -> x0, starting transfers between devices: 7.28 us -> none  [local(): lax.all_to_all(raw, 'ch', split_axis=2, concat_axis=1, tiled=True)]
    dynamic_slice x4 -> x0, local copies, waits for them, and re-layouts: 6.37 us -> none  [local(): sources = lax.dynamic_slice_in_dim(window[0], source_start, SRC, 0)]
    unnamed x44 -> x14, local copies, waits for them, and re-layouts: 7.08 us -> 1.36 us
    slice x4 -> x0, local copies, waits for them, and re-layouts: 4.02 us -> none  [the longest x3 2.6 us: correlate(): sources[..., :half_len]]
  transfers between devices with their start and end apart: 17 -> 7, of which waited for: 6 -> 6; matrix products, arithmetic and copies ran while one was open for 2% -> 0% of each run, Pallas kernels for 0% -> 0%
where the time goes in v1:
time: 34 us; the launch traced here: 33.8 us
  waiting for transfers between devices  11.4 us (34%)
  Pallas kernels  10.2 us (30%)
  starting transfers between devices  9.76 us (29%)
  local copies, waits for them, and re-layouts  1.48 us (4%)
  other arithmetic  0.96 us (3%)
    ppermute x7, waiting for transfers between devices, swap(): lax.ppermute(value, ('ch', 'grp'), [(d, d ^ flip) for d in range(total)])  11.4 us
    pallas_call x1, Pallas kernels, one_block(): pl.pallas_call(correlate_kernel, out_shape=jax.ShapeDtypeStruct((RECV, MA...  10.2 us
    ppermute x7, starting transfers between devices, swap(): lax.ppermute(value, ('ch', 'grp'), [(d, d ^ flip) for d in range(total)])  9.76 us
    unnamed x14, local copies, waits for them, and re-layouts  1.36 us
    concatenate x1, other arithmetic, one_block(): block = jnp.concatenate([raw, tail], axis=1)  0.83 us
  transfers between devices with their start and end apart: 7, of which 6 were waited for; matrix products, arithmetic and copies ran while one was open for 0% of the time, Pallas kernels for 0%

profile of v1, /device:TPU:0, one launch (start us, length us, event | category | flops | bytes accessed | tf_op | source)
XLA Modules:
  0.0 33.8 jit_solution(11625067179010116349)
XLA Ops:
  0.0 0.7 %copy-done.5 = s32[1,16]{1,0:T(1,128)S(1)} copy-done((s32[1,16]{1,0:T(1,128)S(1)}, s32[1,16]{1,0:T(1,128)}, u32[]{:S(2)}) %copy-start.5) | copy-done | bytes 88
  0.7 0.1 add.34
  0.8 0.0 copy-start.3
  0.8 0.8 %pad_maximum_fusion.2 = bf16[1,136,128]{2,1,0:T(8,128)(2,1)S(1)} fusion(bf16[1,8,128]{2,1,0:T(8,128)(2,1)S(1)} %broadcast_in_dim.4, bf16[1,128,128]{2,1,0:T(8,128)(2,1)} %param.6), kind=kLoop, calls=%fused_computation.2 | loop fusion | flops 69632 | bytes 69632 | tf_op jit(solution)/shard_map/concatenate | solution.py:225
  1.6 4.0 %collective-permute-start = (bf16[1,136,128]{2,1,0:T(8,128)(2,1)S(1)}, bf16[1,136,128]{2,1,0:T(8,128)(2,1)S(1)}, u32[]{:S(2)}, u32[]{:S(2)}) collective-permute-start(bf16[1,136,128]{2,1,0:T(8,128)(2,1)S(1)} %pad_maximum_fusion.2), channel_id=1, source_target_pairs={{0,16},{1,17},{2,18},{3,19},{4,20},{5,21},{6,22},{7,23},{8,24},{9,... | collective-permute-start | bytes 104456 | tf_op jit(solution)/shard_map/ppermute | solution.py:229
  5.6 2.3 %collective-permute-done = bf16[1,136,128]{2,1,0:T(8,128)(2,1)S(1)} collective-permute-done((bf16[1,136,128]{2,1,0:T(8,128)(2,1)S(1)}, bf16[1,136,128]{2,1,0:T(8,128)(2,1)S(1)}, u32[]{:S(2)}, u32[]{:S(2)}) %collective-permute-start) | collective-permute-done | bytes 34848 | tf_op jit(solution)/shard_map/ppermute | solution.py:229
  7.9 1.6 %collective-permute-start.1 = (bf16[2,136,128]{2,1,0:T(8,128)(2,1)S(1)}, bf16[2,136,128]{2,1,0:T(8,128)(2,1)S(1)}, u32[]{:S(2)}, u32[]{:S(2)}) collective-permute-start(bf16[2,136,128]{2,1,0:T(8,128)(2,1)S(1)} %pad_maximum_fusion.1), channel_id=1, source_target_pairs={{0,8},{1,9},{2,10},{3,11},{4,12},{5,13},{6,14},{7,15},{8,0},{9,1},... | collective-permute-start | bytes 208904 | tf_op jit(solution)/shard_map/ppermute | solution.py:229
  9.5 2.8 %collective-permute-done.1 = bf16[2,136,128]{2,1,0:T(8,128)(2,1)S(1)} collective-permute-done((bf16[2,136,128]{2,1,0:T(8,128)(2,1)S(1)}, bf16[2,136,128]{2,1,0:T(8,128)(2,1)S(1)}, u32[]{:S(2)}, u32[]{:S(2)}) %collective-permute-start.1) | collective-permute-done | bytes 69664 | tf_op jit(solution)/shard_map/ppermute | solution.py:229
  12.3 1.8 %collective-permute-start.2 = (bf16[4,136,128]{2,1,0:T(8,128)(2,1)S(1)}, bf16[4,136,128]{2,1,0:T(8,128)(2,1)S(1)}, u32[]{:S(2)}, u32[]{:S(2)}) collective-permute-start(bf16[4,136,128]{2,1,0:T(8,128)(2,1)S(1)} %pad_maximum_fusion.own), channel_id=1, source_target_pairs={{0,2},{1,3},{2,0},{3,1},{4,6},{5,7},{6,4},{7,5},{8,10},{9,11},{10,... | collective-permute-start | bytes 417800 | tf_op jit(solution)/shard_map/ppermute | solution.py:229
  14.1 1.5 %collective-permute-start.3 = (bf16[4,136,128]{2,1,0:T(8,128)(2,1)S(1)}, bf16[4,136,128]{2,1,0:T(8,128)(2,1)S(1)}, u32[]{:S(2)}, u32[]{:S(2)}) collective-permute-start(bf16[4,136,128]{2,1,0:T(8,128)(2,1)S(1)} %pad_maximum_fusion.own), channel_id=1, source_target_pairs={{0,4},{1,5},{2,6},{3,7},{4,0},{5,1},{6,2},{7,3},{8,12},{9,13},{10,... | collective-permute-start | bytes 417800 | tf_op jit(solution)/shard_map/ppermute | solution.py:229
  15.6 0.3 collective-permute-start.4
  15.9 2.0 %collective-permute-done.2 = bf16[4,136,128]{2,1,0:T(8,128)(2,1)S(1)} collective-permute-done((bf16[4,136,128]{2,1,0:T(8,128)(2,1)S(1)}, bf16[4,136,128]{2,1,0:T(8,128)(2,1)S(1)}, u32[]{:S(2)}, u32[]{:S(2)}) %collective-permute-start.2) | collective-permute-done | bytes 139296 | tf_op jit(solution)/shard_map/ppermute | solution.py:229
  17.9 0.0 copy-start
  17.9 0.0 copy-start.1
  17.9 1.2 %collective-permute-done.3 = bf16[4,136,128]{2,1,0:T(8,128)(2,1)S(1)} collective-permute-done((bf16[4,136,128]{2,1,0:T(8,128)(2,1)S(1)}, bf16[4,136,128]{2,1,0:T(8,128)(2,1)S(1)}, u32[]{:S(2)}, u32[]{:S(2)}) %collective-permute-start.3) | collective-permute-done | bytes 139296 | tf_op jit(solution)/shard_map/ppermute | solution.py:229
  19.2 2.4 %collective-permute-done.4 = bf16[4,136,128]{2,1,0:T(8,128)(2,1)S(1)} collective-permute-done((bf16[4,136,128]{2,1,0:T(8,128)(2,1)S(1)}, bf16[4,136,128]{2,1,0:T(8,128)(2,1)S(1)}, u32[]{:S(2)}, u32[]{:S(2)}) %collective-permute-start.4) | collective-permute-done | bytes 139296 | tf_op jit(solution)/shard_map/ppermute | solution.py:229
  21.6 0.1 collective-permute-start.6
  21.7 0.5 %collective-permute-start.5 = (bf16[4,136,128]{2,1,0:T(8,128)(2,1)S(1)}, bf16[4,136,128]{2,1,0:T(8,128)(2,1)S(1)}, u32[]{:S(2)}, u32[]{:S(2)}) collective-permute-start(bf16[4,136,128]{2,1,0:T(8,128)(2,1)S(1)} %pad_maximum_fusion.own), channel_id=1, source_target_pairs={{0,1},{1,0},{2,3},{3,2},{4,5},{5,4},{6,7},{7,6},{8,9},{9,8},{10,11... | collective-permute-start | bytes 417800 | tf_op jit(solution)/shard_map/ppermute | solution.py:229
  22.2 0.7 %copy-done.4 = s32[1,3]{1,0:T(1,128)S(1)} copy-done((s32[1,3]{1,0:T(1,128)S(1)}, s32[1,3]{1,0:T(1,128)}, u32[]{:S(2)}) %copy-start.4) | copy-done | bytes 36
  22.8 0.1 pad_add_fusion.info
  22.9 0.7 %collective-permute-done.5.own_sib = bf16[4,136,128]{2,1,0:T(8,128)(2,1)S(1)} collective-permute-done((bf16[4,136,128]{2,1,0:T(8,128)(2,1)S(1)}, bf16[4,136,128]{2,1,0:T(8,128)(2,1)S(1)}, u32[]{:S(2)}, u32[]{:S(2)}) %collective-permute-start.5) | collective-permute-done | bytes 139296 | tf_op jit(solution)/shard_map/ppermute | solution.py:229
  23.6 0.0 collective-permute-done.6.rest_sib
  23.6 0.0 copy-done.2
  23.6 10.2 %shard_map.64 = bf16[4,3,128,256]{3,2,1,0:T(8,128)(2,1)} custom-call(s32[3]{0:T(128)S(1)} %pad_add_fusion.info, bf16[4,136,128]{2,1,0:T(8,128)(2,1)S(1)} %pad_maximum_fusion.own, bf16[12,136,128]{2,1,0:T(8,128)(2,1)S(1)} %constant_dynamic-update-slice_fusion.rest, bf16[4,136,128]{2,1,0:T(8,128)(2,1)S(1)} %collective-permute-done.5.own_sib, ...), custom_call_target="tpu_custom_call" | custom-call | tf_op jit(solution)/shard_map/pallas_call | solution.py:241
  (15 shorter events, 0.1 us)
Async XLA Ops:
  0.0 0.7 %copy-start.5 = (s32[1,16]{1,0:T(1,128)S(1)}, s32[1,16]{1,0:T(1,128)}, u32[]{:S(2)}) copy-start(s32[1,16]{1,0:T(1,128)} %param.7) | copy-start | bytes 196
  0.8 7.2 %copy-start.3 = (bf16[1,128,128]{2,1,0:T(8,128)(2,1)S(1)}, bf16[1,128,128]{2,1,0:T(8,128)(2,1)}, u32[]{:S(2)}) copy-start(bf16[1,128,128]{2,1,0:T(8,128)(2,1)} %param.6) | copy-start | bytes 98308
  1.6 6.3 %collective-permute-start = (bf16[1,136,128]{2,1,0:T(8,128)(2,1)S(1)}, bf16[1,136,128]{2,1,0:T(8,128)(2,1)S(1)}, u32[]{:S(2)}, u32[]{:S(2)}) collective-permute-start(bf16[1,136,128]{2,1,0:T(8,128)(2,1)S(1)} %pad_maximum_fusion.2), channel_id=1, source_target_pairs={{0,16},{1,17},{2,18},{3,19},{4,20},{5,21},{6,22},{7,23},{8,24},{9,... | collective-permute-start | bytes 104456 | tf_op jit(solution)/shard_map/ppermute | solution.py:229
  7.9 4.4 %collective-permute-start.1 = (bf16[2,136,128]{2,1,0:T(8,128)(2,1)S(1)}, bf16[2,136,128]{2,1,0:T(8,128)(2,1)S(1)}, u32[]{:S(2)}, u32[]{:S(2)}) collective-permute-start(bf16[2,136,128]{2,1,0:T(8,128)(2,1)S(1)} %pad_maximum_fusion.1), channel_id=1, source_target_pairs={{0,8},{1,9},{2,10},{3,11},{4,12},{5,13},{6,14},{7,15},{8,0},{9,1},... | collective-permute-start | bytes 208904 | tf_op jit(solution)/shard_map/ppermute | solution.py:229
  12.3 5.6 %collective-permute-start.2 = (bf16[4,136,128]{2,1,0:T(8,128)(2,1)S(1)}, bf16[4,136,128]{2,1,0:T(8,128)(2,1)S(1)}, u32[]{:S(2)}, u32[]{:S(2)}) collective-permute-start(bf16[4,136,128]{2,1,0:T(8,128)(2,1)S(1)} %pad_maximum_fusion.own), channel_id=1, source_target_pairs={{0,2},{1,3},{2,0},{3,1},{4,6},{5,7},{6,4},{7,5},{8,10},{9,11},{10,... | collective-permute-start | bytes 417800 | tf_op jit(solution)/shard_map/ppermute | solution.py:229
  14.1 5.1 %collective-permute-start.3 = (bf16[4,136,128]{2,1,0:T(8,128)(2,1)S(1)}, bf16[4,136,128]{2,1,0:T(8,128)(2,1)S(1)}, u32[]{:S(2)}, u32[]{:S(2)}) collective-permute-start(bf16[4,136,128]{2,1,0:T(8,128)(2,1)S(1)} %pad_maximum_fusion.own), channel_id=1, source_target_pairs={{0,4},{1,5},{2,6},{3,7},{4,0},{5,1},{6,2},{7,3},{8,12},{9,13},{10,... | collective-permute-start | bytes 417800 | tf_op jit(solution)/shard_map/ppermute | solution.py:229
  15.6 6.0 %collective-permute-start.4 = (bf16[4,136,128]{2,1,0:T(8,128)(2,1)S(1)}, bf16[4,136,128]{2,1,0:T(8,128)(2,1)S(1)}, u32[]{:S(2)}, u32[]{:S(2)}) collective-permute-start(bf16[4,136,128]{2,1,0:T(8,128)(2,1)S(1)} %pad_maximum_fusion.own), channel_id=1, source_target_pairs={{0,6},{1,7},{2,4},{3,5},{4,2},{5,3},{6,0},{7,1},{8,14},{9,15},{10,... | collective-permute-start | bytes 417800 | tf_op jit(solution)/shard_map/ppermute | solution.py:229
  17.9 5.7 %copy-start.2 = (bf16[256,256]{1,0:T(8,128)(2,1)S(1)}, bf16[256,256]{1,0:T(8,128)(2,1)}, u32[]{:S(2)}) copy-start(bf16[256,256]{1,0:T(8,128)(2,1)} %constant.53.band) | copy-start | bytes 393220
  17.9 5.7 %copy-start = (bf16[512,256]{1,0:T(8,128)(2,1)S(1)}, bf16[512,256]{1,0:T(8,128)(2,1)}, u32[]{:S(2)}) copy-start(bf16[512,256]{1,0:T(8,128)(2,1)} %constant.48.clone.inverse) | copy-start | bytes 786436
  17.9 5.7 %copy-start.1 = (bf16[256,512]{1,0:T(8,128)(2,1)S(1)}, bf16[256,512]{1,0:T(8,128)(2,1)}, u32[]{:S(2)}) copy-start(bf16[256,512]{1,0:T(8,128)(2,1)} %constant.47.clone.forward) | copy-start | bytes 786436
  21.6 2.0 %collective-permute-start.6 = (bf16[12,136,128]{2,1,0:T(8,128)(2,1)S(1)}, bf16[12,136,128]{2,1,0:T(8,128)(2,1)S(1)}, u32[]{:S(2)}, u32[]{:S(2)}) collective-permute-start(bf16[12,136,128]{2,1,0:T(8,128)(2,1)S(1)} %constant_dynamic-update-slice_fusion.rest), channel_id=1, source_target_pairs={{0,1},{1,0},{2,3},{3,2},{4,5},{5,4},{6,7},{7,6},{8,9},{9,8},{10,11... | collective-permute-start | bytes 1253384 | tf_op jit(solution)/shard_map/ppermute | solution.py:229
  21.7 1.9 %collective-permute-start.5 = (bf16[4,136,128]{2,1,0:T(8,128)(2,1)S(1)}, bf16[4,136,128]{2,1,0:T(8,128)(2,1)S(1)}, u32[]{:S(2)}, u32[]{:S(2)}) collective-permute-start(bf16[4,136,128]{2,1,0:T(8,128)(2,1)S(1)} %pad_maximum_fusion.own), channel_id=1, source_target_pairs={{0,1},{1,0},{2,3},{3,2},{4,5},{5,4},{6,7},{7,6},{8,9},{9,8},{10,11... | collective-permute-start | bytes 417800 | tf_op jit(solution)/shard_map/ppermute | solution.py:229
  22.2 0.7 %copy-start.4 = (s32[1,3]{1,0:T(1,128)S(1)}, s32[1,3]{1,0:T(1,128)}, u32[]{:S(2)}) copy-start(s32[1,3]{1,0:T(1,128)} %param.8) | copy-start | bytes 40

commit v2 on v0

--- a/solution.py
+++ b/solution.py
@@ -1,8 +1,12 @@
+import functools
 import math
 
 import jax
 import jax.numpy as jnp
+import numpy as np
 from jax import lax
+from jax.experimental import pallas as pl
+from jax.experimental.pallas import tpu as pltpu
 from jax.sharding import PartitionSpec as P
 
 SRC = 128
@@ -23,35 +27,27 @@
 
 
 def transform_tables(half_len, lag_count, smooth_half):
-    samples = jnp.arange(half_len, dtype=jnp.int32)
-    column = jnp.arange(2 * half_len, dtype=jnp.int32)
+    samples = np.arange(half_len)
+    column = np.arange(2 * half_len)
     freq = column % half_len + 1
-    phase_fwd = samples[:, None] * freq[None, :] % (2 * half_len)
-    angle_fwd = phase_fwd.astype(jnp.float32) * (math.pi / half_len)
-    forward = jnp.where(column[None, :] < half_len, jnp.cos(angle_fwd), -jnp.sin(angle_fwd)).astype(
-        jnp.bfloat16
-    )
-    lag_steps = jnp.arange(lag_count, dtype=jnp.int32) - lag_count // 2
-    phase_inv = freq[:, None] * lag_steps[None, :] % (2 * half_len)
-    angle_inv = phase_inv.astype(jnp.float32) * (math.pi / half_len)
-    inverse = (
-        jnp.where(column[:, None] < half_len, jnp.cos(angle_inv), -jnp.sin(angle_inv)) * lag_scale
-    ).astype(jnp.bfloat16)
-    bins = jnp.arange(half_len, dtype=jnp.int32)
-    smoothing = (jnp.abs(bins[:, None] - bins[None, :]) <= smooth_half).astype(jnp.float32) / (
-        2 * smooth_half + 1
-    )
-    return (forward, inverse, smoothing)
-
-
-def whiten(segments, forward, smoothing):
+    angle_fwd = (samples[:, None] * freq[None, :] % (2 * half_len)) * (math.pi / half_len)
+    forward = np.where(column[None, :] < half_len, np.cos(angle_fwd), -np.sin(angle_fwd))
+    lag_steps = np.arange(lag_count) - lag_count // 2
+    angle_inv = (freq[:, None] * lag_steps[None, :] % (2 * half_len)) * (math.pi / half_len)
+    inverse = np.where(column[:, None] < half_len, np.cos(angle_inv), -np.sin(angle_inv)) * lag_scale
+    bins = np.arange(half_len)
+    band = np.abs(bins[:, None] - bins[None, :]) <= smooth_half
+    return (forward.astype(np.float32), inverse.astype(np.float32), band.astype(np.float32))
+
+
+def whiten(segments, forward, band):
     half_len = segments.shape[-1]
     flat_rows = segments.reshape(-1, half_len)
     spectrum = jnp.dot(flat_rows, forward, preferred_element_type=jnp.float32)
     real_part = spectrum[:, :half_len]
     imag_part = spectrum[:, half_len:]
     power_bins = real_part * real_part + imag_part * imag_part
-    smoothed = jnp.dot(power_bins, smoothing, precision=lax.Precision.HIGHEST)
+    smoothed = jnp.dot(power_bins, band, precision=lax.Precision.HIGHEST) / (2 * SMOOTH + 1)
     water_level = jnp.mean(power_bins, axis=1, keepdims=True)
     divisor = jnp.sqrt(smoothed + 0.1 * water_level + 1e-06)
     whitened = spectrum / jnp.concatenate([divisor, divisor], axis=1)
@@ -83,7 +79,7 @@
     return lag_values.reshape(recv_count, src_count, inverse.shape[1])
 
 
-def local(raw, order, pair_blocks):
+def many_blocks(raw, order, pair_blocks):
     recorded = lax.all_to_all(raw, "ch", split_axis=2, concat_axis=1, tiled=True)
     local_channels = recorded.shape[2]
     onehot = (order[0][:, None] == jnp.arange(local_channels, dtype=jnp.int32)[None, :]).astype(
@@ -93,8 +89,10 @@
         "ck,tc->kt", onehot, recorded[0], preferred_element_type=jnp.float32
     ).astype(jnp.bfloat16)
     segments = series.reshape(1, local_channels, -1, SEG)
-    forward, inverse, smoothing = transform_tables(SEG, LAGS, SMOOTH)
-    own_white = whiten(segments, forward, smoothing)
+    forward, inverse, band = transform_tables(SEG, LAGS, SMOOTH)
+    forward = jnp.asarray(forward, jnp.bfloat16)
+    inverse = jnp.asarray(inverse, jnp.bfloat16)
+    own_white = whiten(segments, forward, band)
     before_list = []
     for distance in range(REACH, 0, -1):
         before_list.append(from_behind(own_white, "ch", distance))
@@ -119,6 +117,227 @@
     return (stacked / groups).astype(jnp.bfloat16)
 
 
+RECV = 4
+KB = 8
+WIDTH = 2 * SMOOTH + 1
+
+
+def label_kernel(order, pairs, raw, out, keep):
+    held = order.shape[1]
+    half, channels = raw.shape[1:]
+    me = lax.axis_index("ch")
+    lanes = lax.broadcasted_iota(jnp.int32, (8, channels), 1)
+    row = jnp.zeros((8, channels), jnp.int32)
+    for c in range(held):
+        row = jnp.where(lanes % held == c, order[0, c], row)
+    row = jnp.where(lanes // held == me, row + held * me, 0)
+    keep[...] = jnp.broadcast_to(jnp.where(pairs[0, 0] >= 0, 1.0, 0.0), keep.shape)
+    out[0, 0:half, :] = raw[0]
+    out[0, half : half + 8, :] = row.astype(jnp.float32).astype(out.dtype)
+
+
+def whiten_group(items, fwd, band, spec, pows, white):
+    bins = band.shape[0]
+    levels = []
+    for i, (first, second, first_next, second_next) in enumerate(items):
+        samples = jnp.concatenate(
+            [
+                jnp.concatenate([first, first_next], axis=1),
+                jnp.concatenate([second, second_next], axis=1),
+            ],
+            axis=0,
+        )
+        re = jnp.dot(fwd[0:bins, :], samples, preferred_element_type=jnp.float32)
+        im = jnp.dot(fwd[bins:, :], samples, preferred_element_type=jnp.float32)
+        power = re * re + im * im
+        spec[i, 0] = re
+        spec[i, 1] = im
+        pows[i] = power.astype(jnp.bfloat16)
+        levels.append(jnp.sum(power.reshape(bins // 8, 8, 2 * SRC), axis=0))
+    for i in range(len(items)):
+        level = jnp.sum(levels[i], axis=0, keepdims=True) * (0.1 * WIDTH / bins) + 1e-6 * WIDTH
+        smoothed = jnp.dot(band[...], pows[i], preferred_element_type=jnp.float32)
+        scale = lax.rsqrt(smoothed + level)
+        for part in range(2):
+            value = spec[i, part] * scale
+            left = value[:, 0:SRC].reshape(bins // KB, KB, SRC)
+            right = value[:, SRC:].reshape(bins // KB, KB, SRC)
+            both = jnp.concatenate([left, right], axis=1).astype(jnp.bfloat16)
+            white[:, part, 2 * KB * i : 2 * KB * (i + 1), :] = both
+
+
+def own_kernel(own, near, other, diag, forward, band, white, fwd, perm, select, spec, pows):
+    half = forward.shape[1] // 2
+    zb = own.shape[0]
+    ch = lax.axis_index("ch")
+    base = (ch * lax.axis_size("grp") + lax.axis_index("grp")) * RECV
+    mine = ch % 2
+    fwd[:, 0:half] = forward[:, pl.ds(pl.multiple_of(mine * half, half), half)]
+    fwd[:, half:] = forward[:, pl.ds(pl.multiple_of((1 - mine) * half, half), half)]
+
+    dest = own[0, half : half + 8, :]
+    for z in range(1, zb):
+        dest = jnp.maximum(dest, own[z, half : half + 8, :])
+    for z in range(zb):
+        dest = jnp.maximum(dest, near[z, half : half + 8, :])
+    dest = dest.astype(jnp.float32)[0:1, :]
+    rows = lax.broadcasted_iota(jnp.int32, (SRC, SRC), 0)
+    perm[...] = (rows.astype(jnp.float32) == dest).astype(jnp.bfloat16)
+    wanted = (lax.broadcasted_iota(jnp.int32, (KB * RECV, SRC), 0) // KB + base).astype(jnp.float32)
+    select[...] = (wanted == dest).astype(jnp.bfloat16)
+
+    items = [(own[z, 0:half], near[z, 0:half], other[z], diag[z]) for z in range(zb)]
+    whiten_group(items, fwd, band, spec, pows, white)
+
+
+def cross_kernel(
+    keep, sib, own_white, fwd, perm, select, band, inverse, out,
+    white, pick, cross, lags, blank, spec, pows, sems,
+):
+    bins = band.shape[0]
+    zb = sib.shape[0] // 4
+    count = 4 * zb
+    blocks = bins // KB
+    deep = 2 * count * KB
+
+    blank[...] = jnp.zeros(blank.shape, blank.dtype)
+    copies = [
+        pltpu.make_async_copy(blank, out.at[q, pl.ds(1, MAXP - 1)], sems.at[q]) for q in range(RECV)
+    ]
+    for copy in copies:
+        copy.start()
+
+    items = [(sib[z], sib[2 * zb + z], sib[zb + z], sib[3 * zb + z]) for z in range(zb)]
+    whiten_group(items, fwd, band, spec, pows, white)
+
+    def both(kb):
+        return jnp.concatenate(
+            [own_white[kb, 0], white[kb, 0], own_white[kb, 1], white[kb, 1]], axis=0
+        )
+
+    lane = lax.broadcasted_iota(jnp.int32, (KB * RECV, deep), 1) % KB
+    sub = lax.broadcasted_iota(jnp.int32, (KB * RECV, deep), 0) % KB
+    same = (lane == sub).astype(jnp.float32)
+    for kb in range(blocks):
+        v = lax.dot_general(
+            select[...], both(kb), (((1,), (1,)), ((), ())), preferred_element_type=jnp.float32
+        )
+        v = v * same
+        pick[kb, 0 : KB * RECV, :] = v.astype(jnp.bfloat16)
+        turned = jnp.concatenate([v[:, deep // 2 :], -v[:, 0 : deep // 2]], axis=1)
+        pick[kb, KB * RECV :, :] = turned.astype(jnp.bfloat16)
+
+    sums = [jnp.dot(pick[kb], both(kb), preferred_element_type=jnp.float32) for kb in range(blocks)]
+    for part in range(2):
+        for q in range(RECV):
+            at = (part * RECV + q) * KB
+            column = jnp.concatenate([s[at : at + KB] for s in sums], axis=0) * (WIDTH / count)
+            lanes = slice((q % 2) * SRC, (q % 2 + 1) * SRC)
+            cross[q // 2, part * bins : (part + 1) * bins, lanes] = column.astype(jnp.bfloat16)
+
+    for p in range(RECV // 2):
+        turned = jnp.dot(inverse[...], cross[p], preferred_element_type=jnp.float32) * keep[0:1, :]
+        turned = turned.astype(jnp.bfloat16)
+        for u in range(2):
+            q = 2 * p + u
+            lags[q] = lax.dot_general(
+                perm[...],
+                turned[:, u * SRC : (u + 1) * SRC],
+                (((1,), (1,)), ((), ())),
+                preferred_element_type=jnp.float32,
+            ).astype(jnp.bfloat16)
+            copy = pltpu.make_async_copy(lags.at[q], out.at[q, 0], sems.at[RECV + q])
+            copy.start()
+            copies.append(copy)
+    for copy in copies:
+        copy.wait()
+
+
+def one_block(raw, order, pair_blocks):
+    groups = lax.axis_size("grp")
+    total = lax.axis_size("ch") * groups
+    half, channels = raw.shape[1:]
+    vmem = pl.BlockSpec(memory_space=pltpu.VMEM)
+    smem = pl.BlockSpec(memory_space=pltpu.SMEM)
+    params = pltpu.CompilerParams(vmem_limit_bytes=24 * 1024 * 1024)
+    dtype = raw.dtype
+
+    block, keep = pl.pallas_call(
+        label_kernel,
+        out_shape=[pltpu.VMEM((1, half + 8, channels), dtype), pltpu.VMEM((8, 2 * SRC), jnp.float32)],
+        in_specs=[smem, smem, vmem],
+        out_specs=[vmem, vmem],
+    )(order, pair_blocks, raw)
+
+    def swap(value, ch_bits, grp_bits):
+        flip = ch_bits * groups + grp_bits
+        return lax.ppermute(value, ("ch", "grp"), [(d, d ^ flip) for d in range(total)])
+
+    parts = [block, swap(block, 4, 0), swap(block, 2, 0), swap(block, 6, 0)]
+    own = jnp.concatenate(parts, axis=0)
+    bare = jnp.concatenate([p[:, 0:half] for p in parts], axis=0)
+    diag = swap(bare, 1, 2)
+    near = swap(own, 1, 0)
+    other = swap(bare, 0, 2)
+    sib = swap(jnp.concatenate([bare, other, near[:, 0:half], diag], axis=0), 0, 1)
+
+    forward, inverse, band = transform_tables(SEG, LAGS, SMOOTH)
+    forward, band, inverse = [
+        jnp.asarray(np.ascontiguousarray(t), jnp.bfloat16) for t in (forward.T, band, inverse.T)
+    ]
+    zb = own.shape[0]
+    blocks = SEG // KB
+    white = pltpu.VMEM((blocks, 2, 2 * zb * KB, SRC), jnp.bfloat16)
+    work = [
+        pltpu.VMEM((zb, 2, SEG, 2 * SRC), jnp.float32),
+        pltpu.VMEM((zb, SEG, 2 * SRC), jnp.bfloat16),
+    ]
+    own_white, fwd, perm, select = pl.pallas_call(
+        own_kernel,
+        out_shape=[
+            white,
+            pltpu.VMEM((2 * SEG, SEG), jnp.bfloat16),
+            pltpu.VMEM((SRC, SRC), jnp.bfloat16),
+            pltpu.VMEM((KB * RECV, SRC), jnp.bfloat16),
+        ],
+        in_specs=[vmem] * 6,
+        out_specs=[vmem] * 4,
+        scratch_shapes=work,
+        compiler_params=params,
+    )(own, near, other, diag, forward, band)
+    return pl.pallas_call(
+        cross_kernel,
+        out_shape=jax.ShapeDtypeStruct((RECV, MAXP, SRC, LAGS), jnp.bfloat16),
+        in_specs=[vmem] * 8,
+        out_specs=pl.BlockSpec(memory_space=pl.ANY),
+        scratch_shapes=[
+            white,
+            pltpu.VMEM((blocks, 2 * RECV * KB, 8 * zb * KB), jnp.bfloat16),
+            pltpu.VMEM((RECV // 2, 2 * SEG, 2 * SRC), jnp.bfloat16),
+            pltpu.VMEM((RECV, SRC, LAGS), jnp.bfloat16),
+            pltpu.VMEM((MAXP - 1, SRC, LAGS), jnp.bfloat16),
+            *work,
+            pltpu.SemaphoreType.DMA((2 * RECV,)),
+        ],
+        compiler_params=params,
+    )(keep, sib, own_white, fwd, perm, select, band, inverse)
+
+
+def local(raw, order, pair_blocks):
+    held = order.shape[1]
+    gathered = (
+        raw.shape[2] == SRC
+        and lax.axis_size("ch") == 8
+        and lax.axis_size("grp") == 4
+        and raw.shape[0] == 1
+        and 2 * raw.shape[1] == SEG
+        and held == 4 * RECV
+    )
+    if gathered:
+        return one_block(raw, order, pair_blocks)
+    return many_blocks(raw, order, pair_blocks)
+
+
 def solution(mesh):
     placed = (P("grp", "ch", None), P("ch", None), P("ch", None))
     return jax.shard_map(

time: 174 us -> 25.4 us (0.15)
  waiting for transfers between devices: 76.3 us -> 10.9 us
  starting transfers between devices: 33 us -> 9.45 us
  matrix products: 21.2 us -> 0 us
  local copies, waits for them, and re-layouts: 19.2 us -> 0.16 us
  between operations: 18.4 us -> 0.12 us
  other arithmetic: 5.47 us -> 0.02 us
  Pallas kernels: 0 us -> 4.62 us
    unnamed x2 -> x0, waiting for transfers between devices: 64 us -> none
    dot_general x12 -> x0, matrix products: 21.2 us -> none  [the longest x3 10.2 us: correlate(): jnp.dot(cross_spec.reshape(-1, 2 * half_len), inverse, preferred_element_...]
    ppermute x15 -> x7, starting transfers between devices: 25.6 us -> 9.45 us  [swap(): lax.ppermute(value, ('ch', 'grp'), [(d, d ^ flip) for d in range(total)])]
    all_to_all x1 -> x0, starting transfers between devices: 7.28 us -> none  [local(): lax.all_to_all(raw, 'ch', split_axis=2, concat_axis=1, tiled=True)]
    unnamed x44 -> x11, local copies, waits for them, and re-layouts: 7.08 us -> 0.08 us
    dynamic_slice x4 -> x0, local copies, waits for them, and re-layouts: 6.37 us -> none  [local(): sources = lax.dynamic_slice_in_dim(window[0], source_start, SRC, 0)]
    pallas_call x0 -> x3, Pallas kernels: none -> 4.62 us  [the longest x1 3.18 us: one_block(): pl.pallas_call(cross_kernel, out_shape=jax.ShapeDtypeStruct((RECV, MAXP,...]
    slice x4, local copies, waits for them, and re-layouts: 4.02 us -> 0.05 us  [one_block(): bare = jnp.concatenate([p[:, 0:half] for p in parts], axis=0)]
  transfers between devices with their start and end apart: 17 -> 7, of which waited for: 6 -> 5; matrix products, arithmetic and copies ran while one was open for 2% -> 0% of each run, Pallas kernels for 0% -> 3%
where the time goes in v2:
time: 25.4 us; the launch traced here: 25.2 us
  waiting for transfers between devices  10.9 us (43%)
  starting transfers between devices  9.45 us (37%)
  Pallas kernels  4.62 us (18%)
    ppermute x7, waiting for transfers between devices, swap(): lax.ppermute(value, ('ch', 'grp'), [(d, d ^ flip) for d in range(total)])  10.9 us
    ppermute x7, starting transfers between devices, swap(): lax.ppermute(value, ('ch', 'grp'), [(d, d ^ flip) for d in range(total)])  9.45 us
    pallas_call x1, Pallas kernels, one_block(): pl.pallas_call(cross_kernel, out_shape=jax.ShapeDtypeStruct((RECV, MAXP,...  3.18 us
    pallas_call x1, Pallas kernels, one_block(): pl.pallas_call(label_kernel, out_shape=[pltpu.VMEM((1, half + 8, channels...  0.78 us
    pallas_call x1, Pallas kernels, one_block(): pl.pallas_call(own_kernel, out_shape=[white, pltpu.VMEM((2 * SEG, SEG), j...  0.65 us
  transfers between devices with their start and end apart: 7, of which 5 were waited for; matrix products, arithmetic and copies ran while one was open for 0% of the time, Pallas kernels for 3%

profile of v2, /device:TPU:0, one launch (start us, length us, event | category | flops | bytes accessed | tf_op | source)
XLA Modules:
  0.0 25.2 jit_solution(3876325573095860321)
XLA Ops:
  0.0 0.8 %shard_map.64 = (bf16[1,136,128]{2,1,0:T(8,128)(2,1)S(1)}, f32[8,256]{1,0:T(8,128)S(1)}) custom-call(s32[1,16]{1,0:T(1,128)} %order.1, s32[1,3]{1,0:T(1,128)} %pairs.1, bf16[1,128,128]{2,1,0:T(8,128)(2,1)} %raw.1), custom_call_target="tpu_custom_call" | custom-call | tf_op jit(solution)/shard_map/pallas_call | solution.py:265
  0.8 5.1 %collective-permute-start.2 = (bf16[1,136,128]{2,1,0:T(8,128)(2,1)S(1)}, bf16[1,136,128]{2,1,0:T(8,128)(2,1)S(1)}, u32[]{:S(2)}, u32[]{:S(2)}) collective-permute-start(bf16[1,136,128]{2,1,0:T(8,128)(2,1)S(1)} %get-tuple-element.12), channel_id=1, source_target_pairs={{0,24},{1,25},{2,26},{3,27},{4,28},{5,29},{6,30},{7,31},{8,16},{9,... | collective-permute-start | bytes 104456 | tf_op jit(solution)/shard_map/ppermute | solution.py:274
  5.9 0.0 collective-permute-start.1
  5.9 0.6 %collective-permute-start = (bf16[1,136,128]{2,1,0:T(8,128)(2,1)S(1)}, bf16[1,136,128]{2,1,0:T(8,128)(2,1)S(1)}, u32[]{:S(2)}, u32[]{:S(2)}) collective-permute-start(bf16[1,136,128]{2,1,0:T(8,128)(2,1)S(1)} %get-tuple-element.12), channel_id=1, source_target_pairs={{0,16},{1,17},{2,18},{3,19},{4,20},{5,21},{6,22},{7,23},{8,24},{9,... | collective-permute-start | bytes 104456 | tf_op jit(solution)/shard_map/ppermute | solution.py:274
  6.6 4.3 %collective-permute-done = bf16[1,136,128]{2,1,0:T(8,128)(2,1)S(1)} collective-permute-done((bf16[1,136,128]{2,1,0:T(8,128)(2,1)S(1)}, bf16[1,136,128]{2,1,0:T(8,128)(2,1)S(1)}, u32[]{:S(2)}, u32[]{:S(2)}) %collective-permute-start) | collective-permute-done | bytes 34848 | tf_op jit(solution)/shard_map/ppermute | solution.py:274
  10.9 0.0 collective-permute-done.1
  10.9 0.0 collective-permute-done.2
  11.0 1.6 %collective-permute-start.3 = (bf16[4,128,128]{2,1,0:T(8,128)(2,1)S(1)}, bf16[4,128,128]{2,1,0:T(8,128)(2,1)S(1)}, u32[]{:S(2)}, u32[]{:S(2)}) collective-permute-start(bf16[4,128,128]{2,1,0:T(8,128)(2,1)S(1)} %pad_maximum_fusion), channel_id=1, source_target_pairs={{0,2},{1,3},{2,0},{3,1},{4,6},{5,7},{6,4},{7,5},{8,10},{9,11},{10,... | collective-permute-start | bytes 393224 | tf_op jit(solution)/shard_map/ppermute | solution.py:274
  12.6 1.6 %collective-permute-start.4 = (bf16[4,136,128]{2,1,0:T(8,128)(2,1)S(1)}, bf16[4,136,128]{2,1,0:T(8,128)(2,1)S(1)}, u32[]{:S(2)}, u32[]{:S(2)}) collective-permute-start(bf16[4,136,128]{2,1,0:T(8,128)(2,1)S(1)} %constant_dynamic-update-slice_fusion.own), channel_id=1, source_target_pairs={{0,4},{1,5},{2,6},{3,7},{4,0},{5,1},{6,2},{7,3},{8,12},{9,13},{10,... | collective-permute-start | bytes 417800 | tf_op jit(solution)/shard_map/ppermute | solution.py:274
  14.2 0.5 %collective-permute-start.5 = (bf16[4,128,128]{2,1,0:T(8,128)(2,1)S(1)}, bf16[4,128,128]{2,1,0:T(8,128)(2,1)S(1)}, u32[]{:S(2)}, u32[]{:S(2)}) collective-permute-start(bf16[4,128,128]{2,1,0:T(8,128)(2,1)S(1)} %pad_maximum_fusion), channel_id=1, source_target_pairs={{0,6},{1,7},{2,4},{3,5},{4,2},{5,3},{6,0},{7,1},{8,14},{9,15},{10,... | collective-permute-start | bytes 393224 | tf_op jit(solution)/shard_map/ppermute | solution.py:274
  14.6 2.6 %collective-permute-done.3.other = bf16[4,128,128]{2,1,0:T(8,128)(2,1)S(1)} collective-permute-done((bf16[4,128,128]{2,1,0:T(8,128)(2,1)S(1)}, bf16[4,128,128]{2,1,0:T(8,128)(2,1)S(1)}, u32[]{:S(2)}, u32[]{:S(2)}) %collective-permute-start.3) | collective-permute-done | bytes 131104 | tf_op jit(solution)/shard_map/ppermute | solution.py:274
  17.2 0.0 copy-start.2
  17.3 1.3 %collective-permute-done.4.near = bf16[4,136,128]{2,1,0:T(8,128)(2,1)S(1)} collective-permute-done((bf16[4,136,128]{2,1,0:T(8,128)(2,1)S(1)}, bf16[4,136,128]{2,1,0:T(8,128)(2,1)S(1)}, u32[]{:S(2)}, u32[]{:S(2)}) %collective-permute-start.4) | collective-permute-done | bytes 139296 | tf_op jit(solution)/shard_map/ppermute | solution.py:274
  18.6 0.0 copy-start
  18.6 1.4 %collective-permute-done.5.diag = bf16[4,128,128]{2,1,0:T(8,128)(2,1)S(1)} collective-permute-done((bf16[4,128,128]{2,1,0:T(8,128)(2,1)S(1)}, bf16[4,128,128]{2,1,0:T(8,128)(2,1)S(1)}, u32[]{:S(2)}, u32[]{:S(2)}) %collective-permute-start.5) | collective-permute-done | bytes 131104 | tf_op jit(solution)/shard_map/ppermute | solution.py:274
  20.1 0.0 copy-start.1
  20.1 0.1 collective-permute-start.6
  20.1 0.0 copy-done.2
  20.2 0.0 copy-done
  20.2 0.6 %shard_map.65 = (bf16[32,2,64,128]{3,2,1,0:T(8,128)(2,1)S(1)}, bf16[512,256]{1,0:T(8,128)(2,1)S(1)}, bf16[128,128]{1,0:T(8,128)(2,1)S(1)}, bf16[32,128]{1,0:T(8,128)(2,1)S(1)}) custom-call(bf16[4,136,128]{2,1,0:T(8,128)(2,1)S(1)} %constant_dynamic-update-slice_fusion.own, bf16[4,136,128]{2,1,0:T(8,128)(2,1)S(1)} %collective-permute-done.4.near, ...), custom_call_target="tpu_custom_call" | custom-call | tf_op jit(solution)/shard_map/pallas_call | solution.py:295
  20.8 1.2 %collective-permute-done.6.sib = bf16[16,128,128]{2,1,0:T(8,128)(2,1)S(1)} collective-permute-done((bf16[16,128,128]{2,1,0:T(8,128)(2,1)S(1)}, bf16[16,128,128]{2,1,0:T(8,128)(2,1)S(1)}, u32[]{:S(2)}, u32[]{:S(2)}) %collective-permute-start.6) | collective-permute-done | bytes 524320 | tf_op jit(solution)/shard_map/ppermute | solution.py:274
  22.0 0.0 copy-done.1
  22.0 3.2 %shard_map.66 = bf16[4,3,128,256]{3,2,1,0:T(8,128)(2,1)} custom-call(f32[8,256]{1,0:T(8,128)S(1)} %get-tuple-element.11.keep, bf16[16,128,128]{2,1,0:T(8,128)(2,1)S(1)} %collective-permute-done.6.sib, bf16[32,2,64,128]{3,2,1,0:T(8,128)(2,1)S(1)} %get-tuple-element.13.own_white, bf16[512,256]{1,0:T(8,128)(2,1)S(1)} %get-tuple-element.14.fwd, ...), custom_call_target="tpu_custom_call" | custom-call | tf_op jit(solution)/shard_map/pallas_call | solution.py:308
  (12 shorter events, 0.2 us)
Async XLA Ops:
  0.8 10.1 %collective-permute-start.2 = (bf16[1,136,128]{2,1,0:T(8,128)(2,1)S(1)}, bf16[1,136,128]{2,1,0:T(8,128)(2,1)S(1)}, u32[]{:S(2)}, u32[]{:S(2)}) collective-permute-start(bf16[1,136,128]{2,1,0:T(8,128)(2,1)S(1)} %get-tuple-element.12), channel_id=1, source_target_pairs={{0,24},{1,25},{2,26},{3,27},{4,28},{5,29},{6,30},{7,31},{8,16},{9,... | collective-permute-start | bytes 104456 | tf_op jit(solution)/shard_map/ppermute | solution.py:274
  5.9 5.0 %collective-permute-start.1 = (bf16[1,136,128]{2,1,0:T(8,128)(2,1)S(1)}, bf16[1,136,128]{2,1,0:T(8,128)(2,1)S(1)}, u32[]{:S(2)}, u32[]{:S(2)}) collective-permute-start(bf16[1,136,128]{2,1,0:T(8,128)(2,1)S(1)} %get-tuple-element.12), channel_id=1, source_target_pairs={{0,8},{1,9},{2,10},{3,11},{4,12},{5,13},{6,14},{7,15},{8,0},{9,1},... | collective-permute-start | bytes 104456 | tf_op jit(solution)/shard_map/ppermute | solution.py:274
  5.9 5.0 %collective-permute-start = (bf16[1,136,128]{2,1,0:T(8,128)(2,1)S(1)}, bf16[1,136,128]{2,1,0:T(8,128)(2,1)S(1)}, u32[]{:S(2)}, u32[]{:S(2)}) collective-permute-start(bf16[1,136,128]{2,1,0:T(8,128)(2,1)S(1)} %get-tuple-element.12), channel_id=1, source_target_pairs={{0,16},{1,17},{2,18},{3,19},{4,20},{5,21},{6,22},{7,23},{8,24},{9,... | collective-permute-start | bytes 104456 | tf_op jit(solution)/shard_map/ppermute | solution.py:274
  11.0 6.2 %collective-permute-start.3 = (bf16[4,128,128]{2,1,0:T(8,128)(2,1)S(1)}, bf16[4,128,128]{2,1,0:T(8,128)(2,1)S(1)}, u32[]{:S(2)}, u32[]{:S(2)}) collective-permute-start(bf16[4,128,128]{2,1,0:T(8,128)(2,1)S(1)} %pad_maximum_fusion), channel_id=1, source_target_pairs={{0,2},{1,3},{2,0},{3,1},{4,6},{5,7},{6,4},{7,5},{8,10},{9,11},{10,... | collective-permute-start | bytes 393224 | tf_op jit(solution)/shard_map/ppermute | solution.py:274
  12.6 6.0 %collective-permute-start.4 = (bf16[4,136,128]{2,1,0:T(8,128)(2,1)S(1)}, bf16[4,136,128]{2,1,0:T(8,128)(2,1)S(1)}, u32[]{:S(2)}, u32[]{:S(2)}) collective-permute-start(bf16[4,136,128]{2,1,0:T(8,128)(2,1)S(1)} %constant_dynamic-update-slice_fusion.own), channel_id=1, source_target_pairs={{0,4},{1,5},{2,6},{3,7},{4,0},{5,1},{6,2},{7,3},{8,12},{9,13},{10,... | collective-permute-start | bytes 417800 | tf_op jit(solution)/shard_map/ppermute | solution.py:274
  14.2 5.9 %collective-permute-start.5 = (bf16[4,128,128]{2,1,0:T(8,128)(2,1)S(1)}, bf16[4,128,128]{2,1,0:T(8,128)(2,1)S(1)}, u32[]{:S(2)}, u32[]{:S(2)}) collective-permute-start(bf16[4,128,128]{2,1,0:T(8,128)(2,1)S(1)} %pad_maximum_fusion), channel_id=1, source_target_pairs={{0,6},{1,7},{2,4},{3,5},{4,2},{5,3},{6,0},{7,1},{8,14},{9,15},{10,... | collective-permute-start | bytes 393224 | tf_op jit(solution)/shard_map/ppermute | solution.py:274
  17.2 2.9 %copy-start.2 = (bf16[512,256]{1,0:T(8,128)(2,1)S(1)}, bf16[512,256]{1,0:T(8,128)(2,1)}, u32[]{:S(2)}) copy-start(bf16[512,256]{1,0:T(8,128)(2,1)} %constant.6.clone.forward) | copy-start | bytes 786436
  18.6 1.6 %copy-start = (bf16[256,256]{1,0:T(8,128)(2,1)S(1)}, bf16[256,256]{1,0:T(8,128)(2,1)}, u32[]{:S(2)}) copy-start(bf16[256,256]{1,0:T(8,128)(2,1)} %constant.7.clone.band) | copy-start | bytes 393220
  20.1 2.0 %copy-start.1 = (bf16[256,512]{1,0:T(8,128)(2,1)S(1)}, bf16[256,512]{1,0:T(8,128)(2,1)}, u32[]{:S(2)}) copy-start(bf16[256,512]{1,0:T(8,128)(2,1)} %constant.8.clone.inverse) | copy-start | bytes 786436
  20.1 2.0 %collective-permute-start.6 = (bf16[16,128,128]{2,1,0:T(8,128)(2,1)S(1)}, bf16[16,128,128]{2,1,0:T(8,128)(2,1)S(1)}, u32[]{:S(2)}, u32[]{:S(2)}) collective-permute-start(bf16[16,128,128]{2,1,0:T(8,128)(2,1)S(1)} %constant_dynamic-update-slice_fusion.4), channel_id=1, source_target_pairs={{0,1},{1,0},{2,3},{3,2},{4,5},{5,4},{6,7},{7,6},{8,9},{9,8},{10,11... | collective-permute-start | bytes 1572872 | tf_op jit(solution)/shard_map/ppermute | solution.py:274

commit v3 on v2

--- a/solution.py
+++ b/solution.py
@@ -118,8 +118,8 @@
 
 
 RECV = 4
-KB = 8
 WIDTH = 2 * SMOOTH + 1
+DEEP = 128
 
 
 def label_kernel(order, pairs, raw, out, keep):
@@ -154,19 +154,58 @@
         spec[i, 1] = im
         pows[i] = power.astype(jnp.bfloat16)
         levels.append(jnp.sum(power.reshape(bins // 8, 8, 2 * SRC), axis=0))
+    blocks, _, rows, _ = white.shape
+    kb = bins // blocks
     for i in range(len(items)):
         level = jnp.sum(levels[i], axis=0, keepdims=True) * (0.1 * WIDTH / bins) + 1e-6 * WIDTH
         smoothed = jnp.dot(band[...], pows[i], preferred_element_type=jnp.float32)
         scale = lax.rsqrt(smoothed + level)
         for part in range(2):
             value = spec[i, part] * scale
-            left = value[:, 0:SRC].reshape(bins // KB, KB, SRC)
-            right = value[:, SRC:].reshape(bins // KB, KB, SRC)
+            left = value[:, 0:SRC].reshape(blocks, kb, SRC)
+            right = value[:, SRC:].reshape(blocks, kb, SRC)
             both = jnp.concatenate([left, right], axis=1).astype(jnp.bfloat16)
-            white[:, part, 2 * KB * i : 2 * KB * (i + 1), :] = both
-
-
-def own_kernel(own, near, other, diag, forward, band, white, fwd, perm, select, spec, pows):
+            white[:, part, 2 * kb * i : 2 * kb * (i + 1), :] = both
+
+
+def receiver_products(white, select, pick):
+    blocks, parts, rows, _ = white.shape
+    kb = SEG // blocks
+    deep = parts * rows
+    lane = lax.broadcasted_iota(jnp.int32, (kb * RECV, deep), 1)
+    sub = lax.broadcasted_iota(jnp.int32, (kb * RECV, deep), 0)
+    same = (lane % kb == sub % kb).astype(jnp.float32)
+    sign = jnp.where(lane < rows, 1.0, -1.0)
+    for g in range(0, blocks, 2):
+        sources = white[g : g + 2].reshape(2 * deep, SRC)
+        both = lax.dot_general(
+            select, sources, (((1,), (1,)), ((), ())), preferred_element_type=jnp.float32
+        )
+        for u in range(2):
+            v = both[:, u * deep : (u + 1) * deep] * same
+            turned = pltpu.roll(v, rows, 1) * sign
+            pick[g + u, 0 : kb * RECV, :] = v.astype(jnp.bfloat16)
+            pick[g + u, kb * RECV :, :] = turned.astype(jnp.bfloat16)
+    sums = [
+        jnp.dot(pick[g], white[g].reshape(deep, SRC), preferred_element_type=jnp.float32)
+        for g in range(blocks)
+    ]
+    return [
+        jnp.concatenate([s[at * kb : (at + 1) * kb] for s in sums], axis=0)
+        for at in range(2 * RECV)
+    ]
+
+
+def pair_items(first, second, half):
+    return [
+        (first[z, 0:half], second[z, 0:half], first[z + 1, 0:half], second[z + 1, 0:half])
+        for z in range(0, first.shape[0], 2)
+    ]
+
+
+def window_kernel(
+    own, near, forward, band, partial, fwd, perm, chosen, white, pick, spec, pows
+):
     half = forward.shape[1] // 2
     zb = own.shape[0]
     ch = lax.axis_index("ch")
@@ -183,22 +222,33 @@
     dest = dest.astype(jnp.float32)[0:1, :]
     rows = lax.broadcasted_iota(jnp.int32, (SRC, SRC), 0)
     perm[...] = (rows.astype(jnp.float32) == dest).astype(jnp.bfloat16)
-    wanted = (lax.broadcasted_iota(jnp.int32, (KB * RECV, SRC), 0) // KB + base).astype(jnp.float32)
-    select[...] = (wanted == dest).astype(jnp.bfloat16)
-
-    items = [(own[z, 0:half], near[z, 0:half], other[z], diag[z]) for z in range(zb)]
+    wanted = lax.broadcasted_iota(jnp.int32, chosen.shape, 0) * RECV // chosen.shape[0] + base
+    chosen[...] = (wanted.astype(jnp.float32) == dest).astype(jnp.bfloat16)
+
+    whiten_group(pair_items(own, near, half), fwd, band, spec, pows, white)
+    for at, value in enumerate(receiver_products(white, chosen[...], pick)):
+        partial[at] = value
+
+
+def middle_kernel(sib, other, diag, fwd, band, chosen, before, partial, white, pick, spec, pows):
+    zb, half = other.shape[0:2]
+    items = pair_items(sib.at[0:zb], sib.at[zb : 2 * zb], half) + pair_items(other, diag, half)
     whiten_group(items, fwd, band, spec, pows, white)
+    each = RECV * SEG // white.shape[0]
+    step = chosen.shape[0] // RECV
+    select = jnp.concatenate(
+        [chosen[q * step : q * step + each // RECV, :] for q in range(RECV)], axis=0
+    )
+    for at, value in enumerate(receiver_products(white, select, pick)):
+        partial[at] = before[at] + value
 
 
 def cross_kernel(
-    keep, sib, own_white, fwd, perm, select, band, inverse, out,
+    keep, sib, before, fwd, perm, chosen, band, inverse, out,
     white, pick, cross, lags, blank, spec, pows, sems,
 ):
     bins = band.shape[0]
-    zb = sib.shape[0] // 4
-    count = 4 * zb
-    blocks = bins // KB
-    deep = 2 * count * KB
+    zb, half = sib.shape[0] // 2, sib.shape[1]
 
     blank[...] = jnp.zeros(blank.shape, blank.dtype)
     copies = [
@@ -207,33 +257,14 @@
     for copy in copies:
         copy.start()
 
-    items = [(sib[z], sib[2 * zb + z], sib[zb + z], sib[3 * zb + z]) for z in range(zb)]
-    whiten_group(items, fwd, band, spec, pows, white)
-
-    def both(kb):
-        return jnp.concatenate(
-            [own_white[kb, 0], white[kb, 0], own_white[kb, 1], white[kb, 1]], axis=0
-        )
-
-    lane = lax.broadcasted_iota(jnp.int32, (KB * RECV, deep), 1) % KB
-    sub = lax.broadcasted_iota(jnp.int32, (KB * RECV, deep), 0) % KB
-    same = (lane == sub).astype(jnp.float32)
-    for kb in range(blocks):
-        v = lax.dot_general(
-            select[...], both(kb), (((1,), (1,)), ((), ())), preferred_element_type=jnp.float32
-        )
-        v = v * same
-        pick[kb, 0 : KB * RECV, :] = v.astype(jnp.bfloat16)
-        turned = jnp.concatenate([v[:, deep // 2 :], -v[:, 0 : deep // 2]], axis=1)
-        pick[kb, KB * RECV :, :] = turned.astype(jnp.bfloat16)
-
-    sums = [jnp.dot(pick[kb], both(kb), preferred_element_type=jnp.float32) for kb in range(blocks)]
-    for part in range(2):
-        for q in range(RECV):
-            at = (part * RECV + q) * KB
-            column = jnp.concatenate([s[at : at + KB] for s in sums], axis=0) * (WIDTH / count)
-            lanes = slice((q % 2) * SRC, (q % 2 + 1) * SRC)
-            cross[q // 2, part * bins : (part + 1) * bins, lanes] = column.astype(jnp.bfloat16)
+    whiten_group(
+        pair_items(sib.at[0:zb], sib.at[zb : 2 * zb], half), fwd, band, spec, pows, white
+    )
+    for at, value in enumerate(receiver_products(white, chosen[...], pick)):
+        total = (before[at] + value) * (WIDTH / (4 * zb))
+        part, q = at // RECV, at % RECV
+        lanes = slice((q % 2) * SRC, (q % 2 + 1) * SRC)
+        cross[q // 2, part * bins : (part + 1) * bins, lanes] = total.astype(jnp.bfloat16)
 
     for p in range(RECV // 2):
         turned = jnp.dot(inverse[...], cross[p], preferred_element_type=jnp.float32) * keep[0:1, :]
@@ -276,43 +307,60 @@
     parts = [block, swap(block, 4, 0), swap(block, 2, 0), swap(block, 6, 0)]
     own = jnp.concatenate(parts, axis=0)
     bare = jnp.concatenate([p[:, 0:half] for p in parts], axis=0)
+    near = swap(own, 1, 0)
     diag = swap(bare, 1, 2)
-    near = swap(own, 1, 0)
     other = swap(bare, 0, 2)
-    sib = swap(jnp.concatenate([bare, other, near[:, 0:half], diag], axis=0), 0, 1)
+    first_sib = swap(jnp.concatenate([bare, near[:, 0:half]], axis=0), 0, 1)
 
     forward, inverse, band = transform_tables(SEG, LAGS, SMOOTH)
     forward, band, inverse = [
         jnp.asarray(np.ascontiguousarray(t), jnp.bfloat16) for t in (forward.T, band, inverse.T)
     ]
     zb = own.shape[0]
-    blocks = SEG // KB
-    white = pltpu.VMEM((blocks, 2, 2 * zb * KB, SRC), jnp.bfloat16)
-    work = [
-        pltpu.VMEM((zb, 2, SEG, 2 * SRC), jnp.float32),
-        pltpu.VMEM((zb, SEG, 2 * SRC), jnp.bfloat16),
-    ]
-    own_white, fwd, perm, select = pl.pallas_call(
-        own_kernel,
+
+    def scratch(segments):
+        kb = DEEP // (2 * segments)
+        return [
+            pltpu.VMEM((SEG // kb, 2, DEEP // 2, SRC), jnp.bfloat16),
+            pltpu.VMEM((SEG // kb, 2 * RECV * kb, DEEP), jnp.bfloat16),
+        ], [
+            pltpu.VMEM((segments // 2, 2, SEG, 2 * SRC), jnp.float32),
+            pltpu.VMEM((segments // 2, SEG, 2 * SRC), jnp.bfloat16),
+        ]
+
+    partial = pltpu.VMEM((2 * RECV, SEG, SRC), jnp.float32)
+    spectra, work = scratch(zb)
+    before, fwd, perm, chosen = pl.pallas_call(
+        window_kernel,
         out_shape=[
-            white,
+            partial,
             pltpu.VMEM((2 * SEG, SEG), jnp.bfloat16),
             pltpu.VMEM((SRC, SRC), jnp.bfloat16),
-            pltpu.VMEM((KB * RECV, SRC), jnp.bfloat16),
+            pltpu.VMEM((RECV * DEEP // (2 * zb), SRC), jnp.bfloat16),
         ],
-        in_specs=[vmem] * 6,
+        in_specs=[vmem] * 4,
         out_specs=[vmem] * 4,
-        scratch_shapes=work,
+        scratch_shapes=[*spectra, *work],
         compiler_params=params,
-    )(own, near, other, diag, forward, band)
+    )(own, near, forward, band)
+    other, diag, chosen = lax.optimization_barrier((other, diag, chosen))
+    second_sib = swap(jnp.concatenate([other, diag], axis=0), 0, 1)
+    many_spectra, many_work = scratch(2 * zb)
+    before = pl.pallas_call(
+        middle_kernel,
+        out_shape=partial,
+        in_specs=[vmem] * 7,
+        out_specs=vmem,
+        scratch_shapes=[*many_spectra, *many_work],
+        compiler_params=params,
+    )(first_sib, other, diag, fwd, band, chosen, before)
     return pl.pallas_call(
         cross_kernel,
         out_shape=jax.ShapeDtypeStruct((RECV, MAXP, SRC, LAGS), jnp.bfloat16),
         in_specs=[vmem] * 8,
         out_specs=pl.BlockSpec(memory_space=pl.ANY),
         scratch_shapes=[
-            white,
-            pltpu.VMEM((blocks, 2 * RECV * KB, 8 * zb * KB), jnp.bfloat16),
+            *spectra,
             pltpu.VMEM((RECV // 2, 2 * SEG, 2 * SRC), jnp.bfloat16),
             pltpu.VMEM((RECV, SRC, LAGS), jnp.bfloat16),
             pltpu.VMEM((MAXP - 1, SRC, LAGS), jnp.bfloat16),
@@ -320,7 +368,7 @@
             pltpu.SemaphoreType.DMA((2 * RECV,)),
         ],
         compiler_params=params,
-    )(keep, sib, own_white, fwd, perm, select, band, inverse)
+    )(keep, second_sib, before, fwd, perm, chosen, band, inverse)
 
 
 def local(raw, order, pair_blocks):

time: 25.4 us -> 23.4 us (0.921)
  waiting for transfers between devices: 10.9 us -> 6.99 us
  Pallas kernels: 4.62 us -> 5.61 us
  local copies, waits for them, and re-layouts: 0.16 us -> 0.91 us
    ppermute x7 -> x8, waiting for transfers between devices: 10.9 us -> 6.99 us  [swap(): lax.ppermute(value, ('ch', 'grp'), [(d, d ^ flip) for d in range(total)])]
    pallas_call x1 -> x2, Pallas kernels: 0.65 us -> 2.34 us  [the longest x1 1.32 us: one_block(): pl.pallas_call(middle_kernel, out_shape=partial, in_specs=[vmem] * 7, out...]
    unnamed x11 -> x13, local copies, waits for them, and re-layouts: 0.08 us -> 0.88 us
    pallas_call x1, Pallas kernels: 3.18 us -> 2.48 us  [one_block(): pl.pallas_call(cross_kernel, out_shape=jax.ShapeDtypeStruct((RECV, MAXP,...]
    ppermute x7 -> x8, starting transfers between devices: 9.45 us -> 9.52 us  [swap(): lax.ppermute(value, ('ch', 'grp'), [(d, d ^ flip) for d in range(total)])]
  transfers between devices with their start and end apart: 7 -> 8, of which waited for: 5 -> 4; matrix products, arithmetic and copies ran while one was open for 0% -> 1% of each run, Pallas kernels for 3% -> 10%
where the time goes in v3:
time: 23.4 us; the launch traced here: 23.2 us
  starting transfers between devices  9.52 us (41%)
  waiting for transfers between devices  6.99 us (30%)
  Pallas kernels  5.61 us (24%)
  local copies, waits for them, and re-layouts  0.91 us (4%)
    ppermute x8, starting transfers between devices, swap(): lax.ppermute(value, ('ch', 'grp'), [(d, d ^ flip) for d in range(total)])  9.52 us
    ppermute x8, waiting for transfers between devices, swap(): lax.ppermute(value, ('ch', 'grp'), [(d, d ^ flip) for d in range(total)])  6.99 us
    pallas_call x1, Pallas kernels, one_block(): pl.pallas_call(cross_kernel, out_shape=jax.ShapeDtypeStruct((RECV, MAXP,...  2.48 us
    pallas_call x1, Pallas kernels, one_block(): pl.pallas_call(middle_kernel, out_shape=partial, in_specs=[vmem] * 7, out...  1.32 us
    pallas_call x1, Pallas kernels, one_block(): pl.pallas_call(window_kernel, out_shape=[partial, pltpu.VMEM((2 * SEG, SE...  1.02 us
    unnamed x13, local copies, waits for them, and re-layouts  0.88 us
    pallas_call x1, Pallas kernels, one_block(): pl.pallas_call(label_kernel, out_shape=[pltpu.VMEM((1, half + 8, channels...  0.78 us
  transfers between devices with their start and end apart: 8, of which 4 were waited for; matrix products, arithmetic and copies ran while one was open for 1% of the time, Pallas kernels for 10%

profile of v3, /device:TPU:0, one launch (start us, length us, event | category | flops | bytes accessed | tf_op | source)
XLA Modules:
  0.0 23.2 jit_solution(13889410495555730400)
XLA Ops:
  0.0 0.8 %shard_map.64 = (bf16[1,136,128]{2,1,0:T(8,128)(2,1)S(1)}, f32[8,256]{1,0:T(8,128)S(1)}) custom-call(s32[1,16]{1,0:T(1,128)} %order.1, s32[1,3]{1,0:T(1,128)} %pairs.1, bf16[1,128,128]{2,1,0:T(8,128)(2,1)} %raw.1), custom_call_target="tpu_custom_call" | custom-call | tf_op jit(solution)/shard_map/pallas_call | solution.py:296
  0.8 5.1 %collective-permute-start.2 = (bf16[1,136,128]{2,1,0:T(8,128)(2,1)S(1)}, bf16[1,136,128]{2,1,0:T(8,128)(2,1)S(1)}, u32[]{:S(2)}, u32[]{:S(2)}) collective-permute-start(bf16[1,136,128]{2,1,0:T(8,128)(2,1)S(1)} %get-tuple-element.15), channel_id=1, source_target_pairs={{0,24},{1,25},{2,26},{3,27},{4,28},{5,29},{6,30},{7,31},{8,16},{9,... | collective-permute-start | bytes 104456 | tf_op jit(solution)/shard_map/ppermute | solution.py:305
  5.9 0.0 collective-permute-start.1
  5.9 0.6 %collective-permute-start = (bf16[1,136,128]{2,1,0:T(8,128)(2,1)S(1)}, bf16[1,136,128]{2,1,0:T(8,128)(2,1)S(1)}, u32[]{:S(2)}, u32[]{:S(2)}) collective-permute-start(bf16[1,136,128]{2,1,0:T(8,128)(2,1)S(1)} %get-tuple-element.15), channel_id=1, source_target_pairs={{0,16},{1,17},{2,18},{3,19},{4,20},{5,21},{6,22},{7,23},{8,24},{9,... | collective-permute-start | bytes 104456 | tf_op jit(solution)/shard_map/ppermute | solution.py:305
  6.6 4.3 %collective-permute-done = bf16[1,136,128]{2,1,0:T(8,128)(2,1)S(1)} collective-permute-done((bf16[1,136,128]{2,1,0:T(8,128)(2,1)S(1)}, bf16[1,136,128]{2,1,0:T(8,128)(2,1)S(1)}, u32[]{:S(2)}, u32[]{:S(2)}) %collective-permute-start) | collective-permute-done | bytes 34848 | tf_op jit(solution)/shard_map/ppermute | solution.py:305
  10.9 0.0 collective-permute-done.1
  10.9 0.0 collective-permute-done.2
  10.9 1.6 %collective-permute-start.5 = (bf16[4,136,128]{2,1,0:T(8,128)(2,1)S(1)}, bf16[4,136,128]{2,1,0:T(8,128)(2,1)S(1)}, u32[]{:S(2)}, u32[]{:S(2)}) collective-permute-start(bf16[4,136,128]{2,1,0:T(8,128)(2,1)S(1)} %constant_dynamic-update-slice_fusion.own), channel_id=1, source_target_pairs={{0,4},{1,5},{2,6},{3,7},{4,0},{5,1},{6,2},{7,3},{8,12},{9,13},{10,... | collective-permute-start | bytes 417800 | tf_op jit(solution)/shard_map/ppermute | solution.py:305
  12.6 0.0 copy-start.1
  12.6 1.5 %collective-permute-start.4 = (bf16[4,128,128]{2,1,0:T(8,128)(2,1)S(1)}, bf16[4,128,128]{2,1,0:T(8,128)(2,1)S(1)}, u32[]{:S(2)}, u32[]{:S(2)}) collective-permute-start(bf16[4,128,128]{2,1,0:T(8,128)(2,1)S(1)} %pad_maximum_fusion.1), channel_id=1, source_target_pairs={{0,6},{1,7},{2,4},{3,5},{4,2},{5,3},{6,0},{7,1},{8,14},{9,15},{10,... | collective-permute-start | bytes 393224 | tf_op jit(solution)/shard_map/ppermute | solution.py:305
  14.1 0.5 %collective-permute-start.3 = (bf16[4,128,128]{2,1,0:T(8,128)(2,1)S(1)}, bf16[4,128,128]{2,1,0:T(8,128)(2,1)S(1)}, u32[]{:S(2)}, u32[]{:S(2)}) collective-permute-start(bf16[4,128,128]{2,1,0:T(8,128)(2,1)S(1)} %pad_maximum_fusion.1), channel_id=1, source_target_pairs={{0,2},{1,3},{2,0},{3,1},{4,6},{5,7},{6,4},{7,5},{8,10},{9,11},{10,... | collective-permute-start | bytes 393224 | tf_op jit(solution)/shard_map/ppermute | solution.py:305
  14.7 2.4 %collective-permute-done.5.near = bf16[4,136,128]{2,1,0:T(8,128)(2,1)S(1)} collective-permute-done((bf16[4,136,128]{2,1,0:T(8,128)(2,1)S(1)}, bf16[4,136,128]{2,1,0:T(8,128)(2,1)S(1)}, u32[]{:S(2)}, u32[]{:S(2)}) %collective-permute-start.5) | collective-permute-done | bytes 139296 | tf_op jit(solution)/shard_map/ppermute | solution.py:305
  17.1 0.1 collective-permute-start.7
  17.2 0.0 copy-done.1
  17.2 0.8 %copy-done = bf16[256,256]{1,0:T(8,128)(2,1)S(1)} copy-done((bf16[256,256]{1,0:T(8,128)(2,1)S(1)}, bf16[256,256]{1,0:T(8,128)(2,1)}, u32[]{:S(2)}) %copy-start) | copy-done | bytes 131096
  18.0 1.0 %shard_map.65 = (f32[8,256,128]{2,1,0:T(8,128)S(1)}, bf16[512,256]{1,0:T(8,128)(2,1)S(1)}, bf16[128,128]{1,0:T(8,128)(2,1)S(1)}, bf16[64,128]{1,0:T(8,128)(2,1)S(1)}) custom-call(bf16[4,136,128]{2,1,0:T(8,128)(2,1)S(1)} %constant_dynamic-update-slice_fusion.own, bf16[4,136,128]{2,1,0:T(8,128)(2,1)S(1)} %collective-permute-done.5.near, ...), custom_call_target="tpu_custom_call" | custom-call | tf_op jit(solution)/shard_map/pallas_call | solution.py:333
  19.0 0.0 collective-permute-done.4.diag
  19.0 0.1 collective-permute-done.3.other
  19.1 0.1 collective-permute-start.6
  19.2 0.0 collective-permute-done.7.sib
  19.2 0.0 copy-start.2
  19.2 1.3 %shard_map.66.before = f32[8,256,128]{2,1,0:T(8,128)S(1)} custom-call(bf16[8,128,128]{2,1,0:T(8,128)(2,1)S(1)} %collective-permute-done.7.sib, bf16[4,128,128]{2,1,0:T(8,128)(2,1)S(1)} %collective-permute-done.3.other, bf16[4,128,128]{2,1,0:T(8,128)(2,1)S(1)} %collective-permute-done.4.diag, bf16[512,256]{1,0:T(8,128)(2,1)S(1)} %get-tuple-element.19.fwd, ...), custom_call_target="tpu_custom_call" | custom-call | tf_op jit(solution)/shard_map/pallas_call | solution.py:349
  20.5 0.2 collective-permute-done.6.sib
  20.7 2.5 %shard_map.67 = bf16[4,3,128,256]{3,2,1,0:T(8,128)(2,1)} custom-call(f32[8,256]{1,0:T(8,128)S(1)} %get-tuple-element.14.keep, bf16[8,128,128]{2,1,0:T(8,128)(2,1)S(1)} %collective-permute-done.6.sib, f32[8,256,128]{2,1,0:T(8,128)S(1)} %shard_map.66.before, bf16[512,256]{1,0:T(8,128)(2,1)S(1)} %get-tuple-element.19.fwd, ...), custom_call_target="tpu_custom_call" | custom-call | tf_op jit(solution)/shard_map/pallas_call | solution.py:357
  (13 shorter events, 0.2 us)
Async XLA Ops:
  0.8 10.1 %collective-permute-start.2 = (bf16[1,136,128]{2,1,0:T(8,128)(2,1)S(1)}, bf16[1,136,128]{2,1,0:T(8,128)(2,1)S(1)}, u32[]{:S(2)}, u32[]{:S(2)}) collective-permute-start(bf16[1,136,128]{2,1,0:T(8,128)(2,1)S(1)} %get-tuple-element.15), channel_id=1, source_target_pairs={{0,24},{1,25},{2,26},{3,27},{4,28},{5,29},{6,30},{7,31},{8,16},{9,... | collective-permute-start | bytes 104456 | tf_op jit(solution)/shard_map/ppermute | solution.py:305
  5.9 5.0 %collective-permute-start.1 = (bf16[1,136,128]{2,1,0:T(8,128)(2,1)S(1)}, bf16[1,136,128]{2,1,0:T(8,128)(2,1)S(1)}, u32[]{:S(2)}, u32[]{:S(2)}) collective-permute-start(bf16[1,136,128]{2,1,0:T(8,128)(2,1)S(1)} %get-tuple-element.15), channel_id=1, source_target_pairs={{0,8},{1,9},{2,10},{3,11},{4,12},{5,13},{6,14},{7,15},{8,0},{9,1},... | collective-permute-start | bytes 104456 | tf_op jit(solution)/shard_map/ppermute | solution.py:305
  5.9 5.0 %collective-permute-start = (bf16[1,136,128]{2,1,0:T(8,128)(2,1)S(1)}, bf16[1,136,128]{2,1,0:T(8,128)(2,1)S(1)}, u32[]{:S(2)}, u32[]{:S(2)}) collective-permute-start(bf16[1,136,128]{2,1,0:T(8,128)(2,1)S(1)} %get-tuple-element.15), channel_id=1, source_target_pairs={{0,16},{1,17},{2,18},{3,19},{4,20},{5,21},{6,22},{7,23},{8,24},{9,... | collective-permute-start | bytes 104456 | tf_op jit(solution)/shard_map/ppermute | solution.py:305
  10.9 6.1 %collective-permute-start.5 = (bf16[4,136,128]{2,1,0:T(8,128)(2,1)S(1)}, bf16[4,136,128]{2,1,0:T(8,128)(2,1)S(1)}, u32[]{:S(2)}, u32[]{:S(2)}) collective-permute-start(bf16[4,136,128]{2,1,0:T(8,128)(2,1)S(1)} %constant_dynamic-update-slice_fusion.own), channel_id=1, source_target_pairs={{0,4},{1,5},{2,6},{3,7},{4,0},{5,1},{6,2},{7,3},{8,12},{9,13},{10,... | collective-permute-start | bytes 417800 | tf_op jit(solution)/shard_map/ppermute | solution.py:305
  12.6 4.6 %copy-start.1 = (bf16[512,256]{1,0:T(8,128)(2,1)S(1)}, bf16[512,256]{1,0:T(8,128)(2,1)}, u32[]{:S(2)}) copy-start(bf16[512,256]{1,0:T(8,128)(2,1)} %constant.6.clone.forward) | copy-start | bytes 786436
  12.6 6.4 %collective-permute-start.4 = (bf16[4,128,128]{2,1,0:T(8,128)(2,1)S(1)}, bf16[4,128,128]{2,1,0:T(8,128)(2,1)S(1)}, u32[]{:S(2)}, u32[]{:S(2)}) collective-permute-start(bf16[4,128,128]{2,1,0:T(8,128)(2,1)S(1)} %pad_maximum_fusion.1), channel_id=1, source_target_pairs={{0,6},{1,7},{2,4},{3,5},{4,2},{5,3},{6,0},{7,1},{8,14},{9,15},{10,... | collective-permute-start | bytes 393224 | tf_op jit(solution)/shard_map/ppermute | solution.py:305
  14.1 5.0 %collective-permute-start.3 = (bf16[4,128,128]{2,1,0:T(8,128)(2,1)S(1)}, bf16[4,128,128]{2,1,0:T(8,128)(2,1)S(1)}, u32[]{:S(2)}, u32[]{:S(2)}) collective-permute-start(bf16[4,128,128]{2,1,0:T(8,128)(2,1)S(1)} %pad_maximum_fusion.1), channel_id=1, source_target_pairs={{0,2},{1,3},{2,0},{3,1},{4,6},{5,7},{6,4},{7,5},{8,10},{9,11},{10,... | collective-permute-start | bytes 393224 | tf_op jit(solution)/shard_map/ppermute | solution.py:305
  17.1 0.9 %copy-start = (bf16[256,256]{1,0:T(8,128)(2,1)S(1)}, bf16[256,256]{1,0:T(8,128)(2,1)}, u32[]{:S(2)}) copy-start(bf16[256,256]{1,0:T(8,128)(2,1)} %constant.7.clone.band) | copy-start | bytes 393220
  17.1 2.1 %collective-permute-start.7 = (bf16[8,128,128]{2,1,0:T(8,128)(2,1)S(1)}, bf16[8,128,128]{2,1,0:T(8,128)(2,1)S(1)}, u32[]{:S(2)}, u32[]{:S(2)}) collective-permute-start(bf16[8,128,128]{2,1,0:T(8,128)(2,1)S(1)} %slice_dynamic-update-slice_fusion), channel_id=1, source_target_pairs={{0,1},{1,0},{2,3},{3,2},{4,5},{5,4},{6,7},{7,6},{8,9},{9,8},{10,11... | collective-permute-start | bytes 786440 | tf_op jit(solution)/shard_map/ppermute | solution.py:305
  19.1 1.6 %collective-permute-start.6 = (bf16[8,128,128]{2,1,0:T(8,128)(2,1)S(1)}, bf16[8,128,128]{2,1,0:T(8,128)(2,1)S(1)}, u32[]{:S(2)}, u32[]{:S(2)}) collective-permute-start(bf16[8,128,128]{2,1,0:T(8,128)(2,1)S(1)} %pad_maximum_fusion), channel_id=1, source_target_pairs={{0,1},{1,0},{2,3},{3,2},{4,5},{5,4},{6,7},{7,6},{8,9},{9,8},{10,11... | collective-permute-start | bytes 786440 | tf_op jit(solution)/shard_map/ppermute | solution.py:305
  19.2 1.5 %copy-start.2 = (bf16[256,512]{1,0:T(8,128)(2,1)S(1)}, bf16[256,512]{1,0:T(8,128)(2,1)}, u32[]{:S(2)}) copy-start(bf16[256,512]{1,0:T(8,128)(2,1)} %constant.8.clone.inverse) | copy-start | bytes 786436

commit v4 on v3

--- a/solution.py
+++ b/solution.py
@@ -136,6 +136,23 @@
     out[0, half : half + 8, :] = row.astype(jnp.float32).astype(out.dtype)
 
 
+def tables_kernel(forward, band_from, inverse_from, fwd, band, inverse, sems):
+    half = forward.shape[1] // 2
+    mine = lax.axis_index("ch") % 2
+    near = forward.at[:, pl.ds(pl.multiple_of(mine * half, half), half)]
+    far = forward.at[:, pl.ds(pl.multiple_of((1 - mine) * half, half), half)]
+    copies = [
+        pltpu.make_async_copy(near, fwd.at[:, 0:half], sems.at[0]),
+        pltpu.make_async_copy(far, fwd.at[:, half : 2 * half], sems.at[1]),
+        pltpu.make_async_copy(band_from, band, sems.at[2]),
+        pltpu.make_async_copy(inverse_from, inverse, sems.at[3]),
+    ]
+    for copy in copies:
+        copy.start()
+    for copy in copies:
+        copy.wait()
+
+
 def whiten_group(items, fwd, band, spec, pows, white):
     bins = band.shape[0]
     levels = []
@@ -204,15 +221,12 @@
 
 
 def window_kernel(
-    own, near, forward, band, partial, fwd, perm, chosen, white, pick, spec, pows
+    own, near, fwd, band, partial, perm, chosen, white, pick, spec, pows
 ):
-    half = forward.shape[1] // 2
+    half = fwd.shape[1] // 2
     zb = own.shape[0]
     ch = lax.axis_index("ch")
     base = (ch * lax.axis_size("grp") + lax.axis_index("grp")) * RECV
-    mine = ch % 2
-    fwd[:, 0:half] = forward[:, pl.ds(pl.multiple_of(mine * half, half), half)]
-    fwd[:, half:] = forward[:, pl.ds(pl.multiple_of((1 - mine) * half, half), half)]
 
     dest = own[0, half : half + 8, :]
     for z in range(1, zb):
@@ -266,20 +280,16 @@
         lanes = slice((q % 2) * SRC, (q % 2 + 1) * SRC)
         cross[q // 2, part * bins : (part + 1) * bins, lanes] = total.astype(jnp.bfloat16)
 
-    for p in range(RECV // 2):
-        turned = jnp.dot(inverse[...], cross[p], preferred_element_type=jnp.float32) * keep[0:1, :]
-        turned = turned.astype(jnp.bfloat16)
-        for u in range(2):
-            q = 2 * p + u
-            lags[q] = lax.dot_general(
-                perm[...],
-                turned[:, u * SRC : (u + 1) * SRC],
-                (((1,), (1,)), ((), ())),
-                preferred_element_type=jnp.float32,
-            ).astype(jnp.bfloat16)
-            copy = pltpu.make_async_copy(lags.at[q], out.at[q, 0], sems.at[RECV + q])
-            copy.start()
-            copies.append(copy)
+    for q in range(RECV):
+        held = cross[q // 2, :, (q % 2) * SRC : (q % 2 + 1) * SRC]
+        turned = lax.dot_general(
+            perm[...], held, (((1,), (1,)), ((), ())), preferred_element_type=jnp.float32
+        ).astype(jnp.bfloat16)
+        lag_values = jnp.dot(turned, inverse[...], preferred_element_type=jnp.float32)
+        lags[q] = (lag_values * keep[0:1, :]).astype(jnp.bfloat16)
+        copy = pltpu.make_async_copy(lags.at[q], out.at[q, 0], sems.at[RECV + q])
+        copy.start()
+        copies.append(copy)
     for copy in copies:
         copy.wait()
 
@@ -304,7 +314,21 @@
         flip = ch_bits * groups + grp_bits
         return lax.ppermute(value, ("ch", "grp"), [(d, d ^ flip) for d in range(total)])
 
-    parts = [block, swap(block, 4, 0), swap(block, 2, 0), swap(block, 6, 0)]
+    parts = [block, swap(block, 2, 0), swap(block, 6, 0), swap(block, 4, 0)]
+
+    forward, inverse, band = transform_tables(SEG, LAGS, SMOOTH)
+    forward, band, inverse = [
+        jnp.asarray(np.ascontiguousarray(t), jnp.bfloat16) for t in (forward.T, band, inverse)
+    ]
+    anywhere = pl.BlockSpec(memory_space=pl.ANY)
+    fwd, band, inverse = pl.pallas_call(
+        tables_kernel,
+        out_shape=[pltpu.VMEM(t.shape, t.dtype) for t in (forward, band, inverse)],
+        in_specs=[anywhere] * 3,
+        out_specs=[vmem] * 3,
+        scratch_shapes=[pltpu.SemaphoreType.DMA((4,))],
+    )(forward, band, inverse)
+    parts, fwd, band, inverse = lax.optimization_barrier((parts, fwd, band, inverse))
     own = jnp.concatenate(parts, axis=0)
     bare = jnp.concatenate([p[:, 0:half] for p in parts], axis=0)
     near = swap(own, 1, 0)
@@ -312,10 +336,6 @@
     other = swap(bare, 0, 2)
     first_sib = swap(jnp.concatenate([bare, near[:, 0:half]], axis=0), 0, 1)
 
-    forward, inverse, band = transform_tables(SEG, LAGS, SMOOTH)
-    forward, band, inverse = [
-        jnp.asarray(np.ascontiguousarray(t), jnp.bfloat16) for t in (forward.T, band, inverse.T)
-    ]
     zb = own.shape[0]
 
     def scratch(segments):
@@ -330,19 +350,18 @@
 
     partial = pltpu.VMEM((2 * RECV, SEG, SRC), jnp.float32)
     spectra, work = scratch(zb)
-    before, fwd, perm, chosen = pl.pallas_call(
+    before, perm, chosen = pl.pallas_call(
         window_kernel,
         out_shape=[
             partial,
-            pltpu.VMEM((2 * SEG, SEG), jnp.bfloat16),
             pltpu.VMEM((SRC, SRC), jnp.bfloat16),
             pltpu.VMEM((RECV * DEEP // (2 * zb), SRC), jnp.bfloat16),
         ],
         in_specs=[vmem] * 4,
-        out_specs=[vmem] * 4,
+        out_specs=[vmem] * 3,
         scratch_shapes=[*spectra, *work],
         compiler_params=params,
-    )(own, near, forward, band)
+    )(own, near, fwd, band)
     other, diag, chosen = lax.optimization_barrier((other, diag, chosen))
     second_sib = swap(jnp.concatenate([other, diag], axis=0), 0, 1)
     many_spectra, many_work = scratch(2 * zb)

time: 23.4 us -> 23 us (0.983)
  Pallas kernels: 5.61 us -> 6.6 us
  local copies, waits for them, and re-layouts: 0.91 us -> 0.1 us
  waiting for transfers between devices: 6.99 us -> 6.45 us
    pallas_call x1 -> x2, Pallas kernels: 1.02 us -> 2.2 us  [the longest x1 1.18 us: one_block(): pl.pallas_call(tables_kernel, out_shape=[pltpu.VMEM(t.shape, t.dtype) for...]
    unnamed x13 -> x7, local copies, waits for them, and re-layouts: 0.88 us -> 0.07 us
    ppermute x8, waiting for transfers between devices: 6.99 us -> 6.45 us  [swap(): lax.ppermute(value, ('ch', 'grp'), [(d, d ^ flip) for d in range(total)])]
  transfers between devices with their start and end apart: 8 -> 8, of which waited for: 4 -> 5; matrix products, arithmetic and copies ran while one was open for 1% -> 0% of each run, Pallas kernels for 10% -> 15%
where the time goes in v4:
time: 23 us; the launch traced here: 22.8 us
  starting transfers between devices  9.44 us (41%)
  Pallas kernels  6.6 us (29%)
  waiting for transfers between devices  6.45 us (28%)
    ppermute x8, starting transfers between devices, swap(): lax.ppermute(value, ('ch', 'grp'), [(d, d ^ flip) for d in range(total)])  9.44 us
    ppermute x8, waiting for transfers between devices, swap(): lax.ppermute(value, ('ch', 'grp'), [(d, d ^ flip) for d in range(total)])  6.45 us
    pallas_call x1, Pallas kernels, one_block(): pl.pallas_call(cross_kernel, out_shape=jax.ShapeDtypeStruct((RECV, MAXP,...  2.29 us
    pallas_call x1, Pallas kernels, one_block(): pl.pallas_call(middle_kernel, out_shape=partial, in_specs=[vmem] * 7, out...  1.32 us
    pallas_call x1, Pallas kernels, one_block(): pl.pallas_call(tables_kernel, out_shape=[pltpu.VMEM(t.shape, t.dtype) for...  1.18 us
    pallas_call x1, Pallas kernels, one_block(): pl.pallas_call(window_kernel, out_shape=[partial, pltpu.VMEM((SRC, SRC),...  1.02 us
    pallas_call x1, Pallas kernels, one_block(): pl.pallas_call(label_kernel, out_shape=[pltpu.VMEM((1, half + 8, channels...  0.78 us
  transfers between devices with their start and end apart: 8, of which 5 were waited for; matrix products, arithmetic and copies ran while one was open for 0% of the time, Pallas kernels for 15%

profile of v4, /device:TPU:0, one launch (start us, length us, event | category | flops | bytes accessed | tf_op | source)
XLA Modules:
  0.0 22.8 jit_solution(13513690098366097361)
XLA Ops:
  0.0 0.8 %shard_map.64 = (bf16[1,136,128]{2,1,0:T(8,128)(2,1)S(1)}, f32[8,256]{1,0:T(8,128)S(1)}) custom-call(s32[1,16]{1,0:T(1,128)} %order.1, s32[1,3]{1,0:T(1,128)} %pairs.1, bf16[1,128,128]{2,1,0:T(8,128)(2,1)} %raw.1), custom_call_target="tpu_custom_call" | custom-call | tf_op jit(solution)/shard_map/pallas_call | solution.py:306
  0.8 4.1 %collective-permute-start.2 = (bf16[1,136,128]{2,1,0:T(8,128)(2,1)S(1)}, bf16[1,136,128]{2,1,0:T(8,128)(2,1)S(1)}, u32[]{:S(2)}, u32[]{:S(2)}) collective-permute-start(bf16[1,136,128]{2,1,0:T(8,128)(2,1)S(1)} %get-tuple-element.28), channel_id=1, source_target_pairs={{0,16},{1,17},{2,18},{3,19},{4,20},{5,21},{6,22},{7,23},{8,24},{9,... | collective-permute-start | bytes 104456 | tf_op jit(solution)/shard_map/ppermute | solution.py:315
  4.9 1.3 %collective-permute-start.1 = (bf16[1,136,128]{2,1,0:T(8,128)(2,1)S(1)}, bf16[1,136,128]{2,1,0:T(8,128)(2,1)S(1)}, u32[]{:S(2)}, u32[]{:S(2)}) collective-permute-start(bf16[1,136,128]{2,1,0:T(8,128)(2,1)S(1)} %get-tuple-element.28), channel_id=1, source_target_pairs={{0,24},{1,25},{2,26},{3,27},{4,28},{5,29},{6,30},{7,31},{8,16},{9,... | collective-permute-start | bytes 104456 | tf_op jit(solution)/shard_map/ppermute | solution.py:315
  6.2 0.2 %collective-permute-start = (bf16[1,136,128]{2,1,0:T(8,128)(2,1)S(1)}, bf16[1,136,128]{2,1,0:T(8,128)(2,1)S(1)}, u32[]{:S(2)}, u32[]{:S(2)}) collective-permute-start(bf16[1,136,128]{2,1,0:T(8,128)(2,1)S(1)} %get-tuple-element.28), channel_id=1, source_target_pairs={{0,8},{1,9},{2,10},{3,11},{4,12},{5,13},{6,14},{7,15},{8,0},{9,1},... | collective-permute-start | bytes 104456 | tf_op jit(solution)/shard_map/ppermute | solution.py:315
  6.5 1.2 %shard_map.65 = (bf16[512,256]{1,0:T(8,128)(2,1)S(1)}, bf16[256,256]{1,0:T(8,128)(2,1)S(1)}, bf16[512,256]{1,0:T(8,128)(2,1)S(1)}) custom-call(bf16[512,256]{1,0:T(8,128)(2,1)} %constant.6.clone.forward, bf16[256,256]{1,0:T(8,128)(2,1)} %constant.7.clone.band_from, bf16[512,256]{1,0:T(8,128)(2,1)} %constant.8.clone.inverse_from), custom_call_target="tpu_custom_call" | custom-call | tf_op jit(solution)/shard_map/pallas_call | solution.py:324
  7.7 0.0 collective-permute-done.2
  7.7 3.0 %collective-permute-done.1 = bf16[1,136,128]{2,1,0:T(8,128)(2,1)S(1)} collective-permute-done((bf16[1,136,128]{2,1,0:T(8,128)(2,1)S(1)}, bf16[1,136,128]{2,1,0:T(8,128)(2,1)S(1)}, u32[]{:S(2)}, u32[]{:S(2)}) %collective-permute-start.1) | collective-permute-done | bytes 34848 | tf_op jit(solution)/shard_map/ppermute | solution.py:315
  10.6 0.0 collective-permute-done
  10.7 1.6 %collective-permute-start.5 = (bf16[4,136,128]{2,1,0:T(8,128)(2,1)S(1)}, bf16[4,136,128]{2,1,0:T(8,128)(2,1)S(1)}, u32[]{:S(2)}, u32[]{:S(2)}) collective-permute-start(bf16[4,136,128]{2,1,0:T(8,128)(2,1)S(1)} %constant_dynamic-update-slice_fusion.own), channel_id=1, source_target_pairs={{0,4},{1,5},{2,6},{3,7},{4,0},{5,1},{6,2},{7,3},{8,12},{9,13},{10,... | collective-permute-start | bytes 417800 | tf_op jit(solution)/shard_map/ppermute | solution.py:315
  12.4 1.5 %collective-permute-start.4 = (bf16[4,128,128]{2,1,0:T(8,128)(2,1)S(1)}, bf16[4,128,128]{2,1,0:T(8,128)(2,1)S(1)}, u32[]{:S(2)}, u32[]{:S(2)}) collective-permute-start(bf16[4,128,128]{2,1,0:T(8,128)(2,1)S(1)} %pad_maximum_fusion.1), channel_id=1, source_target_pairs={{0,6},{1,7},{2,4},{3,5},{4,2},{5,3},{6,0},{7,1},{8,14},{9,15},{10,... | collective-permute-start | bytes 393224 | tf_op jit(solution)/shard_map/ppermute | solution.py:315
  13.9 0.5 %collective-permute-start.3 = (bf16[4,128,128]{2,1,0:T(8,128)(2,1)S(1)}, bf16[4,128,128]{2,1,0:T(8,128)(2,1)S(1)}, u32[]{:S(2)}, u32[]{:S(2)}) collective-permute-start(bf16[4,128,128]{2,1,0:T(8,128)(2,1)S(1)} %pad_maximum_fusion.1), channel_id=1, source_target_pairs={{0,2},{1,3},{2,0},{3,1},{4,6},{5,7},{6,4},{7,5},{8,10},{9,11},{10,... | collective-permute-start | bytes 393224 | tf_op jit(solution)/shard_map/ppermute | solution.py:315
  14.4 2.6 %collective-permute-done.5.near = bf16[4,136,128]{2,1,0:T(8,128)(2,1)S(1)} collective-permute-done((bf16[4,136,128]{2,1,0:T(8,128)(2,1)S(1)}, bf16[4,136,128]{2,1,0:T(8,128)(2,1)S(1)}, u32[]{:S(2)}, u32[]{:S(2)}) %collective-permute-start.5) | collective-permute-done | bytes 139296 | tf_op jit(solution)/shard_map/ppermute | solution.py:315
  17.0 0.1 collective-permute-start.7
  17.1 1.0 %shard_map.66 = (f32[8,256,128]{2,1,0:T(8,128)S(1)}, bf16[128,128]{1,0:T(8,128)(2,1)S(1)}, bf16[64,128]{1,0:T(8,128)(2,1)S(1)}) custom-call(bf16[4,136,128]{2,1,0:T(8,128)(2,1)S(1)} %constant_dynamic-update-slice_fusion.own, bf16[4,136,128]{2,1,0:T(8,128)(2,1)S(1)} %collective-permute-done.5.near, bf16[512,256]{1,0:T(8,128)(2,1)S(1)} %get-tuple-element.32.fwd, ...), custom_call_target="tpu_custom_call" | custom-call | tf_op jit(solution)/shard_map/pallas_call | solution.py:353
  18.1 0.3 %collective-permute-done.4.diag = bf16[4,128,128]{2,1,0:T(8,128)(2,1)S(1)} collective-permute-done((bf16[4,128,128]{2,1,0:T(8,128)(2,1)S(1)}, bf16[4,128,128]{2,1,0:T(8,128)(2,1)S(1)}, u32[]{:S(2)}, u32[]{:S(2)}) %collective-permute-start.4) | collective-permute-done | bytes 131104 | tf_op jit(solution)/shard_map/ppermute | solution.py:315
  18.3 0.5 %collective-permute-done.3.other = bf16[4,128,128]{2,1,0:T(8,128)(2,1)S(1)} collective-permute-done((bf16[4,128,128]{2,1,0:T(8,128)(2,1)S(1)}, bf16[4,128,128]{2,1,0:T(8,128)(2,1)S(1)}, u32[]{:S(2)}, u32[]{:S(2)}) %collective-permute-start.3) | collective-permute-done | bytes 131104 | tf_op jit(solution)/shard_map/ppermute | solution.py:315
  18.9 0.1 collective-permute-start.6
  18.9 0.0 collective-permute-done.7.sib
  18.9 1.3 %shard_map.67.before = f32[8,256,128]{2,1,0:T(8,128)S(1)} custom-call(bf16[8,128,128]{2,1,0:T(8,128)(2,1)S(1)} %collective-permute-done.7.sib, bf16[4,128,128]{2,1,0:T(8,128)(2,1)S(1)} %collective-permute-done.3.other, bf16[4,128,128]{2,1,0:T(8,128)(2,1)S(1)} %collective-permute-done.4.diag, bf16[512,256]{1,0:T(8,128)(2,1)S(1)} %get-tuple-element.32.fwd, ...), custom_call_target="tpu_custom_call" | custom-call | tf_op jit(solution)/shard_map/pallas_call | solution.py:368
  20.3 0.2 collective-permute-done.6.sib
  20.5 2.3 %shard_map.68 = bf16[4,3,128,256]{3,2,1,0:T(8,128)(2,1)} custom-call(f32[8,256]{1,0:T(8,128)S(1)} %get-tuple-element.23.keep, bf16[8,128,128]{2,1,0:T(8,128)(2,1)S(1)} %collective-permute-done.6.sib, f32[8,256,128]{2,1,0:T(8,128)S(1)} %shard_map.67.before, bf16[512,256]{1,0:T(8,128)(2,1)S(1)} %get-tuple-element.32.fwd, ...), custom_call_target="tpu_custom_call" | custom-call | tf_op jit(solution)/shard_map/pallas_call | solution.py:376
  (11 shorter events, 0.1 us)
Async XLA Ops:
  0.8 6.9 %collective-permute-start.2 = (bf16[1,136,128]{2,1,0:T(8,128)(2,1)S(1)}, bf16[1,136,128]{2,1,0:T(8,128)(2,1)S(1)}, u32[]{:S(2)}, u32[]{:S(2)}) collective-permute-start(bf16[1,136,128]{2,1,0:T(8,128)(2,1)S(1)} %get-tuple-element.28), channel_id=1, source_target_pairs={{0,16},{1,17},{2,18},{3,19},{4,20},{5,21},{6,22},{7,23},{8,24},{9,... | collective-permute-start | bytes 104456 | tf_op jit(solution)/shard_map/ppermute | solution.py:315
  4.9 5.7 %collective-permute-start.1 = (bf16[1,136,128]{2,1,0:T(8,128)(2,1)S(1)}, bf16[1,136,128]{2,1,0:T(8,128)(2,1)S(1)}, u32[]{:S(2)}, u32[]{:S(2)}) collective-permute-start(bf16[1,136,128]{2,1,0:T(8,128)(2,1)S(1)} %get-tuple-element.28), channel_id=1, source_target_pairs={{0,24},{1,25},{2,26},{3,27},{4,28},{5,29},{6,30},{7,31},{8,16},{9,... | collective-permute-start | bytes 104456 | tf_op jit(solution)/shard_map/ppermute | solution.py:315
  6.2 4.4 %collective-permute-start = (bf16[1,136,128]{2,1,0:T(8,128)(2,1)S(1)}, bf16[1,136,128]{2,1,0:T(8,128)(2,1)S(1)}, u32[]{:S(2)}, u32[]{:S(2)}) collective-permute-start(bf16[1,136,128]{2,1,0:T(8,128)(2,1)S(1)} %get-tuple-element.28), channel_id=1, source_target_pairs={{0,8},{1,9},{2,10},{3,11},{4,12},{5,13},{6,14},{7,15},{8,0},{9,1},... | collective-permute-start | bytes 104456 | tf_op jit(solution)/shard_map/ppermute | solution.py:315
  10.7 6.3 %collective-permute-start.5 = (bf16[4,136,128]{2,1,0:T(8,128)(2,1)S(1)}, bf16[4,136,128]{2,1,0:T(8,128)(2,1)S(1)}, u32[]{:S(2)}, u32[]{:S(2)}) collective-permute-start(bf16[4,136,128]{2,1,0:T(8,128)(2,1)S(1)} %constant_dynamic-update-slice_fusion.own), channel_id=1, source_target_pairs={{0,4},{1,5},{2,6},{3,7},{4,0},{5,1},{6,2},{7,3},{8,12},{9,13},{10,... | collective-permute-start | bytes 417800 | tf_op jit(solution)/shard_map/ppermute | solution.py:315
  12.4 6.0 %collective-permute-start.4 = (bf16[4,128,128]{2,1,0:T(8,128)(2,1)S(1)}, bf16[4,128,128]{2,1,0:T(8,128)(2,1)S(1)}, u32[]{:S(2)}, u32[]{:S(2)}) collective-permute-start(bf16[4,128,128]{2,1,0:T(8,128)(2,1)S(1)} %pad_maximum_fusion.1), channel_id=1, source_target_pairs={{0,6},{1,7},{2,4},{3,5},{4,2},{5,3},{6,0},{7,1},{8,14},{9,15},{10,... | collective-permute-start | bytes 393224 | tf_op jit(solution)/shard_map/ppermute | solution.py:315
  13.9 5.0 %collective-permute-start.3 = (bf16[4,128,128]{2,1,0:T(8,128)(2,1)S(1)}, bf16[4,128,128]{2,1,0:T(8,128)(2,1)S(1)}, u32[]{:S(2)}, u32[]{:S(2)}) collective-permute-start(bf16[4,128,128]{2,1,0:T(8,128)(2,1)S(1)} %pad_maximum_fusion.1), channel_id=1, source_target_pairs={{0,2},{1,3},{2,0},{3,1},{4,6},{5,7},{6,4},{7,5},{8,10},{9,11},{10,... | collective-permute-start | bytes 393224 | tf_op jit(solution)/shard_map/ppermute | solution.py:315
  17.0 2.0 %collective-permute-start.7 = (bf16[8,128,128]{2,1,0:T(8,128)(2,1)S(1)}, bf16[8,128,128]{2,1,0:T(8,128)(2,1)S(1)}, u32[]{:S(2)}, u32[]{:S(2)}) collective-permute-start(bf16[8,128,128]{2,1,0:T(8,128)(2,1)S(1)} %slice_dynamic-update-slice_fusion), channel_id=1, source_target_pairs={{0,1},{1,0},{2,3},{3,2},{4,5},{5,4},{6,7},{7,6},{8,9},{9,8},{10,11... | collective-permute-start | bytes 786440 | tf_op jit(solution)/shard_map/ppermute | solution.py:315
  18.9 1.6 %collective-permute-start.6 = (bf16[8,128,128]{2,1,0:T(8,128)(2,1)S(1)}, bf16[8,128,128]{2,1,0:T(8,128)(2,1)S(1)}, u32[]{:S(2)}, u32[]{:S(2)}) collective-permute-start(bf16[8,128,128]{2,1,0:T(8,128)(2,1)S(1)} %pad_maximum_fusion), channel_id=1, source_target_pairs={{0,1},{1,0},{2,3},{3,2},{4,5},{5,4},{6,7},{7,6},{8,9},{9,8},{10,11... | collective-permute-start | bytes 786440 | tf_op jit(solution)/shard_map/ppermute | solution.py:315

commit v5 on v4

--- a/solution.py
+++ b/solution.py
@@ -120,20 +120,21 @@
 RECV = 4
 WIDTH = 2 * SMOOTH + 1
 DEEP = 128
+LABEL = 16
 
 
 def label_kernel(order, pairs, raw, out, keep):
     held = order.shape[1]
     half, channels = raw.shape[1:]
     me = lax.axis_index("ch")
-    lanes = lax.broadcasted_iota(jnp.int32, (8, channels), 1)
-    row = jnp.zeros((8, channels), jnp.int32)
+    lanes = lax.broadcasted_iota(jnp.int32, (LABEL, channels), 1)
+    row = jnp.zeros((LABEL, channels), jnp.int32)
     for c in range(held):
         row = jnp.where(lanes % held == c, order[0, c], row)
     row = jnp.where(lanes // held == me, row + held * me, 0)
     keep[...] = jnp.broadcast_to(jnp.where(pairs[0, 0] >= 0, 1.0, 0.0), keep.shape)
     out[0, 0:half, :] = raw[0]
-    out[0, half : half + 8, :] = row.astype(jnp.float32).astype(out.dtype)
+    out[0, half : half + LABEL, :] = row.astype(jnp.float32).astype(out.dtype)
 
 
 def tables_kernel(forward, band_from, inverse_from, fwd, band, inverse, sems):
@@ -221,26 +222,22 @@
 
 
 def window_kernel(
-    own, near, fwd, band, partial, perm, chosen, white, pick, spec, pows
+    own, near, label, near_label, fwd, band, partial, perm, chosen, white, pick, spec, pows
 ):
     half = fwd.shape[1] // 2
     zb = own.shape[0]
     ch = lax.axis_index("ch")
     base = (ch * lax.axis_size("grp") + lax.axis_index("grp")) * RECV
 
-    dest = own[0, half : half + 8, :]
-    for z in range(1, zb):
-        dest = jnp.maximum(dest, own[z, half : half + 8, :])
-    for z in range(zb):
-        dest = jnp.maximum(dest, near[z, half : half + 8, :])
+    dest = jnp.maximum(label[...], near_label[...])
     dest = dest.astype(jnp.float32)[0:1, :]
     rows = lax.broadcasted_iota(jnp.int32, (SRC, SRC), 0)
     perm[...] = (rows.astype(jnp.float32) == dest).astype(jnp.bfloat16)
     wanted = lax.broadcasted_iota(jnp.int32, chosen.shape, 0) * RECV // chosen.shape[0] + base
-    chosen[...] = (wanted.astype(jnp.float32) == dest).astype(jnp.bfloat16)
+    chosen[...] = (wanted.astype(jnp.float32) == dest).astype(jnp.float32)
 
     whiten_group(pair_items(own, near, half), fwd, band, spec, pows, white)
-    for at, value in enumerate(receiver_products(white, chosen[...], pick)):
+    for at, value in enumerate(receiver_products(white, chosen[...].astype(jnp.bfloat16), pick)):
         partial[at] = value
 
 
@@ -253,7 +250,7 @@
     select = jnp.concatenate(
         [chosen[q * step : q * step + each // RECV, :] for q in range(RECV)], axis=0
     )
-    for at, value in enumerate(receiver_products(white, select, pick)):
+    for at, value in enumerate(receiver_products(white, select.astype(jnp.bfloat16), pick)):
         partial[at] = before[at] + value
 
 
@@ -274,7 +271,7 @@
     whiten_group(
         pair_items(sib.at[0:zb], sib.at[zb : 2 * zb], half), fwd, band, spec, pows, white
     )
-    for at, value in enumerate(receiver_products(white, chosen[...], pick)):
+    for at, value in enumerate(receiver_products(white, chosen[...].astype(jnp.bfloat16), pick)):
         total = (before[at] + value) * (WIDTH / (4 * zb))
         part, q = at // RECV, at % RECV
         lanes = slice((q % 2) * SRC, (q % 2 + 1) * SRC)
@@ -305,7 +302,7 @@
 
     block, keep = pl.pallas_call(
         label_kernel,
-        out_shape=[pltpu.VMEM((1, half + 8, channels), dtype), pltpu.VMEM((8, 2 * SRC), jnp.float32)],
+        out_shape=[pltpu.VMEM((1, half + LABEL, channels), dtype), pltpu.VMEM((8, 2 * SRC), jnp.float32)],
         in_specs=[smem, smem, vmem],
         out_specs=[vmem, vmem],
     )(order, pair_blocks, raw)
@@ -329,12 +326,14 @@
         scratch_shapes=[pltpu.SemaphoreType.DMA((4,))],
     )(forward, band, inverse)
     parts, fwd, band, inverse = lax.optimization_barrier((parts, fwd, band, inverse))
-    own = jnp.concatenate(parts, axis=0)
-    bare = jnp.concatenate([p[:, 0:half] for p in parts], axis=0)
-    near = swap(own, 1, 0)
-    diag = swap(bare, 1, 2)
-    other = swap(bare, 0, 2)
-    first_sib = swap(jnp.concatenate([bare, near[:, 0:half]], axis=0), 0, 1)
+    own = jnp.concatenate([p[0, 0:half] for p in parts], axis=0)
+    label = functools.reduce(jnp.maximum, [p[0, half:] for p in parts])
+    near = swap(jnp.concatenate([own, label], axis=0), 1, 0)
+    diag = swap(own, 1, 2).reshape(-1, half, channels)
+    other = swap(own, 0, 2).reshape(-1, half, channels)
+    near, near_label = near[: own.shape[0]].reshape(-1, half, channels), near[own.shape[0] :]
+    own = own.reshape(-1, half, channels)
+    first_sib = swap(jnp.concatenate([own, near], axis=0), 0, 1)
 
     zb = own.shape[0]
 
@@ -355,13 +354,13 @@
         out_shape=[
             partial,
             pltpu.VMEM((SRC, SRC), jnp.bfloat16),
-            pltpu.VMEM((RECV * DEEP // (2 * zb), SRC), jnp.bfloat16),
+            pltpu.VMEM((RECV * DEEP // (2 * zb), SRC), jnp.float32),
         ],
-        in_specs=[vmem] * 4,
+        in_specs=[vmem] * 6,
         out_specs=[vmem] * 3,
         scratch_shapes=[*spectra, *work],
         compiler_params=params,
-    )(own, near, fwd, band)
+    )(own, near, label, near_label, fwd, band)
     other, diag, chosen = lax.optimization_barrier((other, diag, chosen))
     second_sib = swap(jnp.concatenate([other, diag], axis=0), 0, 1)
     many_spectra, many_work = scratch(2 * zb)

time: 23 us -> 22.9 us (level)
  no operation moved by 1% of the time
where the time goes in v5:
time: 22.9 us; the launch traced here: 22.7 us
  starting transfers between devices  9.44 us (41%)
  Pallas kernels  6.57 us (29%)
  waiting for transfers between devices  6.46 us (28%)
    ppermute x8, starting transfers between devices, swap(): lax.ppermute(value, ('ch', 'grp'), [(d, d ^ flip) for d in range(total)])  9.44 us
    ppermute x8, waiting for transfers between devices, swap(): lax.ppermute(value, ('ch', 'grp'), [(d, d ^ flip) for d in range(total)])  6.46 us
    pallas_call x1, Pallas kernels, one_block(): pl.pallas_call(cross_kernel, out_shape=jax.ShapeDtypeStruct((RECV, MAXP,...  2.28 us
    pallas_call x1, Pallas kernels, one_block(): pl.pallas_call(middle_kernel, out_shape=partial, in_specs=[vmem] * 7, out...  1.31 us
    pallas_call x1, Pallas kernels, one_block(): pl.pallas_call(tables_kernel, out_shape=[pltpu.VMEM(t.shape, t.dtype) for...  1.18 us
    pallas_call x1, Pallas kernels, one_block(): pl.pallas_call(window_kernel, out_shape=[partial, pltpu.VMEM((SRC, SRC),...  1.01 us
    pallas_call x1, Pallas kernels, one_block(): pl.pallas_call(label_kernel, out_shape=[pltpu.VMEM((1, half + LABEL, chan...  0.78 us
  transfers between devices with their start and end apart: 8, of which 5 were waited for; matrix products, arithmetic and copies ran while one was open for 0% of the time, Pallas kernels for 15%

profile of v5, /device:TPU:0, one launch (start us, length us, event | category | flops | bytes accessed | tf_op | source)
XLA Modules:
  0.0 22.7 jit_solution(12015746208296668855)
XLA Ops:
  0.0 0.8 %shard_map.64 = (bf16[1,144,128]{2,1,0:T(8,128)(2,1)S(1)}, f32[8,256]{1,0:T(8,128)S(1)}) custom-call(s32[1,16]{1,0:T(1,128)} %order.1, s32[1,3]{1,0:T(1,128)} %pairs.1, bf16[1,128,128]{2,1,0:T(8,128)(2,1)} %raw.1), custom_call_target="tpu_custom_call" | custom-call | tf_op jit(solution)/shard_map/pallas_call | solution.py:303
  0.8 4.1 %collective-permute-start.2 = (bf16[1,144,128]{2,1,0:T(8,128)(2,1)S(1)}, bf16[1,144,128]{2,1,0:T(8,128)(2,1)S(1)}, u32[]{:S(2)}, u32[]{:S(2)}) collective-permute-start(bf16[1,144,128]{2,1,0:T(8,128)(2,1)S(1)} %get-tuple-element.28), channel_id=1, source_target_pairs={{0,16},{1,17},{2,18},{3,19},{4,20},{5,21},{6,22},{7,23},{8,24},{9,... | collective-permute-start | bytes 110600 | tf_op jit(solution)/shard_map/ppermute | solution.py:312
  4.9 1.3 %collective-permute-start.1 = (bf16[1,144,128]{2,1,0:T(8,128)(2,1)S(1)}, bf16[1,144,128]{2,1,0:T(8,128)(2,1)S(1)}, u32[]{:S(2)}, u32[]{:S(2)}) collective-permute-start(bf16[1,144,128]{2,1,0:T(8,128)(2,1)S(1)} %get-tuple-element.28), channel_id=1, source_target_pairs={{0,24},{1,25},{2,26},{3,27},{4,28},{5,29},{6,30},{7,31},{8,16},{9,... | collective-permute-start | bytes 110600 | tf_op jit(solution)/shard_map/ppermute | solution.py:312
  6.2 0.2 %collective-permute-start = (bf16[1,144,128]{2,1,0:T(8,128)(2,1)S(1)}, bf16[1,144,128]{2,1,0:T(8,128)(2,1)S(1)}, u32[]{:S(2)}, u32[]{:S(2)}) collective-permute-start(bf16[1,144,128]{2,1,0:T(8,128)(2,1)S(1)} %get-tuple-element.28), channel_id=1, source_target_pairs={{0,8},{1,9},{2,10},{3,11},{4,12},{5,13},{6,14},{7,15},{8,0},{9,1},... | collective-permute-start | bytes 110600 | tf_op jit(solution)/shard_map/ppermute | solution.py:312
  6.5 1.2 %shard_map.65 = (bf16[512,256]{1,0:T(8,128)(2,1)S(1)}, bf16[256,256]{1,0:T(8,128)(2,1)S(1)}, bf16[512,256]{1,0:T(8,128)(2,1)S(1)}) custom-call(bf16[512,256]{1,0:T(8,128)(2,1)} %constant.6.clone.forward, bf16[256,256]{1,0:T(8,128)(2,1)} %constant.7.clone.band_from, bf16[512,256]{1,0:T(8,128)(2,1)} %constant.8.clone.inverse_from), custom_call_target="tpu_custom_call" | custom-call | tf_op jit(solution)/shard_map/pallas_call | solution.py:321
  7.7 0.0 collective-permute-done.2
  7.7 3.0 %collective-permute-done.1 = bf16[1,144,128]{2,1,0:T(8,128)(2,1)S(1)} collective-permute-done((bf16[1,144,128]{2,1,0:T(8,128)(2,1)S(1)}, bf16[1,144,128]{2,1,0:T(8,128)(2,1)S(1)}, u32[]{:S(2)}, u32[]{:S(2)}) %collective-permute-start.1) | collective-permute-done | bytes 36896 | tf_op jit(solution)/shard_map/ppermute | solution.py:312
  10.7 0.0 collective-permute-done
  10.7 1.6 %collective-permute-start.5 = (bf16[528,128]{1,0:T(8,128)(2,1)S(1)}, bf16[528,128]{1,0:T(8,128)(2,1)S(1)}, u32[]{:S(2)}, u32[]{:S(2)}) collective-permute-start(bf16[528,128]{1,0:T(8,128)(2,1)S(1)} %get-tuple-element.41), channel_id=1, source_target_pairs={{0,4},{1,5},{2,6},{3,7},{4,0},{5,1},{6,2},{7,3},{8,12},{9,13},{10,... | collective-permute-start | bytes 405512 | tf_op jit(solution)/shard_map/ppermute | solution.py:312
  12.3 1.5 %collective-permute-start.4 = (bf16[512,128]{1,0:T(8,128)(2,1)S(1)}, bf16[512,128]{1,0:T(8,128)(2,1)S(1)}, u32[]{:S(2)}, u32[]{:S(2)}) collective-permute-start(bf16[512,128]{1,0:T(8,128)(2,1)S(1)} %pad_maximum_fusion.2), channel_id=1, source_target_pairs={{0,6},{1,7},{2,4},{3,5},{4,2},{5,3},{6,0},{7,1},{8,14},{9,15},{10,... | collective-permute-start | bytes 393224 | tf_op jit(solution)/shard_map/ppermute | solution.py:312
  13.8 0.5 %collective-permute-start.3 = (bf16[512,128]{1,0:T(8,128)(2,1)S(1)}, bf16[512,128]{1,0:T(8,128)(2,1)S(1)}, u32[]{:S(2)}, u32[]{:S(2)}) collective-permute-start(bf16[512,128]{1,0:T(8,128)(2,1)S(1)} %pad_maximum_fusion.2), channel_id=1, source_target_pairs={{0,2},{1,3},{2,0},{3,1},{4,6},{5,7},{6,4},{7,5},{8,10},{9,11},{10,... | collective-permute-start | bytes 393224 | tf_op jit(solution)/shard_map/ppermute | solution.py:312
  14.4 2.5 %collective-permute-done.5 = bf16[528,128]{1,0:T(8,128)(2,1)S(1)} collective-permute-done((bf16[528,128]{1,0:T(8,128)(2,1)S(1)}, bf16[528,128]{1,0:T(8,128)(2,1)S(1)}, u32[]{:S(2)}, u32[]{:S(2)}) %collective-permute-start.5) | collective-permute-done | bytes 135200 | tf_op jit(solution)/shard_map/ppermute | solution.py:312
  16.9 0.1 collective-permute-start.7
  17.0 1.0 %shard_map.66 = (f32[8,256,128]{2,1,0:T(8,128)S(1)}, bf16[128,128]{1,0:T(8,128)(2,1)S(1)}, f32[64,128]{1,0:T(8,128)S(1)}) custom-call(bf16[4,128,128]{2,1,0:T(8,128)(2,1)S(1)} %bitcast.24, bf16[4,128,128]{2,1,0:T(8,128)(2,1)S(1)} %bitcast.26, bf16[16,128]{1,0:T(8,128)(2,1)S(1)} %get-tuple-element.42.label, bf16[16,128]{1,0:T(8,128)(2,1)S(1)} %slice.41.near_label, ...), custom_call_target="tpu_custom_call" | custom-call | tf_op jit(solution)/shard_map/pallas_call | solution.py:352
  18.0 0.2 %collective-permute-done.4 = bf16[512,128]{1,0:T(8,128)(2,1)S(1)} collective-permute-done((bf16[512,128]{1,0:T(8,128)(2,1)S(1)}, bf16[512,128]{1,0:T(8,128)(2,1)S(1)}, u32[]{:S(2)}, u32[]{:S(2)}) %collective-permute-start.4) | collective-permute-done | bytes 131104 | tf_op jit(solution)/shard_map/ppermute | solution.py:312
  18.3 0.5 %collective-permute-done.3 = bf16[512,128]{1,0:T(8,128)(2,1)S(1)} collective-permute-done((bf16[512,128]{1,0:T(8,128)(2,1)S(1)}, bf16[512,128]{1,0:T(8,128)(2,1)S(1)}, u32[]{:S(2)}, u32[]{:S(2)}) %collective-permute-start.3) | collective-permute-done | bytes 131104 | tf_op jit(solution)/shard_map/ppermute | solution.py:312
  18.8 0.1 collective-permute-start.6
  18.9 0.0 collective-permute-done.7.sib
  18.9 1.3 %shard_map.67.before = f32[8,256,128]{2,1,0:T(8,128)S(1)} custom-call(bf16[8,128,128]{2,1,0:T(8,128)(2,1)S(1)} %collective-permute-done.7.sib, bf16[4,128,128]{2,1,0:T(8,128)(2,1)S(1)} %bitcast.30, bf16[4,128,128]{2,1,0:T(8,128)(2,1)S(1)} %bitcast.28, bf16[512,256]{1,0:T(8,128)(2,1)S(1)} %get-tuple-element.32.fwd, ...), custom_call_target="tpu_custom_call" | custom-call | tf_op jit(solution)/shard_map/pallas_call | solution.py:367
  20.2 0.2 collective-permute-done.6.sib
  20.4 2.3 %shard_map.68 = bf16[4,3,128,256]{3,2,1,0:T(8,128)(2,1)} custom-call(f32[8,256]{1,0:T(8,128)S(1)} %get-tuple-element.23.keep, bf16[8,128,128]{2,1,0:T(8,128)(2,1)S(1)} %collective-permute-done.6.sib, f32[8,256,128]{2,1,0:T(8,128)S(1)} %shard_map.67.before, bf16[512,256]{1,0:T(8,128)(2,1)S(1)} %get-tuple-element.32.fwd, ...), custom_call_target="tpu_custom_call" | custom-call | tf_op jit(solution)/shard_map/pallas_call | solution.py:375
  (12 shorter events, 0.1 us)
Async XLA Ops:
  0.8 6.9 %collective-permute-start.2 = (bf16[1,144,128]{2,1,0:T(8,128)(2,1)S(1)}, bf16[1,144,128]{2,1,0:T(8,128)(2,1)S(1)}, u32[]{:S(2)}, u32[]{:S(2)}) collective-permute-start(bf16[1,144,128]{2,1,0:T(8,128)(2,1)S(1)} %get-tuple-element.28), channel_id=1, source_target_pairs={{0,16},{1,17},{2,18},{3,19},{4,20},{5,21},{6,22},{7,23},{8,24},{9,... | collective-permute-start | bytes 110600 | tf_op jit(solution)/shard_map/ppermute | solution.py:312
  4.9 5.8 %collective-permute-start.1 = (bf16[1,144,128]{2,1,0:T(8,128)(2,1)S(1)}, bf16[1,144,128]{2,1,0:T(8,128)(2,1)S(1)}, u32[]{:S(2)}, u32[]{:S(2)}) collective-permute-start(bf16[1,144,128]{2,1,0:T(8,128)(2,1)S(1)} %get-tuple-element.28), channel_id=1, source_target_pairs={{0,24},{1,25},{2,26},{3,27},{4,28},{5,29},{6,30},{7,31},{8,16},{9,... | collective-permute-start | bytes 110600 | tf_op jit(solution)/shard_map/ppermute | solution.py:312
  6.2 4.4 %collective-permute-start = (bf16[1,144,128]{2,1,0:T(8,128)(2,1)S(1)}, bf16[1,144,128]{2,1,0:T(8,128)(2,1)S(1)}, u32[]{:S(2)}, u32[]{:S(2)}) collective-permute-start(bf16[1,144,128]{2,1,0:T(8,128)(2,1)S(1)} %get-tuple-element.28), channel_id=1, source_target_pairs={{0,8},{1,9},{2,10},{3,11},{4,12},{5,13},{6,14},{7,15},{8,0},{9,1},... | collective-permute-start | bytes 110600 | tf_op jit(solution)/shard_map/ppermute | solution.py:312
  10.7 6.2 %collective-permute-start.5 = (bf16[528,128]{1,0:T(8,128)(2,1)S(1)}, bf16[528,128]{1,0:T(8,128)(2,1)S(1)}, u32[]{:S(2)}, u32[]{:S(2)}) collective-permute-start(bf16[528,128]{1,0:T(8,128)(2,1)S(1)} %get-tuple-element.41), channel_id=1, source_target_pairs={{0,4},{1,5},{2,6},{3,7},{4,0},{5,1},{6,2},{7,3},{8,12},{9,13},{10,... | collective-permute-start | bytes 405512 | tf_op jit(solution)/shard_map/ppermute | solution.py:312
  12.3 5.9 %collective-permute-start.4 = (bf16[512,128]{1,0:T(8,128)(2,1)S(1)}, bf16[512,128]{1,0:T(8,128)(2,1)S(1)}, u32[]{:S(2)}, u32[]{:S(2)}) collective-permute-start(bf16[512,128]{1,0:T(8,128)(2,1)S(1)} %pad_maximum_fusion.2), channel_id=1, source_target_pairs={{0,6},{1,7},{2,4},{3,5},{4,2},{5,3},{6,0},{7,1},{8,14},{9,15},{10,... | collective-permute-start | bytes 393224 | tf_op jit(solution)/shard_map/ppermute | solution.py:312
  13.8 5.0 %collective-permute-start.3 = (bf16[512,128]{1,0:T(8,128)(2,1)S(1)}, bf16[512,128]{1,0:T(8,128)(2,1)S(1)}, u32[]{:S(2)}, u32[]{:S(2)}) collective-permute-start(bf16[512,128]{1,0:T(8,128)(2,1)S(1)} %pad_maximum_fusion.2), channel_id=1, source_target_pairs={{0,2},{1,3},{2,0},{3,1},{4,6},{5,7},{6,4},{7,5},{8,10},{9,11},{10,... | collective-permute-start | bytes 393224 | tf_op jit(solution)/shard_map/ppermute | solution.py:312
  16.9 2.0 %collective-permute-start.7 = (bf16[8,128,128]{2,1,0:T(8,128)(2,1)S(1)}, bf16[8,128,128]{2,1,0:T(8,128)(2,1)S(1)}, u32[]{:S(2)}, u32[]{:S(2)}) collective-permute-start(bf16[8,128,128]{2,1,0:T(8,128)(2,1)S(1)} %pad_maximum_fusion.1), channel_id=1, source_target_pairs={{0,1},{1,0},{2,3},{3,2},{4,5},{5,4},{6,7},{7,6},{8,9},{9,8},{10,11... | collective-permute-start | bytes 786440 | tf_op jit(solution)/shard_map/ppermute | solution.py:312
  18.8 1.6 %collective-permute-start.6 = (bf16[8,128,128]{2,1,0:T(8,128)(2,1)S(1)}, bf16[8,128,128]{2,1,0:T(8,128)(2,1)S(1)}, u32[]{:S(2)}, u32[]{:S(2)}) collective-permute-start(bf16[8,128,128]{2,1,0:T(8,128)(2,1)S(1)} %pad_maximum_fusion), channel_id=1, source_target_pairs={{0,1},{1,0},{2,3},{3,2},{4,5},{5,4},{6,7},{7,6},{8,9},{9,8},{10,11... | collective-permute-start | bytes 786440 | tf_op jit(solution)/shard_map/ppermute | solution.py:312

commit v6 on v5

--- a/solution.py
+++ b/solution.py
@@ -274,15 +274,17 @@
     for at, value in enumerate(receiver_products(white, chosen[...].astype(jnp.bfloat16), pick)):
         total = (before[at] + value) * (WIDTH / (4 * zb))
         part, q = at // RECV, at % RECV
-        lanes = slice((q % 2) * SRC, (q % 2 + 1) * SRC)
-        cross[q // 2, part * bins : (part + 1) * bins, lanes] = total.astype(jnp.bfloat16)
-
+        cross[q, part * bins : (part + 1) * bins, :] = total.astype(jnp.bfloat16)
+
+    turned = lax.dot_general(
+        perm[...],
+        cross[...].reshape(RECV * 2 * bins, SRC),
+        (((1,), (1,)), ((), ())),
+        preferred_element_type=jnp.float32,
+    ).astype(jnp.bfloat16)
     for q in range(RECV):
-        held = cross[q // 2, :, (q % 2) * SRC : (q % 2 + 1) * SRC]
-        turned = lax.dot_general(
-            perm[...], held, (((1,), (1,)), ((), ())), preferred_element_type=jnp.float32
-        ).astype(jnp.bfloat16)
-        lag_values = jnp.dot(turned, inverse[...], preferred_element_type=jnp.float32)
+        held = turned[:, q * 2 * bins : (q + 1) * 2 * bins]
+        lag_values = jnp.dot(held, inverse[...], preferred_element_type=jnp.float32)
         lags[q] = (lag_values * keep[0:1, :]).astype(jnp.bfloat16)
         copy = pltpu.make_async_copy(lags.at[q], out.at[q, 0], sems.at[RECV + q])
         copy.start()
@@ -379,7 +381,7 @@
         out_specs=pl.BlockSpec(memory_space=pl.ANY),
         scratch_shapes=[
             *spectra,
-            pltpu.VMEM((RECV // 2, 2 * SEG, 2 * SRC), jnp.bfloat16),
+            pltpu.VMEM((RECV, 2 * SEG, SRC), jnp.bfloat16),
             pltpu.VMEM((RECV, SRC, LAGS), jnp.bfloat16),
             pltpu.VMEM((MAXP - 1, SRC, LAGS), jnp.bfloat16),
             *work,

time: 22.9 us -> 22.9 us (level)
  no operation moved by 1% of the time
where the time goes in v6:
time: 22.9 us; the launch traced here: 22.7 us
  starting transfers between devices  9.44 us (41%)
  Pallas kernels  6.53 us (29%)
  waiting for transfers between devices  6.46 us (28%)
    ppermute x8, starting transfers between devices, swap(): lax.ppermute(value, ('ch', 'grp'), [(d, d ^ flip) for d in range(total)])  9.44 us
    ppermute x8, waiting for transfers between devices, swap(): lax.ppermute(value, ('ch', 'grp'), [(d, d ^ flip) for d in range(total)])  6.46 us
    pallas_call x1, Pallas kernels, one_block(): pl.pallas_call(cross_kernel, out_shape=jax.ShapeDtypeStruct((RECV, MAXP,...  2.24 us
    pallas_call x1, Pallas kernels, one_block(): pl.pallas_call(middle_kernel, out_shape=partial, in_specs=[vmem] * 7, out...  1.31 us
    pallas_call x1, Pallas kernels, one_block(): pl.pallas_call(tables_kernel, out_shape=[pltpu.VMEM(t.shape, t.dtype) for...  1.18 us
    pallas_call x1, Pallas kernels, one_block(): pl.pallas_call(window_kernel, out_shape=[partial, pltpu.VMEM((SRC, SRC),...  1.01 us
    pallas_call x1, Pallas kernels, one_block(): pl.pallas_call(label_kernel, out_shape=[pltpu.VMEM((1, half + LABEL, chan...  0.78 us
  transfers between devices with their start and end apart: 8, of which 5 were waited for; matrix products, arithmetic and copies ran while one was open for 0% of the time, Pallas kernels for 15%

profile of v6, /device:TPU:0, one launch (start us, length us, event | category | flops | bytes accessed | tf_op | source)
XLA Modules:
  0.0 22.7 jit_solution(4953316392612237565)
XLA Ops:
  0.0 0.8 %shard_map.64 = (bf16[1,144,128]{2,1,0:T(8,128)(2,1)S(1)}, f32[8,256]{1,0:T(8,128)S(1)}) custom-call(s32[1,16]{1,0:T(1,128)} %order.1, s32[1,3]{1,0:T(1,128)} %pairs.1, bf16[1,128,128]{2,1,0:T(8,128)(2,1)} %raw.1), custom_call_target="tpu_custom_call" | custom-call | tf_op jit(solution)/shard_map/pallas_call | solution.py:305
  0.8 4.1 %collective-permute-start.2 = (bf16[1,144,128]{2,1,0:T(8,128)(2,1)S(1)}, bf16[1,144,128]{2,1,0:T(8,128)(2,1)S(1)}, u32[]{:S(2)}, u32[]{:S(2)}) collective-permute-start(bf16[1,144,128]{2,1,0:T(8,128)(2,1)S(1)} %get-tuple-element.28), channel_id=1, source_target_pairs={{0,16},{1,17},{2,18},{3,19},{4,20},{5,21},{6,22},{7,23},{8,24},{9,... | collective-permute-start | bytes 110600 | tf_op jit(solution)/shard_map/ppermute | solution.py:314
  4.9 1.3 %collective-permute-start.1 = (bf16[1,144,128]{2,1,0:T(8,128)(2,1)S(1)}, bf16[1,144,128]{2,1,0:T(8,128)(2,1)S(1)}, u32[]{:S(2)}, u32[]{:S(2)}) collective-permute-start(bf16[1,144,128]{2,1,0:T(8,128)(2,1)S(1)} %get-tuple-element.28), channel_id=1, source_target_pairs={{0,24},{1,25},{2,26},{3,27},{4,28},{5,29},{6,30},{7,31},{8,16},{9,... | collective-permute-start | bytes 110600 | tf_op jit(solution)/shard_map/ppermute | solution.py:314
  6.2 0.2 %collective-permute-start = (bf16[1,144,128]{2,1,0:T(8,128)(2,1)S(1)}, bf16[1,144,128]{2,1,0:T(8,128)(2,1)S(1)}, u32[]{:S(2)}, u32[]{:S(2)}) collective-permute-start(bf16[1,144,128]{2,1,0:T(8,128)(2,1)S(1)} %get-tuple-element.28), channel_id=1, source_target_pairs={{0,8},{1,9},{2,10},{3,11},{4,12},{5,13},{6,14},{7,15},{8,0},{9,1},... | collective-permute-start | bytes 110600 | tf_op jit(solution)/shard_map/ppermute | solution.py:314
  6.5 1.2 %shard_map.65 = (bf16[512,256]{1,0:T(8,128)(2,1)S(1)}, bf16[256,256]{1,0:T(8,128)(2,1)S(1)}, bf16[512,256]{1,0:T(8,128)(2,1)S(1)}) custom-call(bf16[512,256]{1,0:T(8,128)(2,1)} %constant.6.clone.forward, bf16[256,256]{1,0:T(8,128)(2,1)} %constant.7.clone.band_from, bf16[512,256]{1,0:T(8,128)(2,1)} %constant.8.clone.inverse_from), custom_call_target="tpu_custom_call" | custom-call | tf_op jit(solution)/shard_map/pallas_call | solution.py:323
  7.7 0.0 collective-permute-done.2
  7.7 3.0 %collective-permute-done.1 = bf16[1,144,128]{2,1,0:T(8,128)(2,1)S(1)} collective-permute-done((bf16[1,144,128]{2,1,0:T(8,128)(2,1)S(1)}, bf16[1,144,128]{2,1,0:T(8,128)(2,1)S(1)}, u32[]{:S(2)}, u32[]{:S(2)}) %collective-permute-start.1) | collective-permute-done | bytes 36896 | tf_op jit(solution)/shard_map/ppermute | solution.py:314
  10.7 0.0 collective-permute-done
  10.7 1.6 %collective-permute-start.5 = (bf16[528,128]{1,0:T(8,128)(2,1)S(1)}, bf16[528,128]{1,0:T(8,128)(2,1)S(1)}, u32[]{:S(2)}, u32[]{:S(2)}) collective-permute-start(bf16[528,128]{1,0:T(8,128)(2,1)S(1)} %get-tuple-element.41), channel_id=1, source_target_pairs={{0,4},{1,5},{2,6},{3,7},{4,0},{5,1},{6,2},{7,3},{8,12},{9,13},{10,... | collective-permute-start | bytes 405512 | tf_op jit(solution)/shard_map/ppermute | solution.py:314
  12.3 1.5 %collective-permute-start.4 = (bf16[512,128]{1,0:T(8,128)(2,1)S(1)}, bf16[512,128]{1,0:T(8,128)(2,1)S(1)}, u32[]{:S(2)}, u32[]{:S(2)}) collective-permute-start(bf16[512,128]{1,0:T(8,128)(2,1)S(1)} %pad_maximum_fusion.2), channel_id=1, source_target_pairs={{0,6},{1,7},{2,4},{3,5},{4,2},{5,3},{6,0},{7,1},{8,14},{9,15},{10,... | collective-permute-start | bytes 393224 | tf_op jit(solution)/shard_map/ppermute | solution.py:314
  13.8 0.5 %collective-permute-start.3 = (bf16[512,128]{1,0:T(8,128)(2,1)S(1)}, bf16[512,128]{1,0:T(8,128)(2,1)S(1)}, u32[]{:S(2)}, u32[]{:S(2)}) collective-permute-start(bf16[512,128]{1,0:T(8,128)(2,1)S(1)} %pad_maximum_fusion.2), channel_id=1, source_target_pairs={{0,2},{1,3},{2,0},{3,1},{4,6},{5,7},{6,4},{7,5},{8,10},{9,11},{10,... | collective-permute-start | bytes 393224 | tf_op jit(solution)/shard_map/ppermute | solution.py:314
  14.4 2.5 %collective-permute-done.5 = bf16[528,128]{1,0:T(8,128)(2,1)S(1)} collective-permute-done((bf16[528,128]{1,0:T(8,128)(2,1)S(1)}, bf16[528,128]{1,0:T(8,128)(2,1)S(1)}, u32[]{:S(2)}, u32[]{:S(2)}) %collective-permute-start.5) | collective-permute-done | bytes 135200 | tf_op jit(solution)/shard_map/ppermute | solution.py:314
  16.9 0.1 collective-permute-start.7
  17.0 1.0 %shard_map.66 = (f32[8,256,128]{2,1,0:T(8,128)S(1)}, bf16[128,128]{1,0:T(8,128)(2,1)S(1)}, f32[64,128]{1,0:T(8,128)S(1)}) custom-call(bf16[4,128,128]{2,1,0:T(8,128)(2,1)S(1)} %bitcast.24, bf16[4,128,128]{2,1,0:T(8,128)(2,1)S(1)} %bitcast.26, bf16[16,128]{1,0:T(8,128)(2,1)S(1)} %get-tuple-element.42.label, bf16[16,128]{1,0:T(8,128)(2,1)S(1)} %slice.41.near_label, ...), custom_call_target="tpu_custom_call" | custom-call | tf_op jit(solution)/shard_map/pallas_call | solution.py:354
  18.0 0.2 %collective-permute-done.4 = bf16[512,128]{1,0:T(8,128)(2,1)S(1)} collective-permute-done((bf16[512,128]{1,0:T(8,128)(2,1)S(1)}, bf16[512,128]{1,0:T(8,128)(2,1)S(1)}, u32[]{:S(2)}, u32[]{:S(2)}) %collective-permute-start.4) | collective-permute-done | bytes 131104 | tf_op jit(solution)/shard_map/ppermute | solution.py:314
  18.3 0.5 %collective-permute-done.3 = bf16[512,128]{1,0:T(8,128)(2,1)S(1)} collective-permute-done((bf16[512,128]{1,0:T(8,128)(2,1)S(1)}, bf16[512,128]{1,0:T(8,128)(2,1)S(1)}, u32[]{:S(2)}, u32[]{:S(2)}) %collective-permute-start.3) | collective-permute-done | bytes 131104 | tf_op jit(solution)/shard_map/ppermute | solution.py:314
  18.8 0.1 collective-permute-start.6
  18.9 0.0 collective-permute-done.7.sib
  18.9 1.3 %shard_map.67.before = f32[8,256,128]{2,1,0:T(8,128)S(1)} custom-call(bf16[8,128,128]{2,1,0:T(8,128)(2,1)S(1)} %collective-permute-done.7.sib, bf16[4,128,128]{2,1,0:T(8,128)(2,1)S(1)} %bitcast.30, bf16[4,128,128]{2,1,0:T(8,128)(2,1)S(1)} %bitcast.28, bf16[512,256]{1,0:T(8,128)(2,1)S(1)} %get-tuple-element.32.fwd, ...), custom_call_target="tpu_custom_call" | custom-call | tf_op jit(solution)/shard_map/pallas_call | solution.py:369
  20.2 0.2 collective-permute-done.6.sib
  20.4 2.2 %shard_map.68 = bf16[4,3,128,256]{3,2,1,0:T(8,128)(2,1)} custom-call(f32[8,256]{1,0:T(8,128)S(1)} %get-tuple-element.23.keep, bf16[8,128,128]{2,1,0:T(8,128)(2,1)S(1)} %collective-permute-done.6.sib, f32[8,256,128]{2,1,0:T(8,128)S(1)} %shard_map.67.before, bf16[512,256]{1,0:T(8,128)(2,1)S(1)} %get-tuple-element.32.fwd, ...), custom_call_target="tpu_custom_call" | custom-call | tf_op jit(solution)/shard_map/pallas_call | solution.py:377
  (12 shorter events, 0.1 us)
Async XLA Ops:
  0.8 6.9 %collective-permute-start.2 = (bf16[1,144,128]{2,1,0:T(8,128)(2,1)S(1)}, bf16[1,144,128]{2,1,0:T(8,128)(2,1)S(1)}, u32[]{:S(2)}, u32[]{:S(2)}) collective-permute-start(bf16[1,144,128]{2,1,0:T(8,128)(2,1)S(1)} %get-tuple-element.28), channel_id=1, source_target_pairs={{0,16},{1,17},{2,18},{3,19},{4,20},{5,21},{6,22},{7,23},{8,24},{9,... | collective-permute-start | bytes 110600 | tf_op jit(solution)/shard_map/ppermute | solution.py:314
  4.9 5.8 %collective-permute-start.1 = (bf16[1,144,128]{2,1,0:T(8,128)(2,1)S(1)}, bf16[1,144,128]{2,1,0:T(8,128)(2,1)S(1)}, u32[]{:S(2)}, u32[]{:S(2)}) collective-permute-start(bf16[1,144,128]{2,1,0:T(8,128)(2,1)S(1)} %get-tuple-element.28), channel_id=1, source_target_pairs={{0,24},{1,25},{2,26},{3,27},{4,28},{5,29},{6,30},{7,31},{8,16},{9,... | collective-permute-start | bytes 110600 | tf_op jit(solution)/shard_map/ppermute | solution.py:314
  6.2 4.4 %collective-permute-start = (bf16[1,144,128]{2,1,0:T(8,128)(2,1)S(1)}, bf16[1,144,128]{2,1,0:T(8,128)(2,1)S(1)}, u32[]{:S(2)}, u32[]{:S(2)}) collective-permute-start(bf16[1,144,128]{2,1,0:T(8,128)(2,1)S(1)} %get-tuple-element.28), channel_id=1, source_target_pairs={{0,8},{1,9},{2,10},{3,11},{4,12},{5,13},{6,14},{7,15},{8,0},{9,1},... | collective-permute-start | bytes 110600 | tf_op jit(solution)/shard_map/ppermute | solution.py:314
  10.7 6.2 %collective-permute-start.5 = (bf16[528,128]{1,0:T(8,128)(2,1)S(1)}, bf16[528,128]{1,0:T(8,128)(2,1)S(1)}, u32[]{:S(2)}, u32[]{:S(2)}) collective-permute-start(bf16[528,128]{1,0:T(8,128)(2,1)S(1)} %get-tuple-element.41), channel_id=1, source_target_pairs={{0,4},{1,5},{2,6},{3,7},{4,0},{5,1},{6,2},{7,3},{8,12},{9,13},{10,... | collective-permute-start | bytes 405512 | tf_op jit(solution)/shard_map/ppermute | solution.py:314
  12.3 5.9 %collective-permute-start.4 = (bf16[512,128]{1,0:T(8,128)(2,1)S(1)}, bf16[512,128]{1,0:T(8,128)(2,1)S(1)}, u32[]{:S(2)}, u32[]{:S(2)}) collective-permute-start(bf16[512,128]{1,0:T(8,128)(2,1)S(1)} %pad_maximum_fusion.2), channel_id=1, source_target_pairs={{0,6},{1,7},{2,4},{3,5},{4,2},{5,3},{6,0},{7,1},{8,14},{9,15},{10,... | collective-permute-start | bytes 393224 | tf_op jit(solution)/shard_map/ppermute | solution.py:314
  13.8 5.0 %collective-permute-start.3 = (bf16[512,128]{1,0:T(8,128)(2,1)S(1)}, bf16[512,128]{1,0:T(8,128)(2,1)S(1)}, u32[]{:S(2)}, u32[]{:S(2)}) collective-permute-start(bf16[512,128]{1,0:T(8,128)(2,1)S(1)} %pad_maximum_fusion.2), channel_id=1, source_target_pairs={{0,2},{1,3},{2,0},{3,1},{4,6},{5,7},{6,4},{7,5},{8,10},{9,11},{10,... | collective-permute-start | bytes 393224 | tf_op jit(solution)/shard_map/ppermute | solution.py:314
  16.9 2.0 %collective-permute-start.7 = (bf16[8,128,128]{2,1,0:T(8,128)(2,1)S(1)}, bf16[8,128,128]{2,1,0:T(8,128)(2,1)S(1)}, u32[]{:S(2)}, u32[]{:S(2)}) collective-permute-start(bf16[8,128,128]{2,1,0:T(8,128)(2,1)S(1)} %pad_maximum_fusion.1), channel_id=1, source_target_pairs={{0,1},{1,0},{2,3},{3,2},{4,5},{5,4},{6,7},{7,6},{8,9},{9,8},{10,11... | collective-permute-start | bytes 786440 | tf_op jit(solution)/shard_map/ppermute | solution.py:314
  18.8 1.6 %collective-permute-start.6 = (bf16[8,128,128]{2,1,0:T(8,128)(2,1)S(1)}, bf16[8,128,128]{2,1,0:T(8,128)(2,1)S(1)}, u32[]{:S(2)}, u32[]{:S(2)}) collective-permute-start(bf16[8,128,128]{2,1,0:T(8,128)(2,1)S(1)} %pad_maximum_fusion), channel_id=1, source_target_pairs={{0,1},{1,0},{2,3},{3,2},{4,5},{5,4},{6,7},{7,6},{8,9},{9,8},{10,11... | collective-permute-start | bytes 786440 | tf_op jit(solution)/shard_map/ppermute | solution.py:314

commit v7 on v6

--- a/solution.py
+++ b/solution.py
@@ -119,7 +119,7 @@
 
 RECV = 4
 WIDTH = 2 * SMOOTH + 1
-DEEP = 128
+DEEP = 256
 LABEL = 16
 
 
@@ -327,7 +327,6 @@
         out_specs=[vmem] * 3,
         scratch_shapes=[pltpu.SemaphoreType.DMA((4,))],
     )(forward, band, inverse)
-    parts, fwd, band, inverse = lax.optimization_barrier((parts, fwd, band, inverse))
     own = jnp.concatenate([p[0, 0:half] for p in parts], axis=0)
     label = functools.reduce(jnp.maximum, [p[0, half:] for p in parts])
     near = swap(jnp.concatenate([own, label], axis=0), 1, 0)
@@ -335,6 +334,7 @@
     other = swap(own, 0, 2).reshape(-1, half, channels)
     near, near_label = near[: own.shape[0]].reshape(-1, half, channels), near[own.shape[0] :]
     own = own.reshape(-1, half, channels)
+    near, fwd, band, inverse = lax.optimization_barrier((near, fwd, band, inverse))
     first_sib = swap(jnp.concatenate([own, near], axis=0), 0, 1)
 
     zb = own.shape[0]

time: 22.9 us -> 22.8 us (level)
  transfers between devices with their start and end apart: 8 -> 8, of which waited for: 5 -> 6; matrix products, arithmetic and copies ran while one was open for 0% -> 0% of each run, Pallas kernels for 15% -> 16%
where the time goes in v7:
time: 22.8 us; the launch traced here: 22.6 us
  starting transfers between devices  9.44 us (41%)
  Pallas kernels  6.57 us (29%)
  waiting for transfers between devices  6.37 us (28%)
    ppermute x8, starting transfers between devices, swap(): lax.ppermute(value, ('ch', 'grp'), [(d, d ^ flip) for d in range(total)])  9.44 us
    ppermute x8, waiting for transfers between devices, swap(): lax.ppermute(value, ('ch', 'grp'), [(d, d ^ flip) for d in range(total)])  6.37 us
    pallas_call x1, Pallas kernels, one_block(): pl.pallas_call(cross_kernel, out_shape=jax.ShapeDtypeStruct((RECV, MAXP,...  2.21 us
    pallas_call x1, Pallas kernels, one_block(): pl.pallas_call(middle_kernel, out_shape=partial, in_specs=[vmem] * 7, out...  1.36 us
    pallas_call x1, Pallas kernels, one_block(): pl.pallas_call(tables_kernel, out_shape=[pltpu.VMEM(t.shape, t.dtype) for...  1.18 us
    pallas_call x1, Pallas kernels, one_block(): pl.pallas_call(window_kernel, out_shape=[partial, pltpu.VMEM((SRC, SRC),...  1.04 us
    pallas_call x1, Pallas kernels, one_block(): pl.pallas_call(label_kernel, out_shape=[pltpu.VMEM((1, half + LABEL, chan...  0.78 us
  transfers between devices with their start and end apart: 8, of which 6 were waited for; matrix products, arithmetic and copies ran while one was open for 0% of the time, Pallas kernels for 16%

profile of v7, /device:TPU:0, one launch (start us, length us, event | category | flops | bytes accessed | tf_op | source)
XLA Modules:
  0.0 22.6 jit_solution(2624817072295130174)
XLA Ops:
  0.0 0.8 %shard_map.64 = (bf16[1,144,128]{2,1,0:T(8,128)(2,1)S(1)}, f32[8,256]{1,0:T(8,128)S(1)}) custom-call(s32[1,16]{1,0:T(1,128)} %order.1, s32[1,3]{1,0:T(1,128)} %pairs.1, bf16[1,128,128]{2,1,0:T(8,128)(2,1)} %raw.1), custom_call_target="tpu_custom_call" | custom-call | tf_op jit(solution)/shard_map/pallas_call | solution.py:305
  0.8 4.1 %collective-permute-start.2 = (bf16[1,144,128]{2,1,0:T(8,128)(2,1)S(1)}, bf16[1,144,128]{2,1,0:T(8,128)(2,1)S(1)}, u32[]{:S(2)}, u32[]{:S(2)}) collective-permute-start(bf16[1,144,128]{2,1,0:T(8,128)(2,1)S(1)} %get-tuple-element.21), channel_id=1, source_target_pairs={{0,16},{1,17},{2,18},{3,19},{4,20},{5,21},{6,22},{7,23},{8,24},{9,... | collective-permute-start | bytes 110600 | tf_op jit(solution)/shard_map/ppermute | solution.py:314
  4.9 1.3 %collective-permute-start.1 = (bf16[1,144,128]{2,1,0:T(8,128)(2,1)S(1)}, bf16[1,144,128]{2,1,0:T(8,128)(2,1)S(1)}, u32[]{:S(2)}, u32[]{:S(2)}) collective-permute-start(bf16[1,144,128]{2,1,0:T(8,128)(2,1)S(1)} %get-tuple-element.21), channel_id=1, source_target_pairs={{0,24},{1,25},{2,26},{3,27},{4,28},{5,29},{6,30},{7,31},{8,16},{9,... | collective-permute-start | bytes 110600 | tf_op jit(solution)/shard_map/ppermute | solution.py:314
  6.2 0.2 %collective-permute-start = (bf16[1,144,128]{2,1,0:T(8,128)(2,1)S(1)}, bf16[1,144,128]{2,1,0:T(8,128)(2,1)S(1)}, u32[]{:S(2)}, u32[]{:S(2)}) collective-permute-start(bf16[1,144,128]{2,1,0:T(8,128)(2,1)S(1)} %get-tuple-element.21), channel_id=1, source_target_pairs={{0,8},{1,9},{2,10},{3,11},{4,12},{5,13},{6,14},{7,15},{8,0},{9,1},... | collective-permute-start | bytes 110600 | tf_op jit(solution)/shard_map/ppermute | solution.py:314
  6.5 3.7 %collective-permute-done = bf16[1,144,128]{2,1,0:T(8,128)(2,1)S(1)} collective-permute-done((bf16[1,144,128]{2,1,0:T(8,128)(2,1)S(1)}, bf16[1,144,128]{2,1,0:T(8,128)(2,1)S(1)}, u32[]{:S(2)}, u32[]{:S(2)}) %collective-permute-start) | collective-permute-done | bytes 36896 | tf_op jit(solution)/shard_map/ppermute | solution.py:314
  10.2 0.4 %collective-permute-done.1 = bf16[1,144,128]{2,1,0:T(8,128)(2,1)S(1)} collective-permute-done((bf16[1,144,128]{2,1,0:T(8,128)(2,1)S(1)}, bf16[1,144,128]{2,1,0:T(8,128)(2,1)S(1)}, u32[]{:S(2)}, u32[]{:S(2)}) %collective-permute-start.1) | collective-permute-done | bytes 36896 | tf_op jit(solution)/shard_map/ppermute | solution.py:314
  10.7 0.0 collective-permute-done.2
  10.7 1.6 %collective-permute-start.5 = (bf16[528,128]{1,0:T(8,128)(2,1)S(1)}, bf16[528,128]{1,0:T(8,128)(2,1)S(1)}, u32[]{:S(2)}, u32[]{:S(2)}) collective-permute-start(bf16[528,128]{1,0:T(8,128)(2,1)S(1)} %get-tuple-element.35), channel_id=1, source_target_pairs={{0,4},{1,5},{2,6},{3,7},{4,0},{5,1},{6,2},{7,3},{8,12},{9,13},{10,... | collective-permute-start | bytes 405512 | tf_op jit(solution)/shard_map/ppermute | solution.py:314
  12.3 1.5 %collective-permute-start.4 = (bf16[512,128]{1,0:T(8,128)(2,1)S(1)}, bf16[512,128]{1,0:T(8,128)(2,1)S(1)}, u32[]{:S(2)}, u32[]{:S(2)}) collective-permute-start(bf16[512,128]{1,0:T(8,128)(2,1)S(1)} %pad_maximum_fusion.2), channel_id=1, source_target_pairs={{0,6},{1,7},{2,4},{3,5},{4,2},{5,3},{6,0},{7,1},{8,14},{9,15},{10,... | collective-permute-start | bytes 393224 | tf_op jit(solution)/shard_map/ppermute | solution.py:314
  13.8 0.5 %collective-permute-start.3 = (bf16[512,128]{1,0:T(8,128)(2,1)S(1)}, bf16[512,128]{1,0:T(8,128)(2,1)S(1)}, u32[]{:S(2)}, u32[]{:S(2)}) collective-permute-start(bf16[512,128]{1,0:T(8,128)(2,1)S(1)} %pad_maximum_fusion.2), channel_id=1, source_target_pairs={{0,2},{1,3},{2,0},{3,1},{4,6},{5,7},{6,4},{7,5},{8,10},{9,11},{10,... | collective-permute-start | bytes 393224 | tf_op jit(solution)/shard_map/ppermute | solution.py:314
  14.3 1.2 %shard_map.65 = (bf16[512,256]{1,0:T(8,128)(2,1)S(1)}, bf16[256,256]{1,0:T(8,128)(2,1)S(1)}, bf16[512,256]{1,0:T(8,128)(2,1)S(1)}) custom-call(bf16[512,256]{1,0:T(8,128)(2,1)} %constant.6.clone.forward, bf16[256,256]{1,0:T(8,128)(2,1)} %constant.7.clone.band_from, bf16[512,256]{1,0:T(8,128)(2,1)} %constant.8.clone.inverse_from), custom_call_target="tpu_custom_call" | custom-call | tf_op jit(solution)/shard_map/pallas_call | solution.py:323
  15.5 1.3 %collective-permute-done.5 = bf16[528,128]{1,0:T(8,128)(2,1)S(1)} collective-permute-done((bf16[528,128]{1,0:T(8,128)(2,1)S(1)}, bf16[528,128]{1,0:T(8,128)(2,1)S(1)}, u32[]{:S(2)}, u32[]{:S(2)}) %collective-permute-start.5) | collective-permute-done | bytes 135200 | tf_op jit(solution)/shard_map/ppermute | solution.py:314
  16.9 0.1 collective-permute-start.7
  17.0 1.0 %shard_map.66 = (f32[8,256,128]{2,1,0:T(8,128)S(1)}, bf16[128,128]{1,0:T(8,128)(2,1)S(1)}, f32[128,128]{1,0:T(8,128)S(1)}) custom-call(bf16[4,128,128]{2,1,0:T(8,128)(2,1)S(1)} %bitcast.24, bf16[4,128,128]{2,1,0:T(8,128)(2,1)S(1)} %bitcast.26, bf16[16,128]{1,0:T(8,128)(2,1)S(1)} %get-tuple-element.36.label, bf16[16,128]{1,0:T(8,128)(2,1)S(1)} %slice.47.near_label, ...), custom_call_target="tpu_custom_call" | custom-call | tf_op jit(solution)/shard_map/pallas_call | solution.py:354
  18.0 0.2 collective-permute-done.4
  18.3 0.5 %collective-permute-done.3 = bf16[512,128]{1,0:T(8,128)(2,1)S(1)} collective-permute-done((bf16[512,128]{1,0:T(8,128)(2,1)S(1)}, bf16[512,128]{1,0:T(8,128)(2,1)S(1)}, u32[]{:S(2)}, u32[]{:S(2)}) %collective-permute-start.3) | collective-permute-done | bytes 131104 | tf_op jit(solution)/shard_map/ppermute | solution.py:314
  18.8 0.1 collective-permute-start.6
  18.9 0.0 collective-permute-done.7.sib
  18.9 1.4 %shard_map.67.before = f32[8,256,128]{2,1,0:T(8,128)S(1)} custom-call(bf16[8,128,128]{2,1,0:T(8,128)(2,1)S(1)} %collective-permute-done.7.sib, bf16[4,128,128]{2,1,0:T(8,128)(2,1)S(1)} %bitcast.30, bf16[4,128,128]{2,1,0:T(8,128)(2,1)S(1)} %bitcast.28, bf16[512,256]{1,0:T(8,128)(2,1)S(1)} %get-tuple-element.26.fwd, ...), custom_call_target="tpu_custom_call" | custom-call | tf_op jit(solution)/shard_map/pallas_call | solution.py:369
  20.3 0.1 collective-permute-done.6.sib
  20.4 2.2 %shard_map.68 = bf16[4,3,128,256]{3,2,1,0:T(8,128)(2,1)} custom-call(f32[8,256]{1,0:T(8,128)S(1)} %get-tuple-element.20.keep, bf16[8,128,128]{2,1,0:T(8,128)(2,1)S(1)} %collective-permute-done.6.sib, f32[8,256,128]{2,1,0:T(8,128)S(1)} %shard_map.67.before, bf16[512,256]{1,0:T(8,128)(2,1)S(1)} %get-tuple-element.26.fwd, ...), custom_call_target="tpu_custom_call" | custom-call | tf_op jit(solution)/shard_map/pallas_call | solution.py:377
  (14 shorter events, 0.1 us)
Async XLA Ops:
  0.8 9.9 %collective-permute-start.2 = (bf16[1,144,128]{2,1,0:T(8,128)(2,1)S(1)}, bf16[1,144,128]{2,1,0:T(8,128)(2,1)S(1)}, u32[]{:S(2)}, u32[]{:S(2)}) collective-permute-start(bf16[1,144,128]{2,1,0:T(8,128)(2,1)S(1)} %get-tuple-element.21), channel_id=1, source_target_pairs={{0,16},{1,17},{2,18},{3,19},{4,20},{5,21},{6,22},{7,23},{8,24},{9,... | collective-permute-start | bytes 110600 | tf_op jit(solution)/shard_map/ppermute | solution.py:314
  4.9 5.8 %collective-permute-start.1 = (bf16[1,144,128]{2,1,0:T(8,128)(2,1)S(1)}, bf16[1,144,128]{2,1,0:T(8,128)(2,1)S(1)}, u32[]{:S(2)}, u32[]{:S(2)}) collective-permute-start(bf16[1,144,128]{2,1,0:T(8,128)(2,1)S(1)} %get-tuple-element.21), channel_id=1, source_target_pairs={{0,24},{1,25},{2,26},{3,27},{4,28},{5,29},{6,30},{7,31},{8,16},{9,... | collective-permute-start | bytes 110600 | tf_op jit(solution)/shard_map/ppermute | solution.py:314
  6.2 4.0 %collective-permute-start = (bf16[1,144,128]{2,1,0:T(8,128)(2,1)S(1)}, bf16[1,144,128]{2,1,0:T(8,128)(2,1)S(1)}, u32[]{:S(2)}, u32[]{:S(2)}) collective-permute-start(bf16[1,144,128]{2,1,0:T(8,128)(2,1)S(1)} %get-tuple-element.21), channel_id=1, source_target_pairs={{0,8},{1,9},{2,10},{3,11},{4,12},{5,13},{6,14},{7,15},{8,0},{9,1},... | collective-permute-start | bytes 110600 | tf_op jit(solution)/shard_map/ppermute | solution.py:314
  10.7 6.2 %collective-permute-start.5 = (bf16[528,128]{1,0:T(8,128)(2,1)S(1)}, bf16[528,128]{1,0:T(8,128)(2,1)S(1)}, u32[]{:S(2)}, u32[]{:S(2)}) collective-permute-start(bf16[528,128]{1,0:T(8,128)(2,1)S(1)} %get-tuple-element.35), channel_id=1, source_target_pairs={{0,4},{1,5},{2,6},{3,7},{4,0},{5,1},{6,2},{7,3},{8,12},{9,13},{10,... | collective-permute-start | bytes 405512 | tf_op jit(solution)/shard_map/ppermute | solution.py:314
  12.3 5.9 %collective-permute-start.4 = (bf16[512,128]{1,0:T(8,128)(2,1)S(1)}, bf16[512,128]{1,0:T(8,128)(2,1)S(1)}, u32[]{:S(2)}, u32[]{:S(2)}) collective-permute-start(bf16[512,128]{1,0:T(8,128)(2,1)S(1)} %pad_maximum_fusion.2), channel_id=1, source_target_pairs={{0,6},{1,7},{2,4},{3,5},{4,2},{5,3},{6,0},{7,1},{8,14},{9,15},{10,... | collective-permute-start | bytes 393224 | tf_op jit(solution)/shard_map/ppermute | solution.py:314
  13.8 5.0 %collective-permute-start.3 = (bf16[512,128]{1,0:T(8,128)(2,1)S(1)}, bf16[512,128]{1,0:T(8,128)(2,1)S(1)}, u32[]{:S(2)}, u32[]{:S(2)}) collective-permute-start(bf16[512,128]{1,0:T(8,128)(2,1)S(1)} %pad_maximum_fusion.2), channel_id=1, source_target_pairs={{0,2},{1,3},{2,0},{3,1},{4,6},{5,7},{6,4},{7,5},{8,10},{9,11},{10,... | collective-permute-start | bytes 393224 | tf_op jit(solution)/shard_map/ppermute | solution.py:314
  16.9 2.0 %collective-permute-start.7 = (bf16[8,128,128]{2,1,0:T(8,128)(2,1)S(1)}, bf16[8,128,128]{2,1,0:T(8,128)(2,1)S(1)}, u32[]{:S(2)}, u32[]{:S(2)}) collective-permute-start(bf16[8,128,128]{2,1,0:T(8,128)(2,1)S(1)} %pad_maximum_fusion.1), channel_id=1, source_target_pairs={{0,1},{1,0},{2,3},{3,2},{4,5},{5,4},{6,7},{7,6},{8,9},{9,8},{10,11... | collective-permute-start | bytes 786440 | tf_op jit(solution)/shard_map/ppermute | solution.py:314
  18.8 1.6 %collective-permute-start.6 = (bf16[8,128,128]{2,1,0:T(8,128)(2,1)S(1)}, bf16[8,128,128]{2,1,0:T(8,128)(2,1)S(1)}, u32[]{:S(2)}, u32[]{:S(2)}) collective-permute-start(bf16[8,128,128]{2,1,0:T(8,128)(2,1)S(1)} %pad_maximum_fusion), channel_id=1, source_target_pairs={{0,1},{1,0},{2,3},{3,2},{4,5},{5,4},{6,7},{7,6},{8,9},{9,8},{10,11... | collective-permute-start | bytes 786440 | tf_op jit(solution)/shard_map/ppermute | solution.py:314

commit v8 on v7

--- a/solution.py
+++ b/solution.py
@@ -327,9 +327,10 @@
         out_specs=[vmem] * 3,
         scratch_shapes=[pltpu.SemaphoreType.DMA((4,))],
     )(forward, band, inverse)
+    near_1 = swap(block[0, 0:half], 1, 0)
     own = jnp.concatenate([p[0, 0:half] for p in parts], axis=0)
     label = functools.reduce(jnp.maximum, [p[0, half:] for p in parts])
-    near = swap(jnp.concatenate([own, label], axis=0), 1, 0)
+    near = jnp.concatenate([near_1, swap(jnp.concatenate([own[half:], label], axis=0), 1, 0)], axis=0)
     diag = swap(own, 1, 2).reshape(-1, half, channels)
     other = swap(own, 0, 2).reshape(-1, half, channels)
     near, near_label = near[: own.shape[0]].reshape(-1, half, channels), near[own.shape[0] :]

time: 22.8 us -> 22.8 us (level)
  starting transfers between devices: 9.44 us -> 11 us
  waiting for transfers between devices: 6.37 us -> 4.85 us
    ppermute x8 -> x9, waiting for transfers between devices: 6.37 us -> 4.85 us  [swap(): lax.ppermute(value, ('ch', 'grp'), [(d, d ^ flip) for d in range(total)])]
    ppermute x8 -> x9, starting transfers between devices: 9.44 us -> 11 us  [swap(): lax.ppermute(value, ('ch', 'grp'), [(d, d ^ flip) for d in range(total)])]
  transfers between devices with their start and end apart: 8 -> 9, of which waited for: 6 -> 5; matrix products, arithmetic and copies ran while one was open for 0% -> 0% of each run, Pallas kernels for 16% -> 16%
where the time goes in v8:
time: 22.8 us; the launch traced here: 22.6 us
  starting transfers between devices  11 us (48%)
  Pallas kernels  6.57 us (29%)
  waiting for transfers between devices  4.85 us (21%)
    ppermute x9, starting transfers between devices, swap(): lax.ppermute(value, ('ch', 'grp'), [(d, d ^ flip) for d in range(total)])  11 us
    ppermute x9, waiting for transfers between devices, swap(): lax.ppermute(value, ('ch', 'grp'), [(d, d ^ flip) for d in range(total)])  4.85 us
    pallas_call x1, Pallas kernels, one_block(): pl.pallas_call(cross_kernel, out_shape=jax.ShapeDtypeStruct((RECV, MAXP,...  2.21 us
    pallas_call x1, Pallas kernels, one_block(): pl.pallas_call(middle_kernel, out_shape=partial, in_specs=[vmem] * 7, out...  1.36 us
    pallas_call x1, Pallas kernels, one_block(): pl.pallas_call(tables_kernel, out_shape=[pltpu.VMEM(t.shape, t.dtype) for...  1.18 us
    pallas_call x1, Pallas kernels, one_block(): pl.pallas_call(window_kernel, out_shape=[partial, pltpu.VMEM((SRC, SRC),...  1.04 us
    pallas_call x1, Pallas kernels, one_block(): pl.pallas_call(label_kernel, out_shape=[pltpu.VMEM((1, half + LABEL, chan...  0.78 us
  transfers between devices with their start and end apart: 9, of which 5 were waited for; matrix products, arithmetic and copies ran while one was open for 0% of the time, Pallas kernels for 16%

profile of v8, /device:TPU:0, one launch (start us, length us, event | category | flops | bytes accessed | tf_op | source)
XLA Modules:
  0.0 22.6 jit_solution(9093998254015012818)
XLA Ops:
  0.0 0.8 %shard_map.64 = (bf16[1,144,128]{2,1,0:T(8,128)(2,1)S(1)}, f32[8,256]{1,0:T(8,128)S(1)}) custom-call(s32[1,16]{1,0:T(1,128)} %order.1, s32[1,3]{1,0:T(1,128)} %pairs.1, bf16[1,128,128]{2,1,0:T(8,128)(2,1)} %raw.1), custom_call_target="tpu_custom_call" | custom-call | tf_op jit(solution)/shard_map/pallas_call | solution.py:305
  0.8 4.1 %collective-permute-start.2 = (bf16[1,144,128]{2,1,0:T(8,128)(2,1)S(1)}, bf16[1,144,128]{2,1,0:T(8,128)(2,1)S(1)}, u32[]{:S(2)}, u32[]{:S(2)}) collective-permute-start(bf16[1,144,128]{2,1,0:T(8,128)(2,1)S(1)} %get-tuple-element.21), channel_id=1, source_target_pairs={{0,16},{1,17},{2,18},{3,19},{4,20},{5,21},{6,22},{7,23},{8,24},{9,... | collective-permute-start | bytes 110600 | tf_op jit(solution)/shard_map/ppermute | solution.py:314
  4.9 1.3 %collective-permute-start.1 = (bf16[1,144,128]{2,1,0:T(8,128)(2,1)S(1)}, bf16[1,144,128]{2,1,0:T(8,128)(2,1)S(1)}, u32[]{:S(2)}, u32[]{:S(2)}) collective-permute-start(bf16[1,144,128]{2,1,0:T(8,128)(2,1)S(1)} %get-tuple-element.21), channel_id=1, source_target_pairs={{0,24},{1,25},{2,26},{3,27},{4,28},{5,29},{6,30},{7,31},{8,16},{9,... | collective-permute-start | bytes 110600 | tf_op jit(solution)/shard_map/ppermute | solution.py:314
  6.2 0.2 %collective-permute-start = (bf16[1,144,128]{2,1,0:T(8,128)(2,1)S(1)}, bf16[1,144,128]{2,1,0:T(8,128)(2,1)S(1)}, u32[]{:S(2)}, u32[]{:S(2)}) collective-permute-start(bf16[1,144,128]{2,1,0:T(8,128)(2,1)S(1)} %get-tuple-element.21), channel_id=1, source_target_pairs={{0,8},{1,9},{2,10},{3,11},{4,12},{5,13},{6,14},{7,15},{8,0},{9,1},... | collective-permute-start | bytes 110600 | tf_op jit(solution)/shard_map/ppermute | solution.py:314
  6.5 1.5 %collective-permute-start.5 = (bf16[128,128]{1,0:T(8,128)(2,1)S(1)}, bf16[128,128]{1,0:T(8,128)(2,1)S(1)}, u32[]{:S(2)}, u32[]{:S(2)}) collective-permute-start(bf16[128,128]{1,0:T(8,128)(2,1)S(1)} %slice_bitcast_fusion.3), channel_id=1, source_target_pairs={{0,4},{1,5},{2,6},{3,7},{4,0},{5,1},{6,2},{7,3},{8,12},{9,13},{10,... | collective-permute-start | bytes 98312 | tf_op jit(solution)/shard_map/ppermute | solution.py:314
  8.0 1.2 %shard_map.65 = (bf16[512,256]{1,0:T(8,128)(2,1)S(1)}, bf16[256,256]{1,0:T(8,128)(2,1)S(1)}, bf16[512,256]{1,0:T(8,128)(2,1)S(1)}) custom-call(bf16[512,256]{1,0:T(8,128)(2,1)} %constant.6.clone.forward, bf16[256,256]{1,0:T(8,128)(2,1)} %constant.7.clone.band_from, bf16[512,256]{1,0:T(8,128)(2,1)} %constant.8.clone.inverse_from), custom_call_target="tpu_custom_call" | custom-call | tf_op jit(solution)/shard_map/pallas_call | solution.py:323
  9.2 0.0 collective-permute-done.2
  9.2 1.4 %collective-permute-done.1 = bf16[1,144,128]{2,1,0:T(8,128)(2,1)S(1)} collective-permute-done((bf16[1,144,128]{2,1,0:T(8,128)(2,1)S(1)}, bf16[1,144,128]{2,1,0:T(8,128)(2,1)S(1)}, u32[]{:S(2)}, u32[]{:S(2)}) %collective-permute-start.1) | collective-permute-done | bytes 36896 | tf_op jit(solution)/shard_map/ppermute | solution.py:314
  10.7 0.0 collective-permute-done
  10.7 1.6 %collective-permute-start.6 = (bf16[400,128]{1,0:T(8,128)(2,1)S(1)}, bf16[400,128]{1,0:T(8,128)(2,1)S(1)}, u32[]{:S(2)}, u32[]{:S(2)}) collective-permute-start(bf16[400,128]{1,0:T(8,128)(2,1)S(1)} %pad_maximum_fusion.4), channel_id=1, source_target_pairs={{0,4},{1,5},{2,6},{3,7},{4,0},{5,1},{6,2},{7,3},{8,12},{9,13},{10,... | collective-permute-start | bytes 307208 | tf_op jit(solution)/shard_map/ppermute | solution.py:314
  12.3 1.5 %collective-permute-start.4 = (bf16[512,128]{1,0:T(8,128)(2,1)S(1)}, bf16[512,128]{1,0:T(8,128)(2,1)S(1)}, u32[]{:S(2)}, u32[]{:S(2)}) collective-permute-start(bf16[512,128]{1,0:T(8,128)(2,1)S(1)} %pad_maximum_fusion.3), channel_id=1, source_target_pairs={{0,6},{1,7},{2,4},{3,5},{4,2},{5,3},{6,0},{7,1},{8,14},{9,15},{10,... | collective-permute-start | bytes 393224 | tf_op jit(solution)/shard_map/ppermute | solution.py:314
  13.8 0.5 %collective-permute-start.3 = (bf16[512,128]{1,0:T(8,128)(2,1)S(1)}, bf16[512,128]{1,0:T(8,128)(2,1)S(1)}, u32[]{:S(2)}, u32[]{:S(2)}) collective-permute-start(bf16[512,128]{1,0:T(8,128)(2,1)S(1)} %pad_maximum_fusion.3), channel_id=1, source_target_pairs={{0,2},{1,3},{2,0},{3,1},{4,6},{5,7},{6,4},{7,5},{8,10},{9,11},{10,... | collective-permute-start | bytes 393224 | tf_op jit(solution)/shard_map/ppermute | solution.py:314
  14.3 0.0 collective-permute-done.5
  14.3 2.1 %collective-permute-done.6 = bf16[400,128]{1,0:T(8,128)(2,1)S(1)} collective-permute-done((bf16[400,128]{1,0:T(8,128)(2,1)S(1)}, bf16[400,128]{1,0:T(8,128)(2,1)S(1)}, u32[]{:S(2)}, u32[]{:S(2)}) %collective-permute-start.6) | collective-permute-done | bytes 102432 | tf_op jit(solution)/shard_map/ppermute | solution.py:314
  16.5 0.1 collective-permute-start.8
  16.6 1.0 %shard_map.66 = (f32[8,256,128]{2,1,0:T(8,128)S(1)}, bf16[128,128]{1,0:T(8,128)(2,1)S(1)}, f32[128,128]{1,0:T(8,128)S(1)}) custom-call(bf16[4,128,128]{2,1,0:T(8,128)(2,1)S(1)} %bitcast.15, bf16[4,128,128]{2,1,0:T(8,128)(2,1)S(1)} %bitcast.17, bf16[16,128]{1,0:T(8,128)(2,1)S(1)} %fusion.label, bf16[16,128]{1,0:T(8,128)(2,1)S(1)} %slice.49.near_label, ...), custom_call_target="tpu_custom_call" | custom-call | tf_op jit(solution)/shard_map/pallas_call | solution.py:355
  17.7 0.6 %collective-permute-done.4 = bf16[512,128]{1,0:T(8,128)(2,1)S(1)} collective-permute-done((bf16[512,128]{1,0:T(8,128)(2,1)S(1)}, bf16[512,128]{1,0:T(8,128)(2,1)S(1)}, u32[]{:S(2)}, u32[]{:S(2)}) %collective-permute-start.4) | collective-permute-done | bytes 131104 | tf_op jit(solution)/shard_map/ppermute | solution.py:314
  18.2 0.5 %collective-permute-done.3 = bf16[512,128]{1,0:T(8,128)(2,1)S(1)} collective-permute-done((bf16[512,128]{1,0:T(8,128)(2,1)S(1)}, bf16[512,128]{1,0:T(8,128)(2,1)S(1)}, u32[]{:S(2)}, u32[]{:S(2)}) %collective-permute-start.3) | collective-permute-done | bytes 131104 | tf_op jit(solution)/shard_map/ppermute | solution.py:314
  18.8 0.1 collective-permute-start.7
  18.9 0.0 collective-permute-done.8.sib
  18.9 1.4 %shard_map.67.before = f32[8,256,128]{2,1,0:T(8,128)S(1)} custom-call(bf16[8,128,128]{2,1,0:T(8,128)(2,1)S(1)} %collective-permute-done.8.sib, bf16[4,128,128]{2,1,0:T(8,128)(2,1)S(1)} %bitcast.21, bf16[4,128,128]{2,1,0:T(8,128)(2,1)S(1)} %bitcast.19, bf16[512,256]{1,0:T(8,128)(2,1)S(1)} %get-tuple-element.26.fwd, ...), custom_call_target="tpu_custom_call" | custom-call | tf_op jit(solution)/shard_map/pallas_call | solution.py:370
  20.2 0.1 collective-permute-done.7.sib
  20.4 2.2 %shard_map.68 = bf16[4,3,128,256]{3,2,1,0:T(8,128)(2,1)} custom-call(f32[8,256]{1,0:T(8,128)S(1)} %get-tuple-element.20.keep, bf16[8,128,128]{2,1,0:T(8,128)(2,1)S(1)} %collective-permute-done.7.sib, f32[8,256,128]{2,1,0:T(8,128)S(1)} %shard_map.67.before, bf16[512,256]{1,0:T(8,128)(2,1)S(1)} %get-tuple-element.26.fwd, ...), custom_call_target="tpu_custom_call" | custom-call | tf_op jit(solution)/shard_map/pallas_call | solution.py:378
  (11 shorter events, 0.1 us)
Async XLA Ops:
  0.8 8.4 %collective-permute-start.2 = (bf16[1,144,128]{2,1,0:T(8,128)(2,1)S(1)}, bf16[1,144,128]{2,1,0:T(8,128)(2,1)S(1)}, u32[]{:S(2)}, u32[]{:S(2)}) collective-permute-start(bf16[1,144,128]{2,1,0:T(8,128)(2,1)S(1)} %get-tuple-element.21), channel_id=1, source_target_pairs={{0,16},{1,17},{2,18},{3,19},{4,20},{5,21},{6,22},{7,23},{8,24},{9,... | collective-permute-start | bytes 110600 | tf_op jit(solution)/shard_map/ppermute | solution.py:314
  4.9 5.8 %collective-permute-start.1 = (bf16[1,144,128]{2,1,0:T(8,128)(2,1)S(1)}, bf16[1,144,128]{2,1,0:T(8,128)(2,1)S(1)}, u32[]{:S(2)}, u32[]{:S(2)}) collective-permute-start(bf16[1,144,128]{2,1,0:T(8,128)(2,1)S(1)} %get-tuple-element.21), channel_id=1, source_target_pairs={{0,24},{1,25},{2,26},{3,27},{4,28},{5,29},{6,30},{7,31},{8,16},{9,... | collective-permute-start | bytes 110600 | tf_op jit(solution)/shard_map/ppermute | solution.py:314
  6.2 4.4 %collective-permute-start = (bf16[1,144,128]{2,1,0:T(8,128)(2,1)S(1)}, bf16[1,144,128]{2,1,0:T(8,128)(2,1)S(1)}, u32[]{:S(2)}, u32[]{:S(2)}) collective-permute-start(bf16[1,144,128]{2,1,0:T(8,128)(2,1)S(1)} %get-tuple-element.21), channel_id=1, source_target_pairs={{0,8},{1,9},{2,10},{3,11},{4,12},{5,13},{6,14},{7,15},{8,0},{9,1},... | collective-permute-start | bytes 110600 | tf_op jit(solution)/shard_map/ppermute | solution.py:314
  6.5 7.9 %collective-permute-start.5 = (bf16[128,128]{1,0:T(8,128)(2,1)S(1)}, bf16[128,128]{1,0:T(8,128)(2,1)S(1)}, u32[]{:S(2)}, u32[]{:S(2)}) collective-permute-start(bf16[128,128]{1,0:T(8,128)(2,1)S(1)} %slice_bitcast_fusion.3), channel_id=1, source_target_pairs={{0,4},{1,5},{2,6},{3,7},{4,0},{5,1},{6,2},{7,3},{8,12},{9,13},{10,... | collective-permute-start | bytes 98312 | tf_op jit(solution)/shard_map/ppermute | solution.py:314
  10.7 5.8 %collective-permute-start.6 = (bf16[400,128]{1,0:T(8,128)(2,1)S(1)}, bf16[400,128]{1,0:T(8,128)(2,1)S(1)}, u32[]{:S(2)}, u32[]{:S(2)}) collective-permute-start(bf16[400,128]{1,0:T(8,128)(2,1)S(1)} %pad_maximum_fusion.4), channel_id=1, source_target_pairs={{0,4},{1,5},{2,6},{3,7},{4,0},{5,1},{6,2},{7,3},{8,12},{9,13},{10,... | collective-permute-start | bytes 307208 | tf_op jit(solution)/shard_map/ppermute | solution.py:314
  12.3 5.9 %collective-permute-start.4 = (bf16[512,128]{1,0:T(8,128)(2,1)S(1)}, bf16[512,128]{1,0:T(8,128)(2,1)S(1)}, u32[]{:S(2)}, u32[]{:S(2)}) collective-permute-start(bf16[512,128]{1,0:T(8,128)(2,1)S(1)} %pad_maximum_fusion.3), channel_id=1, source_target_pairs={{0,6},{1,7},{2,4},{3,5},{4,2},{5,3},{6,0},{7,1},{8,14},{9,15},{10,... | collective-permute-start | bytes 393224 | tf_op jit(solution)/shard_map/ppermute | solution.py:314
  13.8 5.0 %collective-permute-start.3 = (bf16[512,128]{1,0:T(8,128)(2,1)S(1)}, bf16[512,128]{1,0:T(8,128)(2,1)S(1)}, u32[]{:S(2)}, u32[]{:S(2)}) collective-permute-start(bf16[512,128]{1,0:T(8,128)(2,1)S(1)} %pad_maximum_fusion.3), channel_id=1, source_target_pairs={{0,2},{1,3},{2,0},{3,1},{4,6},{5,7},{6,4},{7,5},{8,10},{9,11},{10,... | collective-permute-start | bytes 393224 | tf_op jit(solution)/shard_map/ppermute | solution.py:314
  16.5 2.3 %collective-permute-start.8 = (bf16[8,128,128]{2,1,0:T(8,128)(2,1)S(1)}, bf16[8,128,128]{2,1,0:T(8,128)(2,1)S(1)}, u32[]{:S(2)}, u32[]{:S(2)}) collective-permute-start(bf16[8,128,128]{2,1,0:T(8,128)(2,1)S(1)} %pad_maximum_fusion.1), channel_id=1, source_target_pairs={{0,1},{1,0},{2,3},{3,2},{4,5},{5,4},{6,7},{7,6},{8,9},{9,8},{10,11... | collective-permute-start | bytes 786440 | tf_op jit(solution)/shard_map/ppermute | solution.py:314
  18.8 1.6 %collective-permute-start.7 = (bf16[8,128,128]{2,1,0:T(8,128)(2,1)S(1)}, bf16[8,128,128]{2,1,0:T(8,128)(2,1)S(1)}, u32[]{:S(2)}, u32[]{:S(2)}) collective-permute-start(bf16[8,128,128]{2,1,0:T(8,128)(2,1)S(1)} %pad_maximum_fusion), channel_id=1, source_target_pairs={{0,1},{1,0},{2,3},{3,2},{4,5},{5,4},{6,7},{7,6},{8,9},{9,8},{10,11... | collective-permute-start | bytes 786440 | tf_op jit(solution)/shard_map/ppermute | solution.py:314

commit v9 on v8

--- a/solution.py
+++ b/solution.py
@@ -186,7 +186,7 @@
             white[:, part, 2 * kb * i : 2 * kb * (i + 1), :] = both
 
 
-def receiver_products(white, select, pick):
+def receiver_products(white, select):
     blocks, parts, rows, _ = white.shape
     kb = SEG // blocks
     deep = parts * rows
@@ -194,6 +194,7 @@
     sub = lax.broadcasted_iota(jnp.int32, (kb * RECV, deep), 0)
     same = (lane % kb == sub % kb).astype(jnp.float32)
     sign = jnp.where(lane < rows, 1.0, -1.0)
+    picks = []
     for g in range(0, blocks, 2):
         sources = white[g : g + 2].reshape(2 * deep, SRC)
         both = lax.dot_general(
@@ -202,10 +203,11 @@
         for u in range(2):
             v = both[:, u * deep : (u + 1) * deep] * same
             turned = pltpu.roll(v, rows, 1) * sign
-            pick[g + u, 0 : kb * RECV, :] = v.astype(jnp.bfloat16)
-            pick[g + u, kb * RECV :, :] = turned.astype(jnp.bfloat16)
+            picks.append(
+                jnp.concatenate([v.astype(jnp.bfloat16), turned.astype(jnp.bfloat16)], axis=0)
+            )
     sums = [
-        jnp.dot(pick[g], white[g].reshape(deep, SRC), preferred_element_type=jnp.float32)
+        jnp.dot(picks[g], white[g].reshape(deep, SRC), preferred_element_type=jnp.float32)
         for g in range(blocks)
     ]
     return [
@@ -222,7 +224,7 @@
 
 
 def window_kernel(
-    own, near, label, near_label, fwd, band, partial, perm, chosen, white, pick, spec, pows
+    own, near, label, near_label, fwd, band, partial, perm, chosen, white, spec, pows
 ):
     half = fwd.shape[1] // 2
     zb = own.shape[0]
@@ -237,11 +239,11 @@
     chosen[...] = (wanted.astype(jnp.float32) == dest).astype(jnp.float32)
 
     whiten_group(pair_items(own, near, half), fwd, band, spec, pows, white)
-    for at, value in enumerate(receiver_products(white, chosen[...].astype(jnp.bfloat16), pick)):
+    for at, value in enumerate(receiver_products(white, chosen[...].astype(jnp.bfloat16))):
         partial[at] = value
 
 
-def middle_kernel(sib, other, diag, fwd, band, chosen, before, partial, white, pick, spec, pows):
+def middle_kernel(sib, other, diag, fwd, band, chosen, before, partial, white, spec, pows):
     zb, half = other.shape[0:2]
     items = pair_items(sib.at[0:zb], sib.at[zb : 2 * zb], half) + pair_items(other, diag, half)
     whiten_group(items, fwd, band, spec, pows, white)
@@ -250,13 +252,13 @@
     select = jnp.concatenate(
         [chosen[q * step : q * step + each // RECV, :] for q in range(RECV)], axis=0
     )
-    for at, value in enumerate(receiver_products(white, select.astype(jnp.bfloat16), pick)):
+    for at, value in enumerate(receiver_products(white, select.astype(jnp.bfloat16))):
         partial[at] = before[at] + value
 
 
 def cross_kernel(
     keep, sib, before, fwd, perm, chosen, band, inverse, out,
-    white, pick, cross, lags, blank, spec, pows, sems,
+    white, cross, lags, blank, spec, pows, sems,
 ):
     bins = band.shape[0]
     zb, half = sib.shape[0] // 2, sib.shape[1]
@@ -271,7 +273,7 @@
     whiten_group(
         pair_items(sib.at[0:zb], sib.at[zb : 2 * zb], half), fwd, band, spec, pows, white
     )
-    for at, value in enumerate(receiver_products(white, chosen[...].astype(jnp.bfloat16), pick)):
+    for at, value in enumerate(receiver_products(white, chosen[...].astype(jnp.bfloat16))):
         total = (before[at] + value) * (WIDTH / (4 * zb))
         part, q = at // RECV, at % RECV
         cross[q, part * bins : (part + 1) * bins, :] = total.astype(jnp.bfloat16)
@@ -344,7 +346,6 @@
         kb = DEEP // (2 * segments)
         return [
             pltpu.VMEM((SEG // kb, 2, DEEP // 2, SRC), jnp.bfloat16),
-            pltpu.VMEM((SEG // kb, 2 * RECV * kb, DEEP), jnp.bfloat16),
         ], [
             pltpu.VMEM((segments // 2, 2, SEG, 2 * SRC), jnp.float32),
             pltpu.VMEM((segments // 2, SEG, 2 * SRC), jnp.bfloat16),

time: 22.8 us -> 22.8 us (level)
  no operation moved by 1% of the time
where the time goes in v9:
time: 22.8 us; the launch traced here: 22.6 us
  starting transfers between devices  11 us (48%)
  Pallas kernels  6.57 us (29%)
  waiting for transfers between devices  4.85 us (21%)
    ppermute x9, starting transfers between devices, swap(): lax.ppermute(value, ('ch', 'grp'), [(d, d ^ flip) for d in range(total)])  11 us
    ppermute x9, waiting for transfers between devices, swap(): lax.ppermute(value, ('ch', 'grp'), [(d, d ^ flip) for d in range(total)])  4.85 us
    pallas_call x1, Pallas kernels, one_block(): pl.pallas_call(cross_kernel, out_shape=jax.ShapeDtypeStruct((RECV, MAXP,...  2.21 us
    pallas_call x1, Pallas kernels, one_block(): pl.pallas_call(middle_kernel, out_shape=partial, in_specs=[vmem] * 7, out...  1.36 us
    pallas_call x1, Pallas kernels, one_block(): pl.pallas_call(tables_kernel, out_shape=[pltpu.VMEM(t.shape, t.dtype) for...  1.18 us
    pallas_call x1, Pallas kernels, one_block(): pl.pallas_call(window_kernel, out_shape=[partial, pltpu.VMEM((SRC, SRC),...  1.04 us
    pallas_call x1, Pallas kernels, one_block(): pl.pallas_call(label_kernel, out_shape=[pltpu.VMEM((1, half + LABEL, chan...  0.78 us
  transfers between devices with their start and end apart: 9, of which 5 were waited for; matrix products, arithmetic and copies ran while one was open for 0% of the time, Pallas kernels for 16%

profile of v9, /device:TPU:0, one launch (start us, length us, event | category | flops | bytes accessed | tf_op | source)
XLA Modules:
  0.0 22.6 jit_solution(9093998254015012818)
XLA Ops:
  0.0 0.8 %shard_map.64 = (bf16[1,144,128]{2,1,0:T(8,128)(2,1)S(1)}, f32[8,256]{1,0:T(8,128)S(1)}) custom-call(s32[1,16]{1,0:T(1,128)} %order.1, s32[1,3]{1,0:T(1,128)} %pairs.1, bf16[1,128,128]{2,1,0:T(8,128)(2,1)} %raw.1), custom_call_target="tpu_custom_call" | custom-call | tf_op jit(solution)/shard_map/pallas_call | solution.py:307
  0.8 4.1 %collective-permute-start.2 = (bf16[1,144,128]{2,1,0:T(8,128)(2,1)S(1)}, bf16[1,144,128]{2,1,0:T(8,128)(2,1)S(1)}, u32[]{:S(2)}, u32[]{:S(2)}) collective-permute-start(bf16[1,144,128]{2,1,0:T(8,128)(2,1)S(1)} %get-tuple-element.21), channel_id=1, source_target_pairs={{0,16},{1,17},{2,18},{3,19},{4,20},{5,21},{6,22},{7,23},{8,24},{9,... | collective-permute-start | bytes 110600 | tf_op jit(solution)/shard_map/ppermute | solution.py:316
  4.9 1.3 %collective-permute-start.1 = (bf16[1,144,128]{2,1,0:T(8,128)(2,1)S(1)}, bf16[1,144,128]{2,1,0:T(8,128)(2,1)S(1)}, u32[]{:S(2)}, u32[]{:S(2)}) collective-permute-start(bf16[1,144,128]{2,1,0:T(8,128)(2,1)S(1)} %get-tuple-element.21), channel_id=1, source_target_pairs={{0,24},{1,25},{2,26},{3,27},{4,28},{5,29},{6,30},{7,31},{8,16},{9,... | collective-permute-start | bytes 110600 | tf_op jit(solution)/shard_map/ppermute | solution.py:316
  6.2 0.2 %collective-permute-start = (bf16[1,144,128]{2,1,0:T(8,128)(2,1)S(1)}, bf16[1,144,128]{2,1,0:T(8,128)(2,1)S(1)}, u32[]{:S(2)}, u32[]{:S(2)}) collective-permute-start(bf16[1,144,128]{2,1,0:T(8,128)(2,1)S(1)} %get-tuple-element.21), channel_id=1, source_target_pairs={{0,8},{1,9},{2,10},{3,11},{4,12},{5,13},{6,14},{7,15},{8,0},{9,1},... | collective-permute-start | bytes 110600 | tf_op jit(solution)/shard_map/ppermute | solution.py:316
  6.5 1.5 %collective-permute-start.5 = (bf16[128,128]{1,0:T(8,128)(2,1)S(1)}, bf16[128,128]{1,0:T(8,128)(2,1)S(1)}, u32[]{:S(2)}, u32[]{:S(2)}) collective-permute-start(bf16[128,128]{1,0:T(8,128)(2,1)S(1)} %slice_bitcast_fusion.3), channel_id=1, source_target_pairs={{0,4},{1,5},{2,6},{3,7},{4,0},{5,1},{6,2},{7,3},{8,12},{9,13},{10,... | collective-permute-start | bytes 98312 | tf_op jit(solution)/shard_map/ppermute | solution.py:316
  8.0 1.2 %shard_map.65 = (bf16[512,256]{1,0:T(8,128)(2,1)S(1)}, bf16[256,256]{1,0:T(8,128)(2,1)S(1)}, bf16[512,256]{1,0:T(8,128)(2,1)S(1)}) custom-call(bf16[512,256]{1,0:T(8,128)(2,1)} %constant.6.clone.forward, bf16[256,256]{1,0:T(8,128)(2,1)} %constant.7.clone.band_from, bf16[512,256]{1,0:T(8,128)(2,1)} %constant.8.clone.inverse_from), custom_call_target="tpu_custom_call" | custom-call | tf_op jit(solution)/shard_map/pallas_call | solution.py:325
  9.2 0.0 collective-permute-done.2
  9.2 1.4 %collective-permute-done.1 = bf16[1,144,128]{2,1,0:T(8,128)(2,1)S(1)} collective-permute-done((bf16[1,144,128]{2,1,0:T(8,128)(2,1)S(1)}, bf16[1,144,128]{2,1,0:T(8,128)(2,1)S(1)}, u32[]{:S(2)}, u32[]{:S(2)}) %collective-permute-start.1) | collective-permute-done | bytes 36896 | tf_op jit(solution)/shard_map/ppermute | solution.py:316
  10.7 0.0 collective-permute-done
  10.7 1.6 %collective-permute-start.6 = (bf16[400,128]{1,0:T(8,128)(2,1)S(1)}, bf16[400,128]{1,0:T(8,128)(2,1)S(1)}, u32[]{:S(2)}, u32[]{:S(2)}) collective-permute-start(bf16[400,128]{1,0:T(8,128)(2,1)S(1)} %pad_maximum_fusion.4), channel_id=1, source_target_pairs={{0,4},{1,5},{2,6},{3,7},{4,0},{5,1},{6,2},{7,3},{8,12},{9,13},{10,... | collective-permute-start | bytes 307208 | tf_op jit(solution)/shard_map/ppermute | solution.py:316
  12.3 1.5 %collective-permute-start.4 = (bf16[512,128]{1,0:T(8,128)(2,1)S(1)}, bf16[512,128]{1,0:T(8,128)(2,1)S(1)}, u32[]{:S(2)}, u32[]{:S(2)}) collective-permute-start(bf16[512,128]{1,0:T(8,128)(2,1)S(1)} %pad_maximum_fusion.3), channel_id=1, source_target_pairs={{0,6},{1,7},{2,4},{3,5},{4,2},{5,3},{6,0},{7,1},{8,14},{9,15},{10,... | collective-permute-start | bytes 393224 | tf_op jit(solution)/shard_map/ppermute | solution.py:316
  13.8 0.5 %collective-permute-start.3 = (bf16[512,128]{1,0:T(8,128)(2,1)S(1)}, bf16[512,128]{1,0:T(8,128)(2,1)S(1)}, u32[]{:S(2)}, u32[]{:S(2)}) collective-permute-start(bf16[512,128]{1,0:T(8,128)(2,1)S(1)} %pad_maximum_fusion.3), channel_id=1, source_target_pairs={{0,2},{1,3},{2,0},{3,1},{4,6},{5,7},{6,4},{7,5},{8,10},{9,11},{10,... | collective-permute-start | bytes 393224 | tf_op jit(solution)/shard_map/ppermute | solution.py:316
  14.3 0.0 collective-permute-done.5
  14.3 2.1 %collective-permute-done.6 = bf16[400,128]{1,0:T(8,128)(2,1)S(1)} collective-permute-done((bf16[400,128]{1,0:T(8,128)(2,1)S(1)}, bf16[400,128]{1,0:T(8,128)(2,1)S(1)}, u32[]{:S(2)}, u32[]{:S(2)}) %collective-permute-start.6) | collective-permute-done | bytes 102432 | tf_op jit(solution)/shard_map/ppermute | solution.py:316
  16.5 0.1 collective-permute-start.8
  16.6 1.0 %shard_map.66 = (f32[8,256,128]{2,1,0:T(8,128)S(1)}, bf16[128,128]{1,0:T(8,128)(2,1)S(1)}, f32[128,128]{1,0:T(8,128)S(1)}) custom-call(bf16[4,128,128]{2,1,0:T(8,128)(2,1)S(1)} %bitcast.15, bf16[4,128,128]{2,1,0:T(8,128)(2,1)S(1)} %bitcast.17, bf16[16,128]{1,0:T(8,128)(2,1)S(1)} %fusion.label, bf16[16,128]{1,0:T(8,128)(2,1)S(1)} %slice.49.near_label, ...), custom_call_target="tpu_custom_call" | custom-call | tf_op jit(solution)/shard_map/pallas_call | solution.py:356
  17.7 0.6 %collective-permute-done.4 = bf16[512,128]{1,0:T(8,128)(2,1)S(1)} collective-permute-done((bf16[512,128]{1,0:T(8,128)(2,1)S(1)}, bf16[512,128]{1,0:T(8,128)(2,1)S(1)}, u32[]{:S(2)}, u32[]{:S(2)}) %collective-permute-start.4) | collective-permute-done | bytes 131104 | tf_op jit(solution)/shard_map/ppermute | solution.py:316
  18.2 0.5 %collective-permute-done.3 = bf16[512,128]{1,0:T(8,128)(2,1)S(1)} collective-permute-done((bf16[512,128]{1,0:T(8,128)(2,1)S(1)}, bf16[512,128]{1,0:T(8,128)(2,1)S(1)}, u32[]{:S(2)}, u32[]{:S(2)}) %collective-permute-start.3) | collective-permute-done | bytes 131104 | tf_op jit(solution)/shard_map/ppermute | solution.py:316
  18.8 0.1 collective-permute-start.7
  18.9 0.0 collective-permute-done.8.sib
  18.9 1.4 %shard_map.67.before = f32[8,256,128]{2,1,0:T(8,128)S(1)} custom-call(bf16[8,128,128]{2,1,0:T(8,128)(2,1)S(1)} %collective-permute-done.8.sib, bf16[4,128,128]{2,1,0:T(8,128)(2,1)S(1)} %bitcast.21, bf16[4,128,128]{2,1,0:T(8,128)(2,1)S(1)} %bitcast.19, bf16[512,256]{1,0:T(8,128)(2,1)S(1)} %get-tuple-element.26.fwd, ...), custom_call_target="tpu_custom_call" | custom-call | tf_op jit(solution)/shard_map/pallas_call | solution.py:371
  20.2 0.1 collective-permute-done.7.sib
  20.4 2.2 %shard_map.68 = bf16[4,3,128,256]{3,2,1,0:T(8,128)(2,1)} custom-call(f32[8,256]{1,0:T(8,128)S(1)} %get-tuple-element.20.keep, bf16[8,128,128]{2,1,0:T(8,128)(2,1)S(1)} %collective-permute-done.7.sib, f32[8,256,128]{2,1,0:T(8,128)S(1)} %shard_map.67.before, bf16[512,256]{1,0:T(8,128)(2,1)S(1)} %get-tuple-element.26.fwd, ...), custom_call_target="tpu_custom_call" | custom-call | tf_op jit(solution)/shard_map/pallas_call | solution.py:379
  (11 shorter events, 0.1 us)
Async XLA Ops:
  0.8 8.4 %collective-permute-start.2 = (bf16[1,144,128]{2,1,0:T(8,128)(2,1)S(1)}, bf16[1,144,128]{2,1,0:T(8,128)(2,1)S(1)}, u32[]{:S(2)}, u32[]{:S(2)}) collective-permute-start(bf16[1,144,128]{2,1,0:T(8,128)(2,1)S(1)} %get-tuple-element.21), channel_id=1, source_target_pairs={{0,16},{1,17},{2,18},{3,19},{4,20},{5,21},{6,22},{7,23},{8,24},{9,... | collective-permute-start | bytes 110600 | tf_op jit(solution)/shard_map/ppermute | solution.py:316
  4.9 5.8 %collective-permute-start.1 = (bf16[1,144,128]{2,1,0:T(8,128)(2,1)S(1)}, bf16[1,144,128]{2,1,0:T(8,128)(2,1)S(1)}, u32[]{:S(2)}, u32[]{:S(2)}) collective-permute-start(bf16[1,144,128]{2,1,0:T(8,128)(2,1)S(1)} %get-tuple-element.21), channel_id=1, source_target_pairs={{0,24},{1,25},{2,26},{3,27},{4,28},{5,29},{6,30},{7,31},{8,16},{9,... | collective-permute-start | bytes 110600 | tf_op jit(solution)/shard_map/ppermute | solution.py:316
  6.2 4.4 %collective-permute-start = (bf16[1,144,128]{2,1,0:T(8,128)(2,1)S(1)}, bf16[1,144,128]{2,1,0:T(8,128)(2,1)S(1)}, u32[]{:S(2)}, u32[]{:S(2)}) collective-permute-start(bf16[1,144,128]{2,1,0:T(8,128)(2,1)S(1)} %get-tuple-element.21), channel_id=1, source_target_pairs={{0,8},{1,9},{2,10},{3,11},{4,12},{5,13},{6,14},{7,15},{8,0},{9,1},... | collective-permute-start | bytes 110600 | tf_op jit(solution)/shard_map/ppermute | solution.py:316
  6.5 7.9 %collective-permute-start.5 = (bf16[128,128]{1,0:T(8,128)(2,1)S(1)}, bf16[128,128]{1,0:T(8,128)(2,1)S(1)}, u32[]{:S(2)}, u32[]{:S(2)}) collective-permute-start(bf16[128,128]{1,0:T(8,128)(2,1)S(1)} %slice_bitcast_fusion.3), channel_id=1, source_target_pairs={{0,4},{1,5},{2,6},{3,7},{4,0},{5,1},{6,2},{7,3},{8,12},{9,13},{10,... | collective-permute-start | bytes 98312 | tf_op jit(solution)/shard_map/ppermute | solution.py:316
  10.7 5.8 %collective-permute-start.6 = (bf16[400,128]{1,0:T(8,128)(2,1)S(1)}, bf16[400,128]{1,0:T(8,128)(2,1)S(1)}, u32[]{:S(2)}, u32[]{:S(2)}) collective-permute-start(bf16[400,128]{1,0:T(8,128)(2,1)S(1)} %pad_maximum_fusion.4), channel_id=1, source_target_pairs={{0,4},{1,5},{2,6},{3,7},{4,0},{5,1},{6,2},{7,3},{8,12},{9,13},{10,... | collective-permute-start | bytes 307208 | tf_op jit(solution)/shard_map/ppermute | solution.py:316
  12.3 5.9 %collective-permute-start.4 = (bf16[512,128]{1,0:T(8,128)(2,1)S(1)}, bf16[512,128]{1,0:T(8,128)(2,1)S(1)}, u32[]{:S(2)}, u32[]{:S(2)}) collective-permute-start(bf16[512,128]{1,0:T(8,128)(2,1)S(1)} %pad_maximum_fusion.3), channel_id=1, source_target_pairs={{0,6},{1,7},{2,4},{3,5},{4,2},{5,3},{6,0},{7,1},{8,14},{9,15},{10,... | collective-permute-start | bytes 393224 | tf_op jit(solution)/shard_map/ppermute | solution.py:316
  13.8 5.0 %collective-permute-start.3 = (bf16[512,128]{1,0:T(8,128)(2,1)S(1)}, bf16[512,128]{1,0:T(8,128)(2,1)S(1)}, u32[]{:S(2)}, u32[]{:S(2)}) collective-permute-start(bf16[512,128]{1,0:T(8,128)(2,1)S(1)} %pad_maximum_fusion.3), channel_id=1, source_target_pairs={{0,2},{1,3},{2,0},{3,1},{4,6},{5,7},{6,4},{7,5},{8,10},{9,11},{10,... | collective-permute-start | bytes 393224 | tf_op jit(solution)/shard_map/ppermute | solution.py:316
  16.5 2.3 %collective-permute-start.8 = (bf16[8,128,128]{2,1,0:T(8,128)(2,1)S(1)}, bf16[8,128,128]{2,1,0:T(8,128)(2,1)S(1)}, u32[]{:S(2)}, u32[]{:S(2)}) collective-permute-start(bf16[8,128,128]{2,1,0:T(8,128)(2,1)S(1)} %pad_maximum_fusion.1), channel_id=1, source_target_pairs={{0,1},{1,0},{2,3},{3,2},{4,5},{5,4},{6,7},{7,6},{8,9},{9,8},{10,11... | collective-permute-start | bytes 786440 | tf_op jit(solution)/shard_map/ppermute | solution.py:316
  18.8 1.6 %collective-permute-start.7 = (bf16[8,128,128]{2,1,0:T(8,128)(2,1)S(1)}, bf16[8,128,128]{2,1,0:T(8,128)(2,1)S(1)}, u32[]{:S(2)}, u32[]{:S(2)}) collective-permute-start(bf16[8,128,128]{2,1,0:T(8,128)(2,1)S(1)} %pad_maximum_fusion), channel_id=1, source_target_pairs={{0,1},{1,0},{2,3},{3,2},{4,5},{5,4},{6,7},{7,6},{8,9},{9,8},{10,11... | collective-permute-start | bytes 786440 | tf_op jit(solution)/shard_map/ppermute | solution.py:316

commit v10 on v9

--- a/solution.py
+++ b/solution.py
@@ -258,7 +258,7 @@
 
 def cross_kernel(
     keep, sib, before, fwd, perm, chosen, band, inverse, out,
-    white, cross, lags, blank, spec, pows, sems,
+    white, lags, blank, spec, pows, sems,
 ):
     bins = band.shape[0]
     zb, half = sib.shape[0] // 2, sib.shape[1]
@@ -273,14 +273,15 @@
     whiten_group(
         pair_items(sib.at[0:zb], sib.at[zb : 2 * zb], half), fwd, band, spec, pows, white
     )
+    pieces = []
     for at, value in enumerate(receiver_products(white, chosen[...].astype(jnp.bfloat16))):
         total = (before[at] + value) * (WIDTH / (4 * zb))
-        part, q = at // RECV, at % RECV
-        cross[q, part * bins : (part + 1) * bins, :] = total.astype(jnp.bfloat16)
+        pieces.append(total.astype(jnp.bfloat16))
+    ordered = [pieces[part * RECV + q] for q in range(RECV) for part in range(2)]
 
     turned = lax.dot_general(
         perm[...],
-        cross[...].reshape(RECV * 2 * bins, SRC),
+        jnp.concatenate(ordered, axis=0),
         (((1,), (1,)), ((), ())),
         preferred_element_type=jnp.float32,
     ).astype(jnp.bfloat16)
@@ -383,7 +384,6 @@
         out_specs=pl.BlockSpec(memory_space=pl.ANY),
         scratch_shapes=[
             *spectra,
-            pltpu.VMEM((RECV, 2 * SEG, SRC), jnp.bfloat16),
             pltpu.VMEM((RECV, SRC, LAGS), jnp.bfloat16),
             pltpu.VMEM((MAXP - 1, SRC, LAGS), jnp.bfloat16),
             *work,

time: 22.8 us -> 22.8 us (level)
  no operation moved by 1% of the time
where the time goes in v10:
time: 22.8 us; the launch traced here: 22.6 us
  starting transfers between devices  11 us (48%)
  Pallas kernels  6.54 us (29%)
  waiting for transfers between devices  4.85 us (21%)
    ppermute x9, starting transfers between devices, swap(): lax.ppermute(value, ('ch', 'grp'), [(d, d ^ flip) for d in range(total)])  11 us
    ppermute x9, waiting for transfers between devices, swap(): lax.ppermute(value, ('ch', 'grp'), [(d, d ^ flip) for d in range(total)])  4.85 us
    pallas_call x1, Pallas kernels, one_block(): pl.pallas_call(cross_kernel, out_shape=jax.ShapeDtypeStruct((RECV, MAXP,...  2.18 us
    pallas_call x1, Pallas kernels, one_block(): pl.pallas_call(middle_kernel, out_shape=partial, in_specs=[vmem] * 7, out...  1.36 us
    pallas_call x1, Pallas kernels, one_block(): pl.pallas_call(tables_kernel, out_shape=[pltpu.VMEM(t.shape, t.dtype) for...  1.18 us
    pallas_call x1, Pallas kernels, one_block(): pl.pallas_call(window_kernel, out_shape=[partial, pltpu.VMEM((SRC, SRC),...  1.04 us
    pallas_call x1, Pallas kernels, one_block(): pl.pallas_call(label_kernel, out_shape=[pltpu.VMEM((1, half + LABEL, chan...  0.78 us
  transfers between devices with their start and end apart: 9, of which 5 were waited for; matrix products, arithmetic and copies ran while one was open for 0% of the time, Pallas kernels for 16%

profile of v10, /device:TPU:0, one launch (start us, length us, event | category | flops | bytes accessed | tf_op | source)
XLA Modules:
  0.0 22.6 jit_solution(16758870179919680021)
XLA Ops:
  0.0 0.8 %shard_map.64 = (bf16[1,144,128]{2,1,0:T(8,128)(2,1)S(1)}, f32[8,256]{1,0:T(8,128)S(1)}) custom-call(s32[1,16]{1,0:T(1,128)} %order.1, s32[1,3]{1,0:T(1,128)} %pairs.1, bf16[1,128,128]{2,1,0:T(8,128)(2,1)} %raw.1), custom_call_target="tpu_custom_call" | custom-call | tf_op jit(solution)/shard_map/pallas_call | solution.py:308
  0.8 4.1 %collective-permute-start.2 = (bf16[1,144,128]{2,1,0:T(8,128)(2,1)S(1)}, bf16[1,144,128]{2,1,0:T(8,128)(2,1)S(1)}, u32[]{:S(2)}, u32[]{:S(2)}) collective-permute-start(bf16[1,144,128]{2,1,0:T(8,128)(2,1)S(1)} %get-tuple-element.21), channel_id=1, source_target_pairs={{0,16},{1,17},{2,18},{3,19},{4,20},{5,21},{6,22},{7,23},{8,24},{9,... | collective-permute-start | bytes 110600 | tf_op jit(solution)/shard_map/ppermute | solution.py:317
  4.9 1.3 %collective-permute-start.1 = (bf16[1,144,128]{2,1,0:T(8,128)(2,1)S(1)}, bf16[1,144,128]{2,1,0:T(8,128)(2,1)S(1)}, u32[]{:S(2)}, u32[]{:S(2)}) collective-permute-start(bf16[1,144,128]{2,1,0:T(8,128)(2,1)S(1)} %get-tuple-element.21), channel_id=1, source_target_pairs={{0,24},{1,25},{2,26},{3,27},{4,28},{5,29},{6,30},{7,31},{8,16},{9,... | collective-permute-start | bytes 110600 | tf_op jit(solution)/shard_map/ppermute | solution.py:317
  6.2 0.2 %collective-permute-start = (bf16[1,144,128]{2,1,0:T(8,128)(2,1)S(1)}, bf16[1,144,128]{2,1,0:T(8,128)(2,1)S(1)}, u32[]{:S(2)}, u32[]{:S(2)}) collective-permute-start(bf16[1,144,128]{2,1,0:T(8,128)(2,1)S(1)} %get-tuple-element.21), channel_id=1, source_target_pairs={{0,8},{1,9},{2,10},{3,11},{4,12},{5,13},{6,14},{7,15},{8,0},{9,1},... | collective-permute-start | bytes 110600 | tf_op jit(solution)/shard_map/ppermute | solution.py:317
  6.5 1.5 %collective-permute-start.5 = (bf16[128,128]{1,0:T(8,128)(2,1)S(1)}, bf16[128,128]{1,0:T(8,128)(2,1)S(1)}, u32[]{:S(2)}, u32[]{:S(2)}) collective-permute-start(bf16[128,128]{1,0:T(8,128)(2,1)S(1)} %slice_bitcast_fusion.3), channel_id=1, source_target_pairs={{0,4},{1,5},{2,6},{3,7},{4,0},{5,1},{6,2},{7,3},{8,12},{9,13},{10,... | collective-permute-start | bytes 98312 | tf_op jit(solution)/shard_map/ppermute | solution.py:317
  8.0 1.2 %shard_map.65 = (bf16[512,256]{1,0:T(8,128)(2,1)S(1)}, bf16[256,256]{1,0:T(8,128)(2,1)S(1)}, bf16[512,256]{1,0:T(8,128)(2,1)S(1)}) custom-call(bf16[512,256]{1,0:T(8,128)(2,1)} %constant.6.clone.forward, bf16[256,256]{1,0:T(8,128)(2,1)} %constant.7.clone.band_from, bf16[512,256]{1,0:T(8,128)(2,1)} %constant.8.clone.inverse_from), custom_call_target="tpu_custom_call" | custom-call | tf_op jit(solution)/shard_map/pallas_call | solution.py:326
  9.2 0.0 collective-permute-done.2
  9.2 1.4 %collective-permute-done.1 = bf16[1,144,128]{2,1,0:T(8,128)(2,1)S(1)} collective-permute-done((bf16[1,144,128]{2,1,0:T(8,128)(2,1)S(1)}, bf16[1,144,128]{2,1,0:T(8,128)(2,1)S(1)}, u32[]{:S(2)}, u32[]{:S(2)}) %collective-permute-start.1) | collective-permute-done | bytes 36896 | tf_op jit(solution)/shard_map/ppermute | solution.py:317
  10.7 0.0 collective-permute-done
  10.7 1.6 %collective-permute-start.6 = (bf16[400,128]{1,0:T(8,128)(2,1)S(1)}, bf16[400,128]{1,0:T(8,128)(2,1)S(1)}, u32[]{:S(2)}, u32[]{:S(2)}) collective-permute-start(bf16[400,128]{1,0:T(8,128)(2,1)S(1)} %pad_maximum_fusion.4), channel_id=1, source_target_pairs={{0,4},{1,5},{2,6},{3,7},{4,0},{5,1},{6,2},{7,3},{8,12},{9,13},{10,... | collective-permute-start | bytes 307208 | tf_op jit(solution)/shard_map/ppermute | solution.py:317
  12.3 1.5 %collective-permute-start.4 = (bf16[512,128]{1,0:T(8,128)(2,1)S(1)}, bf16[512,128]{1,0:T(8,128)(2,1)S(1)}, u32[]{:S(2)}, u32[]{:S(2)}) collective-permute-start(bf16[512,128]{1,0:T(8,128)(2,1)S(1)} %pad_maximum_fusion.3), channel_id=1, source_target_pairs={{0,6},{1,7},{2,4},{3,5},{4,2},{5,3},{6,0},{7,1},{8,14},{9,15},{10,... | collective-permute-start | bytes 393224 | tf_op jit(solution)/shard_map/ppermute | solution.py:317
  13.8 0.5 %collective-permute-start.3 = (bf16[512,128]{1,0:T(8,128)(2,1)S(1)}, bf16[512,128]{1,0:T(8,128)(2,1)S(1)}, u32[]{:S(2)}, u32[]{:S(2)}) collective-permute-start(bf16[512,128]{1,0:T(8,128)(2,1)S(1)} %pad_maximum_fusion.3), channel_id=1, source_target_pairs={{0,2},{1,3},{2,0},{3,1},{4,6},{5,7},{6,4},{7,5},{8,10},{9,11},{10,... | collective-permute-start | bytes 393224 | tf_op jit(solution)/shard_map/ppermute | solution.py:317
  14.3 0.0 collective-permute-done.5
  14.3 2.1 %collective-permute-done.6 = bf16[400,128]{1,0:T(8,128)(2,1)S(1)} collective-permute-done((bf16[400,128]{1,0:T(8,128)(2,1)S(1)}, bf16[400,128]{1,0:T(8,128)(2,1)S(1)}, u32[]{:S(2)}, u32[]{:S(2)}) %collective-permute-start.6) | collective-permute-done | bytes 102432 | tf_op jit(solution)/shard_map/ppermute | solution.py:317
  16.5 0.1 collective-permute-start.8
  16.6 1.0 %shard_map.66 = (f32[8,256,128]{2,1,0:T(8,128)S(1)}, bf16[128,128]{1,0:T(8,128)(2,1)S(1)}, f32[128,128]{1,0:T(8,128)S(1)}) custom-call(bf16[4,128,128]{2,1,0:T(8,128)(2,1)S(1)} %bitcast.15, bf16[4,128,128]{2,1,0:T(8,128)(2,1)S(1)} %bitcast.17, bf16[16,128]{1,0:T(8,128)(2,1)S(1)} %fusion.label, bf16[16,128]{1,0:T(8,128)(2,1)S(1)} %slice.49.near_label, ...), custom_call_target="tpu_custom_call" | custom-call | tf_op jit(solution)/shard_map/pallas_call | solution.py:357
  17.7 0.6 %collective-permute-done.4 = bf16[512,128]{1,0:T(8,128)(2,1)S(1)} collective-permute-done((bf16[512,128]{1,0:T(8,128)(2,1)S(1)}, bf16[512,128]{1,0:T(8,128)(2,1)S(1)}, u32[]{:S(2)}, u32[]{:S(2)}) %collective-permute-start.4) | collective-permute-done | bytes 131104 | tf_op jit(solution)/shard_map/ppermute | solution.py:317
  18.2 0.5 %collective-permute-done.3 = bf16[512,128]{1,0:T(8,128)(2,1)S(1)} collective-permute-done((bf16[512,128]{1,0:T(8,128)(2,1)S(1)}, bf16[512,128]{1,0:T(8,128)(2,1)S(1)}, u32[]{:S(2)}, u32[]{:S(2)}) %collective-permute-start.3) | collective-permute-done | bytes 131104 | tf_op jit(solution)/shard_map/ppermute | solution.py:317
  18.8 0.1 collective-permute-start.7
  18.9 0.0 collective-permute-done.8.sib
  18.9 1.4 %shard_map.67.before = f32[8,256,128]{2,1,0:T(8,128)S(1)} custom-call(bf16[8,128,128]{2,1,0:T(8,128)(2,1)S(1)} %collective-permute-done.8.sib, bf16[4,128,128]{2,1,0:T(8,128)(2,1)S(1)} %bitcast.21, bf16[4,128,128]{2,1,0:T(8,128)(2,1)S(1)} %bitcast.19, bf16[512,256]{1,0:T(8,128)(2,1)S(1)} %get-tuple-element.26.fwd, ...), custom_call_target="tpu_custom_call" | custom-call | tf_op jit(solution)/shard_map/pallas_call | solution.py:372
  20.2 0.1 collective-permute-done.7.sib
  20.4 2.2 %shard_map.68 = bf16[4,3,128,256]{3,2,1,0:T(8,128)(2,1)} custom-call(f32[8,256]{1,0:T(8,128)S(1)} %get-tuple-element.20.keep, bf16[8,128,128]{2,1,0:T(8,128)(2,1)S(1)} %collective-permute-done.7.sib, f32[8,256,128]{2,1,0:T(8,128)S(1)} %shard_map.67.before, bf16[512,256]{1,0:T(8,128)(2,1)S(1)} %get-tuple-element.26.fwd, ...), custom_call_target="tpu_custom_call" | custom-call | tf_op jit(solution)/shard_map/pallas_call | solution.py:380
  (11 shorter events, 0.1 us)
Async XLA Ops:
  0.8 8.4 %collective-permute-start.2 = (bf16[1,144,128]{2,1,0:T(8,128)(2,1)S(1)}, bf16[1,144,128]{2,1,0:T(8,128)(2,1)S(1)}, u32[]{:S(2)}, u32[]{:S(2)}) collective-permute-start(bf16[1,144,128]{2,1,0:T(8,128)(2,1)S(1)} %get-tuple-element.21), channel_id=1, source_target_pairs={{0,16},{1,17},{2,18},{3,19},{4,20},{5,21},{6,22},{7,23},{8,24},{9,... | collective-permute-start | bytes 110600 | tf_op jit(solution)/shard_map/ppermute | solution.py:317
  4.9 5.8 %collective-permute-start.1 = (bf16[1,144,128]{2,1,0:T(8,128)(2,1)S(1)}, bf16[1,144,128]{2,1,0:T(8,128)(2,1)S(1)}, u32[]{:S(2)}, u32[]{:S(2)}) collective-permute-start(bf16[1,144,128]{2,1,0:T(8,128)(2,1)S(1)} %get-tuple-element.21), channel_id=1, source_target_pairs={{0,24},{1,25},{2,26},{3,27},{4,28},{5,29},{6,30},{7,31},{8,16},{9,... | collective-permute-start | bytes 110600 | tf_op jit(solution)/shard_map/ppermute | solution.py:317
  6.2 4.4 %collective-permute-start = (bf16[1,144,128]{2,1,0:T(8,128)(2,1)S(1)}, bf16[1,144,128]{2,1,0:T(8,128)(2,1)S(1)}, u32[]{:S(2)}, u32[]{:S(2)}) collective-permute-start(bf16[1,144,128]{2,1,0:T(8,128)(2,1)S(1)} %get-tuple-element.21), channel_id=1, source_target_pairs={{0,8},{1,9},{2,10},{3,11},{4,12},{5,13},{6,14},{7,15},{8,0},{9,1},... | collective-permute-start | bytes 110600 | tf_op jit(solution)/shard_map/ppermute | solution.py:317
  6.5 7.9 %collective-permute-start.5 = (bf16[128,128]{1,0:T(8,128)(2,1)S(1)}, bf16[128,128]{1,0:T(8,128)(2,1)S(1)}, u32[]{:S(2)}, u32[]{:S(2)}) collective-permute-start(bf16[128,128]{1,0:T(8,128)(2,1)S(1)} %slice_bitcast_fusion.3), channel_id=1, source_target_pairs={{0,4},{1,5},{2,6},{3,7},{4,0},{5,1},{6,2},{7,3},{8,12},{9,13},{10,... | collective-permute-start | bytes 98312 | tf_op jit(solution)/shard_map/ppermute | solution.py:317
  10.7 5.8 %collective-permute-start.6 = (bf16[400,128]{1,0:T(8,128)(2,1)S(1)}, bf16[400,128]{1,0:T(8,128)(2,1)S(1)}, u32[]{:S(2)}, u32[]{:S(2)}) collective-permute-start(bf16[400,128]{1,0:T(8,128)(2,1)S(1)} %pad_maximum_fusion.4), channel_id=1, source_target_pairs={{0,4},{1,5},{2,6},{3,7},{4,0},{5,1},{6,2},{7,3},{8,12},{9,13},{10,... | collective-permute-start | bytes 307208 | tf_op jit(solution)/shard_map/ppermute | solution.py:317
  12.3 5.9 %collective-permute-start.4 = (bf16[512,128]{1,0:T(8,128)(2,1)S(1)}, bf16[512,128]{1,0:T(8,128)(2,1)S(1)}, u32[]{:S(2)}, u32[]{:S(2)}) collective-permute-start(bf16[512,128]{1,0:T(8,128)(2,1)S(1)} %pad_maximum_fusion.3), channel_id=1, source_target_pairs={{0,6},{1,7},{2,4},{3,5},{4,2},{5,3},{6,0},{7,1},{8,14},{9,15},{10,... | collective-permute-start | bytes 393224 | tf_op jit(solution)/shard_map/ppermute | solution.py:317
  13.8 5.0 %collective-permute-start.3 = (bf16[512,128]{1,0:T(8,128)(2,1)S(1)}, bf16[512,128]{1,0:T(8,128)(2,1)S(1)}, u32[]{:S(2)}, u32[]{:S(2)}) collective-permute-start(bf16[512,128]{1,0:T(8,128)(2,1)S(1)} %pad_maximum_fusion.3), channel_id=1, source_target_pairs={{0,2},{1,3},{2,0},{3,1},{4,6},{5,7},{6,4},{7,5},{8,10},{9,11},{10,... | collective-permute-start | bytes 393224 | tf_op jit(solution)/shard_map/ppermute | solution.py:317
  16.5 2.3 %collective-permute-start.8 = (bf16[8,128,128]{2,1,0:T(8,128)(2,1)S(1)}, bf16[8,128,128]{2,1,0:T(8,128)(2,1)S(1)}, u32[]{:S(2)}, u32[]{:S(2)}) collective-permute-start(bf16[8,128,128]{2,1,0:T(8,128)(2,1)S(1)} %pad_maximum_fusion.1), channel_id=1, source_target_pairs={{0,1},{1,0},{2,3},{3,2},{4,5},{5,4},{6,7},{7,6},{8,9},{9,8},{10,11... | collective-permute-start | bytes 786440 | tf_op jit(solution)/shard_map/ppermute | solution.py:317
  18.8 1.6 %collective-permute-start.7 = (bf16[8,128,128]{2,1,0:T(8,128)(2,1)S(1)}, bf16[8,128,128]{2,1,0:T(8,128)(2,1)S(1)}, u32[]{:S(2)}, u32[]{:S(2)}) collective-permute-start(bf16[8,128,128]{2,1,0:T(8,128)(2,1)S(1)} %pad_maximum_fusion), channel_id=1, source_target_pairs={{0,1},{1,0},{2,3},{3,2},{4,5},{5,4},{6,7},{7,6},{8,9},{9,8},{10,11... | collective-permute-start | bytes 786440 | tf_op jit(solution)/shard_map/ppermute | solution.py:317

commit v11 on v10

--- a/solution.py
+++ b/solution.py
@@ -165,13 +165,19 @@
             ],
             axis=0,
         )
-        re = jnp.dot(fwd[0:bins, :], samples, preferred_element_type=jnp.float32)
-        im = jnp.dot(fwd[bins:, :], samples, preferred_element_type=jnp.float32)
-        power = re * re + im * im
-        spec[i, 0] = re
-        spec[i, 1] = im
-        pows[i] = power.astype(jnp.bfloat16)
-        levels.append(jnp.sum(power.reshape(bins // 8, 8, 2 * SRC), axis=0))
+        level = jnp.zeros((8, 2 * SRC), jnp.float32)
+        step = bins // 2
+        for c in range(0, bins, step):
+            re = jnp.dot(fwd[c : c + step, :], samples, preferred_element_type=jnp.float32)
+            im = jnp.dot(
+                fwd[bins + c : bins + c + step, :], samples, preferred_element_type=jnp.float32
+            )
+            power = re * re + im * im
+            spec[i, 0, c : c + step, :] = re
+            spec[i, 1, c : c + step, :] = im
+            pows[i, c : c + step, :] = power.astype(jnp.bfloat16)
+            level += jnp.sum(power.reshape(step // 8, 8, 2 * SRC), axis=0)
+        levels.append(level)
     blocks, _, rows, _ = white.shape
     kb = bins // blocks
     for i in range(len(items)):

time: 22.8 us -> 22.8 us (level)
  no operation moved by 1% of the time
where the time goes in v11:
time: 22.8 us; the launch traced here: 22.6 us
  starting transfers between devices  11 us (48%)
  Pallas kernels  6.57 us (29%)
  waiting for transfers between devices  4.83 us (21%)
    ppermute x9, starting transfers between devices, swap(): lax.ppermute(value, ('ch', 'grp'), [(d, d ^ flip) for d in range(total)])  11 us
    ppermute x9, waiting for transfers between devices, swap(): lax.ppermute(value, ('ch', 'grp'), [(d, d ^ flip) for d in range(total)])  4.83 us
    pallas_call x1, Pallas kernels, one_block(): pl.pallas_call(cross_kernel, out_shape=jax.ShapeDtypeStruct((RECV, MAXP,...  2.19 us
    pallas_call x1, Pallas kernels, one_block(): pl.pallas_call(middle_kernel, out_shape=partial, in_specs=[vmem] * 7, out...  1.36 us
    pallas_call x1, Pallas kernels, one_block(): pl.pallas_call(tables_kernel, out_shape=[pltpu.VMEM(t.shape, t.dtype) for...  1.18 us
    pallas_call x1, Pallas kernels, one_block(): pl.pallas_call(window_kernel, out_shape=[partial, pltpu.VMEM((SRC, SRC),...  1.05 us
    pallas_call x1, Pallas kernels, one_block(): pl.pallas_call(label_kernel, out_shape=[pltpu.VMEM((1, half + LABEL, chan...  0.78 us
  transfers between devices with their start and end apart: 9, of which 5 were waited for; matrix products, arithmetic and copies ran while one was open for 0% of the time, Pallas kernels for 16%

profile of v11, /device:TPU:0, one launch (start us, length us, event | category | flops | bytes accessed | tf_op | source)
XLA Modules:
  0.0 22.6 jit_solution(17516024562932267606)
XLA Ops:
  0.0 0.8 %shard_map.64 = (bf16[1,144,128]{2,1,0:T(8,128)(2,1)S(1)}, f32[8,256]{1,0:T(8,128)S(1)}) custom-call(s32[1,16]{1,0:T(1,128)} %order.1, s32[1,3]{1,0:T(1,128)} %pairs.1, bf16[1,128,128]{2,1,0:T(8,128)(2,1)} %raw.1), custom_call_target="tpu_custom_call" | custom-call | tf_op jit(solution)/shard_map/pallas_call | solution.py:314
  0.8 4.1 %collective-permute-start.2 = (bf16[1,144,128]{2,1,0:T(8,128)(2,1)S(1)}, bf16[1,144,128]{2,1,0:T(8,128)(2,1)S(1)}, u32[]{:S(2)}, u32[]{:S(2)}) collective-permute-start(bf16[1,144,128]{2,1,0:T(8,128)(2,1)S(1)} %get-tuple-element.21), channel_id=1, source_target_pairs={{0,16},{1,17},{2,18},{3,19},{4,20},{5,21},{6,22},{7,23},{8,24},{9,... | collective-permute-start | bytes 110600 | tf_op jit(solution)/shard_map/ppermute | solution.py:323
  4.9 1.3 %collective-permute-start.1 = (bf16[1,144,128]{2,1,0:T(8,128)(2,1)S(1)}, bf16[1,144,128]{2,1,0:T(8,128)(2,1)S(1)}, u32[]{:S(2)}, u32[]{:S(2)}) collective-permute-start(bf16[1,144,128]{2,1,0:T(8,128)(2,1)S(1)} %get-tuple-element.21), channel_id=1, source_target_pairs={{0,24},{1,25},{2,26},{3,27},{4,28},{5,29},{6,30},{7,31},{8,16},{9,... | collective-permute-start | bytes 110600 | tf_op jit(solution)/shard_map/ppermute | solution.py:323
  6.2 0.2 %collective-permute-start = (bf16[1,144,128]{2,1,0:T(8,128)(2,1)S(1)}, bf16[1,144,128]{2,1,0:T(8,128)(2,1)S(1)}, u32[]{:S(2)}, u32[]{:S(2)}) collective-permute-start(bf16[1,144,128]{2,1,0:T(8,128)(2,1)S(1)} %get-tuple-element.21), channel_id=1, source_target_pairs={{0,8},{1,9},{2,10},{3,11},{4,12},{5,13},{6,14},{7,15},{8,0},{9,1},... | collective-permute-start | bytes 110600 | tf_op jit(solution)/shard_map/ppermute | solution.py:323
  6.5 1.5 %collective-permute-start.5 = (bf16[128,128]{1,0:T(8,128)(2,1)S(1)}, bf16[128,128]{1,0:T(8,128)(2,1)S(1)}, u32[]{:S(2)}, u32[]{:S(2)}) collective-permute-start(bf16[128,128]{1,0:T(8,128)(2,1)S(1)} %slice_bitcast_fusion.3), channel_id=1, source_target_pairs={{0,4},{1,5},{2,6},{3,7},{4,0},{5,1},{6,2},{7,3},{8,12},{9,13},{10,... | collective-permute-start | bytes 98312 | tf_op jit(solution)/shard_map/ppermute | solution.py:323
  8.0 1.2 %shard_map.65 = (bf16[512,256]{1,0:T(8,128)(2,1)S(1)}, bf16[256,256]{1,0:T(8,128)(2,1)S(1)}, bf16[512,256]{1,0:T(8,128)(2,1)S(1)}) custom-call(bf16[512,256]{1,0:T(8,128)(2,1)} %constant.6.clone.forward, bf16[256,256]{1,0:T(8,128)(2,1)} %constant.7.clone.band_from, bf16[512,256]{1,0:T(8,128)(2,1)} %constant.8.clone.inverse_from), custom_call_target="tpu_custom_call" | custom-call | tf_op jit(solution)/shard_map/pallas_call | solution.py:332
  9.2 0.0 collective-permute-done.2
  9.2 1.4 %collective-permute-done.1 = bf16[1,144,128]{2,1,0:T(8,128)(2,1)S(1)} collective-permute-done((bf16[1,144,128]{2,1,0:T(8,128)(2,1)S(1)}, bf16[1,144,128]{2,1,0:T(8,128)(2,1)S(1)}, u32[]{:S(2)}, u32[]{:S(2)}) %collective-permute-start.1) | collective-permute-done | bytes 36896 | tf_op jit(solution)/shard_map/ppermute | solution.py:323
  10.7 0.0 collective-permute-done
  10.7 1.6 %collective-permute-start.6 = (bf16[400,128]{1,0:T(8,128)(2,1)S(1)}, bf16[400,128]{1,0:T(8,128)(2,1)S(1)}, u32[]{:S(2)}, u32[]{:S(2)}) collective-permute-start(bf16[400,128]{1,0:T(8,128)(2,1)S(1)} %pad_maximum_fusion.4), channel_id=1, source_target_pairs={{0,4},{1,5},{2,6},{3,7},{4,0},{5,1},{6,2},{7,3},{8,12},{9,13},{10,... | collective-permute-start | bytes 307208 | tf_op jit(solution)/shard_map/ppermute | solution.py:323
  12.3 1.5 %collective-permute-start.4 = (bf16[512,128]{1,0:T(8,128)(2,1)S(1)}, bf16[512,128]{1,0:T(8,128)(2,1)S(1)}, u32[]{:S(2)}, u32[]{:S(2)}) collective-permute-start(bf16[512,128]{1,0:T(8,128)(2,1)S(1)} %pad_maximum_fusion.3), channel_id=1, source_target_pairs={{0,6},{1,7},{2,4},{3,5},{4,2},{5,3},{6,0},{7,1},{8,14},{9,15},{10,... | collective-permute-start | bytes 393224 | tf_op jit(solution)/shard_map/ppermute | solution.py:323
  13.8 0.5 %collective-permute-start.3 = (bf16[512,128]{1,0:T(8,128)(2,1)S(1)}, bf16[512,128]{1,0:T(8,128)(2,1)S(1)}, u32[]{:S(2)}, u32[]{:S(2)}) collective-permute-start(bf16[512,128]{1,0:T(8,128)(2,1)S(1)} %pad_maximum_fusion.3), channel_id=1, source_target_pairs={{0,2},{1,3},{2,0},{3,1},{4,6},{5,7},{6,4},{7,5},{8,10},{9,11},{10,... | collective-permute-start | bytes 393224 | tf_op jit(solution)/shard_map/ppermute | solution.py:323
  14.3 0.0 collective-permute-done.5
  14.3 2.1 %collective-permute-done.6 = bf16[400,128]{1,0:T(8,128)(2,1)S(1)} collective-permute-done((bf16[400,128]{1,0:T(8,128)(2,1)S(1)}, bf16[400,128]{1,0:T(8,128)(2,1)S(1)}, u32[]{:S(2)}, u32[]{:S(2)}) %collective-permute-start.6) | collective-permute-done | bytes 102432 | tf_op jit(solution)/shard_map/ppermute | solution.py:323
  16.5 0.1 collective-permute-start.8
  16.6 1.1 %shard_map.66 = (f32[8,256,128]{2,1,0:T(8,128)S(1)}, bf16[128,128]{1,0:T(8,128)(2,1)S(1)}, f32[128,128]{1,0:T(8,128)S(1)}) custom-call(bf16[4,128,128]{2,1,0:T(8,128)(2,1)S(1)} %bitcast.15, bf16[4,128,128]{2,1,0:T(8,128)(2,1)S(1)} %bitcast.17, bf16[16,128]{1,0:T(8,128)(2,1)S(1)} %fusion.label, bf16[16,128]{1,0:T(8,128)(2,1)S(1)} %slice.49.near_label, ...), custom_call_target="tpu_custom_call" | custom-call | tf_op jit(solution)/shard_map/pallas_call | solution.py:363
  17.7 0.6 %collective-permute-done.4 = bf16[512,128]{1,0:T(8,128)(2,1)S(1)} collective-permute-done((bf16[512,128]{1,0:T(8,128)(2,1)S(1)}, bf16[512,128]{1,0:T(8,128)(2,1)S(1)}, u32[]{:S(2)}, u32[]{:S(2)}) %collective-permute-start.4) | collective-permute-done | bytes 131104 | tf_op jit(solution)/shard_map/ppermute | solution.py:323
  18.2 0.5 %collective-permute-done.3 = bf16[512,128]{1,0:T(8,128)(2,1)S(1)} collective-permute-done((bf16[512,128]{1,0:T(8,128)(2,1)S(1)}, bf16[512,128]{1,0:T(8,128)(2,1)S(1)}, u32[]{:S(2)}, u32[]{:S(2)}) %collective-permute-start.3) | collective-permute-done | bytes 131104 | tf_op jit(solution)/shard_map/ppermute | solution.py:323
  18.8 0.1 collective-permute-start.7
  18.9 0.0 collective-permute-done.8.sib
  18.9 1.4 %shard_map.67.before = f32[8,256,128]{2,1,0:T(8,128)S(1)} custom-call(bf16[8,128,128]{2,1,0:T(8,128)(2,1)S(1)} %collective-permute-done.8.sib, bf16[4,128,128]{2,1,0:T(8,128)(2,1)S(1)} %bitcast.21, bf16[4,128,128]{2,1,0:T(8,128)(2,1)S(1)} %bitcast.19, bf16[512,256]{1,0:T(8,128)(2,1)S(1)} %get-tuple-element.26.fwd, ...), custom_call_target="tpu_custom_call" | custom-call | tf_op jit(solution)/shard_map/pallas_call | solution.py:378
  20.2 0.1 collective-permute-done.7.sib
  20.4 2.2 %shard_map.68 = bf16[4,3,128,256]{3,2,1,0:T(8,128)(2,1)} custom-call(f32[8,256]{1,0:T(8,128)S(1)} %get-tuple-element.20.keep, bf16[8,128,128]{2,1,0:T(8,128)(2,1)S(1)} %collective-permute-done.7.sib, f32[8,256,128]{2,1,0:T(8,128)S(1)} %shard_map.67.before, bf16[512,256]{1,0:T(8,128)(2,1)S(1)} %get-tuple-element.26.fwd, ...), custom_call_target="tpu_custom_call" | custom-call | tf_op jit(solution)/shard_map/pallas_call | solution.py:386
  (11 shorter events, 0.1 us)
Async XLA Ops:
  0.8 8.4 %collective-permute-start.2 = (bf16[1,144,128]{2,1,0:T(8,128)(2,1)S(1)}, bf16[1,144,128]{2,1,0:T(8,128)(2,1)S(1)}, u32[]{:S(2)}, u32[]{:S(2)}) collective-permute-start(bf16[1,144,128]{2,1,0:T(8,128)(2,1)S(1)} %get-tuple-element.21), channel_id=1, source_target_pairs={{0,16},{1,17},{2,18},{3,19},{4,20},{5,21},{6,22},{7,23},{8,24},{9,... | collective-permute-start | bytes 110600 | tf_op jit(solution)/shard_map/ppermute | solution.py:323
  4.9 5.8 %collective-permute-start.1 = (bf16[1,144,128]{2,1,0:T(8,128)(2,1)S(1)}, bf16[1,144,128]{2,1,0:T(8,128)(2,1)S(1)}, u32[]{:S(2)}, u32[]{:S(2)}) collective-permute-start(bf16[1,144,128]{2,1,0:T(8,128)(2,1)S(1)} %get-tuple-element.21), channel_id=1, source_target_pairs={{0,24},{1,25},{2,26},{3,27},{4,28},{5,29},{6,30},{7,31},{8,16},{9,... | collective-permute-start | bytes 110600 | tf_op jit(solution)/shard_map/ppermute | solution.py:323
  6.2 4.4 %collective-permute-start = (bf16[1,144,128]{2,1,0:T(8,128)(2,1)S(1)}, bf16[1,144,128]{2,1,0:T(8,128)(2,1)S(1)}, u32[]{:S(2)}, u32[]{:S(2)}) collective-permute-start(bf16[1,144,128]{2,1,0:T(8,128)(2,1)S(1)} %get-tuple-element.21), channel_id=1, source_target_pairs={{0,8},{1,9},{2,10},{3,11},{4,12},{5,13},{6,14},{7,15},{8,0},{9,1},... | collective-permute-start | bytes 110600 | tf_op jit(solution)/shard_map/ppermute | solution.py:323
  6.5 7.9 %collective-permute-start.5 = (bf16[128,128]{1,0:T(8,128)(2,1)S(1)}, bf16[128,128]{1,0:T(8,128)(2,1)S(1)}, u32[]{:S(2)}, u32[]{:S(2)}) collective-permute-start(bf16[128,128]{1,0:T(8,128)(2,1)S(1)} %slice_bitcast_fusion.3), channel_id=1, source_target_pairs={{0,4},{1,5},{2,6},{3,7},{4,0},{5,1},{6,2},{7,3},{8,12},{9,13},{10,... | collective-permute-start | bytes 98312 | tf_op jit(solution)/shard_map/ppermute | solution.py:323
  10.7 5.8 %collective-permute-start.6 = (bf16[400,128]{1,0:T(8,128)(2,1)S(1)}, bf16[400,128]{1,0:T(8,128)(2,1)S(1)}, u32[]{:S(2)}, u32[]{:S(2)}) collective-permute-start(bf16[400,128]{1,0:T(8,128)(2,1)S(1)} %pad_maximum_fusion.4), channel_id=1, source_target_pairs={{0,4},{1,5},{2,6},{3,7},{4,0},{5,1},{6,2},{7,3},{8,12},{9,13},{10,... | collective-permute-start | bytes 307208 | tf_op jit(solution)/shard_map/ppermute | solution.py:323
  12.3 5.9 %collective-permute-start.4 = (bf16[512,128]{1,0:T(8,128)(2,1)S(1)}, bf16[512,128]{1,0:T(8,128)(2,1)S(1)}, u32[]{:S(2)}, u32[]{:S(2)}) collective-permute-start(bf16[512,128]{1,0:T(8,128)(2,1)S(1)} %pad_maximum_fusion.3), channel_id=1, source_target_pairs={{0,6},{1,7},{2,4},{3,5},{4,2},{5,3},{6,0},{7,1},{8,14},{9,15},{10,... | collective-permute-start | bytes 393224 | tf_op jit(solution)/shard_map/ppermute | solution.py:323
  13.8 5.0 %collective-permute-start.3 = (bf16[512,128]{1,0:T(8,128)(2,1)S(1)}, bf16[512,128]{1,0:T(8,128)(2,1)S(1)}, u32[]{:S(2)}, u32[]{:S(2)}) collective-permute-start(bf16[512,128]{1,0:T(8,128)(2,1)S(1)} %pad_maximum_fusion.3), channel_id=1, source_target_pairs={{0,2},{1,3},{2,0},{3,1},{4,6},{5,7},{6,4},{7,5},{8,10},{9,11},{10,... | collective-permute-start | bytes 393224 | tf_op jit(solution)/shard_map/ppermute | solution.py:323
  16.5 2.3 %collective-permute-start.8 = (bf16[8,128,128]{2,1,0:T(8,128)(2,1)S(1)}, bf16[8,128,128]{2,1,0:T(8,128)(2,1)S(1)}, u32[]{:S(2)}, u32[]{:S(2)}) collective-permute-start(bf16[8,128,128]{2,1,0:T(8,128)(2,1)S(1)} %pad_maximum_fusion.1), channel_id=1, source_target_pairs={{0,1},{1,0},{2,3},{3,2},{4,5},{5,4},{6,7},{7,6},{8,9},{9,8},{10,11... | collective-permute-start | bytes 786440 | tf_op jit(solution)/shard_map/ppermute | solution.py:323
  18.8 1.6 %collective-permute-start.7 = (bf16[8,128,128]{2,1,0:T(8,128)(2,1)S(1)}, bf16[8,128,128]{2,1,0:T(8,128)(2,1)S(1)}, u32[]{:S(2)}, u32[]{:S(2)}) collective-permute-start(bf16[8,128,128]{2,1,0:T(8,128)(2,1)S(1)} %pad_maximum_fusion), channel_id=1, source_target_pairs={{0,1},{1,0},{2,3},{3,2},{4,5},{5,4},{6,7},{7,6},{8,9},{9,8},{10,11... | collective-permute-start | bytes 786440 | tf_op jit(solution)/shard_map/ppermute | solution.py:323
